TPU v7x, 32 devices: a whole 2x2x4 slice. The times are simulated.
32 devices in a mesh: ctx: 8 (over z, y), fsdp: 4 (over x, core).
Axes of the slice: x: 2, y: 2, z: 4, core: 2. Of those that a mesh axis runs over, the one named last changes fastest.
Arguments:
- inputs: bfloat16 [8, 1024, 1024], P('fsdp', 'ctx'), may hold values from -6 to 6
- lengths: int32 [8], P('fsdp'), may hold values from 256 to 1024, as said below
- positions: int32 [8, 1024], P('fsdp', 'ctx'), may hold values from 0 to 2046, as said below
- cotangent: bfloat16 [8, 1024, 1024], P('fsdp', 'ctx'), may hold values from -6 to 6
- w_query: float32 [1024, 1024], P('fsdp'), may hold values from -0.1875 to 0.1875
- w_key: float32 [1024, 512], P('fsdp'), may hold values from -0.1875 to 0.1875
- w_value: float32 [1024, 512], P('fsdp'), may hold values from -0.1875 to 0.1875
- w_output: float32 [1024, 1024], P('fsdp'), may hold values from -2 to 2
- w_gate: float32 [1024, 4608], P('fsdp'), may hold values from -0.1875 to 0.1875
- w_up: float32 [1024, 4608], P('fsdp'), may hold values from -0.1875 to 0.1875
- w_down: float32 [4608, 1024], P('fsdp'), may hold values from -0.09375 to 0.09375
- attn_gain: float32 [1024], P('fsdp'), may hold values from 0.5 to 1.5
- ffn_gain: float32 [1024], P('fsdp'), may hold values from 0.5 to 1.5
- query_gain: float32 [64], P('fsdp'), may hold values from 0.25 to 1.75
- key_gain: float32 [64], P('fsdp'), may hold values from 0.25 to 1.75
Outputs:
- block_output: bfloat16 [8, 1024, 1024], P('fsdp', 'ctx')
- input_grad: float32 [8, 1024, 1024], P('fsdp', 'ctx')
- query_grad: float32 [1024, 1024], P('fsdp')
- key_grad: float32 [1024, 512], P('fsdp')
- value_grad: float32 [1024, 512], P('fsdp')
- output_grad: float32 [1024, 1024], P('fsdp')
- gate_grad: float32 [1024, 4608], P('fsdp')
- up_grad: float32 [1024, 4608], P('fsdp')
- down_grad: float32 [4608, 1024], P('fsdp')
- attn_gain_grad: float32 [1024], P('fsdp')
- ffn_gain_grad: float32 [1024], P('fsdp')
- query_gain_grad: float32 [64], P('fsdp')
- key_gain_grad: float32 [64], P('fsdp')
Inputs may be any that keep to these rules, and one draw needn't show every extreme that they name: `lengths`: of the 2 sequences of each index of fsdp, one (drawn from the seed) has length 1024; in the first index of fsdp another has length 256. Each sequence's positions start at 0 and rise by 1 or 2 from slot to slot; one sequence (drawn from the seed) rises by 2 at every slot.
All inputs are finite; a program needn't handle non-finite values.
Results may differ from a plain program's by a relative error of at most 0.017.
The roundings to bfloat16 on the way count: a program that leaves them out, or rounds other values in their place, can miss the bound.
Values may be sent and summed in bfloat16 or wider, within the bound.
No kernel may reach another device: no remote copies, remote signals or barrier semaphores. Data moves between devices by JAX's collectives and lax.ppermute only.
A program may use at most 320 MiB of HBM per device.

v0:
```python
import jax
import jax.numpy as jnp
from jax import lax
from jax.sharding import PartitionSpec as P

HEADS = 16
KV_HEADS = 8
HEAD = 64


epsilon = 1e-05
rope_base = 1000000.0
masked = -1e30


def rms_scale(values, scales):
    return values * lax.rsqrt(jnp.mean(values * values, axis=-1, keepdims=True) + epsilon) * scales


def rotate(values, cosine, sine_part):
    half_width = values.shape[-1] // 2
    first_half = values[..., :half_width]
    second_half = values[..., half_width:]
    return jnp.concatenate(
        [
            first_half * cosine - second_half * sine_part,
            second_half * cosine + first_half * sine_part,
        ],
        axis=-1,
    )


def angles(positions, head_width):
    frequency = rope_base ** (-jnp.arange(0, head_width, 2).astype(jnp.float32) / head_width)
    turned = positions.astype(jnp.float32)[..., None] * frequency
    return (jnp.cos(turned), jnp.sin(turned))


def prepare(projected, scales, cosine, sine_part):
    head_width = scales.shape[0]
    shaped = projected.reshape(projected.shape[0], projected.shape[1] // head_width, head_width)
    return rotate(rms_scale(shaped, scales), cosine[:, None], sine_part[:, None])


def swiglu(gate_proj, up_proj):
    return gate_proj * jax.nn.sigmoid(gate_proj) * up_proj


def product(left, right):
    return jnp.dot(left, right, preferred_element_type=jnp.float32)


def by_transpose(left, right):
    return lax.dot_general(
        left, right, (((1,), (1,)), ((), ())), preferred_element_type=jnp.float32
    )


def transpose_by(left, right):
    return lax.dot_general(
        left, right, (((0,), (0,)), ((), ())), preferred_element_type=jnp.float32
    )


def per_device(
    inputs,
    lengths,
    positions,
    cotangent,
    w_query,
    w_key,
    w_value,
    w_output,
    w_gate,
    w_up,
    w_down,
    attn_gain,
    ffn_gain,
    query_gain,
    key_gain,
):
    groups, slot_count, model_width = inputs.shape
    row_count = groups * slot_count
    kv_width = w_key.shape[1]
    seq_length = slot_count * lax.axis_size("ctx")
    key_block = min(512, seq_length)
    block_count = seq_length // key_block
    scale = HEAD ** (-0.5)
    repeat = HEADS // KV_HEADS
    first_slot = lax.axis_index("ctx") * slot_count
    slots = first_slot + jnp.arange(slot_count)
    valid = (slots[None, :] < lengths[:, None]).astype(jnp.float32).reshape(row_count, 1)
    gathered = (
        lax.all_gather(w_query.astype(jnp.bfloat16), "fsdp", axis=0, tiled=True),
        lax.all_gather(w_key.astype(jnp.bfloat16), "fsdp", axis=0, tiled=True),
        lax.all_gather(w_value.astype(jnp.bfloat16), "fsdp", axis=0, tiled=True),
        lax.all_gather(w_output.astype(jnp.bfloat16), "fsdp", axis=0, tiled=True),
        lax.all_gather(w_gate.astype(jnp.bfloat16), "fsdp", axis=0, tiled=True),
        lax.all_gather(w_up.astype(jnp.bfloat16), "fsdp", axis=0, tiled=True),
        lax.all_gather(w_down.astype(jnp.bfloat16), "fsdp", axis=0, tiled=True),
        lax.all_gather(attn_gain.astype(jnp.bfloat16), "fsdp", axis=0, tiled=True),
        lax.all_gather(ffn_gain.astype(jnp.bfloat16), "fsdp", axis=0, tiled=True),
        lax.all_gather(query_gain.astype(jnp.bfloat16), "fsdp", axis=0, tiled=True),
        lax.all_gather(key_gain.astype(jnp.bfloat16), "fsdp", axis=0, tiled=True),
    )
    query_weight, key_weight, value_weight, output_weight, gate_weight, up_weight, down_weight = (
        gathered[:7]
    )
    attn_scale = gathered[7].astype(jnp.float32)
    ffn_scale = gathered[8].astype(jnp.float32)
    qgain_scale = gathered[9].astype(jnp.float32)
    kgain_scale = gathered[10].astype(jnp.float32)
    flat = inputs.reshape(row_count, model_width).astype(jnp.float32)
    cosine, sine_part = angles(positions.reshape(row_count), HEAD)
    normed_low = rms_scale(flat, attn_scale).astype(jnp.bfloat16)
    query_proj = product(normed_low, query_weight)
    key_proj = product(normed_low, key_weight)
    value_proj = product(normed_low, value_weight)
    query_low = prepare(query_proj, qgain_scale, cosine, sine_part).astype(jnp.bfloat16)
    key_low = (
        prepare(key_proj, kgain_scale, cosine, sine_part)
        .reshape(row_count, kv_width)
        .astype(jnp.bfloat16)
    )
    value_low = value_proj.astype(jnp.bfloat16)
    kv_local = jnp.concatenate([key_low, value_low], axis=-1).reshape(
        groups, slot_count, 2 * kv_width
    )
    kv_whole = lax.all_gather(kv_local, "ctx", axis=1, tiled=True)

    def split_block(kv_rows, block_start):
        block_rows = lax.dynamic_slice_in_dim(kv_rows, block_start, key_block, 0)
        key_part = block_rows[:, :kv_width].reshape(key_block, KV_HEADS, HEAD)
        value_part = block_rows[:, kv_width:].reshape(key_block, KV_HEADS, HEAD)
        return (key_part, value_part)

    def score_block(query_group, key_part, block_start, seq_len):
        key_slots = block_start + jnp.arange(key_block)
        scores = (
            jnp.einsum("ikrd,jkd->krij", query_group, key_part, preferred_element_type=jnp.float32)
            * scale
        )
        allowed = (key_slots[None, :] <= slots[:, None]) & (key_slots[None, :] < seq_len)
        return jnp.where(allowed, scores, masked)

    def keep_state(current):
        return current

    attn_parts = []
    lse_parts = []
    for sequence in range(groups):
        seq_len = lengths[sequence]
        last_live = jnp.minimum(first_slot + slot_count - 1, seq_len - 1)
        active = first_slot < seq_len
        query_group = query_low[sequence * slot_count : (sequence + 1) * slot_count].reshape(
            slot_count, KV_HEADS, repeat, HEAD
        )
        kv_rows = kv_whole[sequence]

        def stats_step(block_index, running):
            block_start = block_index * key_block

            def stats_update(current):
                key_part, value_part = split_block(kv_rows, block_start)
                scores = score_block(query_group, key_part, block_start, seq_len)
                new_top = jnp.maximum(current[0], jnp.max(scores, axis=-1))
                new_total = current[1] * jnp.exp(current[0] - new_top) + jnp.sum(
                    jnp.exp(scores - new_top[..., None]), axis=-1
                )
                return (new_top, new_total)

            return lax.cond(active & (block_start <= last_live), stats_update, keep_state, running)

        start_state = (
            jnp.full((KV_HEADS, repeat, slot_count), masked, jnp.float32),
            jnp.zeros((KV_HEADS, repeat, slot_count), jnp.float32),
        )
        top_row, total_row = lax.fori_loop(0, block_count, stats_step, start_state)
        log_total = jnp.where(active, top_row + jnp.log(total_row), 0.0)

        def value_step(block_index, running):
            block_start = block_index * key_block

            def value_update(current):
                key_part, value_part = split_block(kv_rows, block_start)
                scores = score_block(query_group, key_part, block_start, seq_len)
                weights_low = jnp.exp(scores - log_total[..., None]).astype(jnp.bfloat16)
                return current + jnp.einsum(
                    "krij,jkd->ikrd", weights_low, value_part, preferred_element_type=jnp.float32
                )

            return lax.cond(active & (block_start <= last_live), value_update, keep_state, running)

        attended_seq = lax.fori_loop(
            0, block_count, value_step, jnp.zeros((slot_count, KV_HEADS, repeat, HEAD), jnp.float32)
        )
        attn_parts.append(attended_seq.reshape(slot_count, HEADS * HEAD))
        lse_parts.append(log_total)
    attended = jnp.concatenate(attn_parts, axis=0)
    attended_low = attended.astype(jnp.bfloat16)
    hidden_res = flat + product(attended_low, output_weight)
    mid_low = rms_scale(hidden_res, ffn_scale).astype(jnp.bfloat16)
    gate_proj = product(mid_low, gate_weight)
    up_proj = product(mid_low, up_weight)
    inner_low = swiglu(gate_proj, up_proj).astype(jnp.bfloat16)
    result = valid * (hidden_res + product(inner_low, down_weight))
    block_output = result.astype(jnp.bfloat16).reshape(groups, slot_count, model_width)
    query_weight, key_weight, value_weight, output_weight, gate_weight, up_weight, down_weight = (
        lax.all_gather(w_query.astype(jnp.bfloat16), "fsdp", axis=0, tiled=True),
        lax.all_gather(w_key.astype(jnp.bfloat16), "fsdp", axis=0, tiled=True),
        lax.all_gather(w_value.astype(jnp.bfloat16), "fsdp", axis=0, tiled=True),
        lax.all_gather(w_output.astype(jnp.bfloat16), "fsdp", axis=0, tiled=True),
        lax.all_gather(w_gate.astype(jnp.bfloat16), "fsdp", axis=0, tiled=True),
        lax.all_gather(w_up.astype(jnp.bfloat16), "fsdp", axis=0, tiled=True),
        lax.all_gather(w_down.astype(jnp.bfloat16), "fsdp", axis=0, tiled=True),
    )
    kv_back = lax.all_gather(kv_local, "ctx", axis=1, tiled=True)
    outer_grad = cotangent.reshape(row_count, model_width).astype(jnp.float32) * valid
    outer_low = outer_grad.astype(jnp.bfloat16)
    grad_inner = by_transpose(outer_low, down_weight)
    down_part = transpose_by(inner_low, outer_low)
    _, pull_swiglu = jax.vjp(swiglu, gate_proj, up_proj)
    grad_gate, grad_up = pull_swiglu(grad_inner)
    grad_gate_low = grad_gate.astype(jnp.bfloat16)
    grad_up_low = grad_up.astype(jnp.bfloat16)
    gate_part = transpose_by(mid_low, grad_gate_low)
    up_part = transpose_by(mid_low, grad_up_low)
    grad_mid = by_transpose(grad_gate_low, gate_weight) + by_transpose(grad_up_low, up_weight)
    _, pull_mid = jax.vjp(rms_scale, hidden_res, ffn_scale)
    grad_hidden_norm, ffn_part = pull_mid(grad_mid)
    grad_hidden = outer_grad + grad_hidden_norm
    grad_attn_low = grad_hidden.astype(jnp.bfloat16)
    output_part = transpose_by(attended_low, grad_attn_low)
    grad_heads_low = by_transpose(grad_attn_low, output_weight).astype(jnp.bfloat16)
    grad_query_parts = []
    kv_terms = []
    for sequence in range(groups):
        seq_len = lengths[sequence]
        last_live = jnp.minimum(first_slot + slot_count - 1, seq_len - 1)
        active = first_slot < seq_len
        lower_row = sequence * slot_count
        upper_row = (sequence + 1) * slot_count
        query_group = query_low[lower_row:upper_row].reshape(slot_count, KV_HEADS, repeat, HEAD)
        out_rows = attended[lower_row:upper_row].reshape(slot_count, KV_HEADS, repeat, HEAD)
        grad_rows = grad_heads_low[lower_row:upper_row].reshape(slot_count, KV_HEADS, repeat, HEAD)
        delta = jnp.sum(grad_rows.astype(jnp.float32) * out_rows, axis=-1).transpose(1, 2, 0)
        log_total = lse_parts[sequence]
        kv_rows = kv_back[sequence]

        def back_step(block_index, running):
            block_start = block_index * key_block

            def back_update(current):
                key_part, value_part = split_block(kv_rows, block_start)
                scores = score_block(query_group, key_part, block_start, seq_len)
                probability = jnp.exp(scores - log_total[..., None])
                weights_low = probability.astype(jnp.bfloat16)
                grad_probs = jnp.einsum(
                    "ikrd,jkd->krij", grad_rows, value_part, preferred_element_type=jnp.float32
                )
                grad_scores = (probability * (grad_probs - delta[..., None])).astype(jnp.bfloat16)
                grad_query = (
                    current[0]
                    + jnp.einsum(
                        "krij,jkd->ikrd", grad_scores, key_part, preferred_element_type=jnp.float32
                    )
                    * scale
                )
                grad_key = (
                    jnp.einsum(
                        "krij,ikrd->jkd",
                        grad_scores,
                        query_group,
                        preferred_element_type=jnp.float32,
                    )
                    * scale
                )
                grad_value = jnp.einsum(
                    "krij,ikrd->jkd", weights_low, grad_rows, preferred_element_type=jnp.float32
                )
                block_grads = jnp.concatenate(
                    [
                        grad_key.reshape(key_block, kv_width),
                        grad_value.reshape(key_block, kv_width),
                    ],
                    axis=-1,
                )
                return (
                    grad_query,
                    lax.dynamic_update_slice_in_dim(current[1], block_grads, block_start, 0),
                )

            return lax.cond(active & (block_start <= last_live), back_update, keep_state, running)

        start_state = (
            jnp.zeros((slot_count, KV_HEADS, repeat, HEAD), jnp.float32),
            jnp.zeros((seq_length, 2 * kv_width), jnp.float32),
        )
        grad_query_seq, seq_terms = lax.fori_loop(0, block_count, back_step, start_state)
        grad_query_parts.append(grad_query_seq.reshape(slot_count, HEADS, HEAD))
        kv_terms.append(seq_terms)
    grad_kv = lax.psum_scatter(jnp.stack(kv_terms), "ctx", scatter_dimension=1, tiled=True).reshape(
        row_count, 2 * kv_width
    )
    grad_key_rot = grad_kv[:, :kv_width].reshape(row_count, KV_HEADS, HEAD)
    grad_value_low = grad_kv[:, kv_width:].astype(jnp.bfloat16)
    grad_query_rot = jnp.concatenate(grad_query_parts, axis=0)
    _, pull_query = jax.vjp(
        lambda projected, scales: prepare(projected, scales, cosine, sine_part),
        query_proj,
        qgain_scale,
    )
    grad_query_proj, qgain_part = pull_query(grad_query_rot)
    _, pull_key = jax.vjp(
        lambda projected, scales: prepare(projected, scales, cosine, sine_part),
        key_proj,
        kgain_scale,
    )
    grad_key_proj, kgain_part = pull_key(grad_key_rot)
    grad_query_low = grad_query_proj.astype(jnp.bfloat16)
    grad_key_low = grad_key_proj.astype(jnp.bfloat16)
    query_part = transpose_by(normed_low, grad_query_low)
    key_part_grad = transpose_by(normed_low, grad_key_low)
    value_part_grad = transpose_by(normed_low, grad_value_low)
    grad_normed = (
        by_transpose(grad_query_low, query_weight)
        + by_transpose(grad_key_low, key_weight)
        + by_transpose(grad_value_low, value_weight)
    )
    _, pull_input = jax.vjp(rms_scale, flat, attn_scale)
    grad_flat_norm, attn_part = pull_input(grad_normed)
    input_grad = (grad_hidden + grad_flat_norm).reshape(groups, slot_count, model_width)
    owned = (
        lax.psum_scatter(
            query_part.astype(jnp.bfloat16), "fsdp", scatter_dimension=0, tiled=True
        ).astype(jnp.float32),
        lax.psum_scatter(
            key_part_grad.astype(jnp.bfloat16), "fsdp", scatter_dimension=0, tiled=True
        ).astype(jnp.float32),
        lax.psum_scatter(
            value_part_grad.astype(jnp.bfloat16), "fsdp", scatter_dimension=0, tiled=True
        ).astype(jnp.float32),
        lax.psum_scatter(
            output_part.astype(jnp.bfloat16), "fsdp", scatter_dimension=0, tiled=True
        ).astype(jnp.float32),
        lax.psum_scatter(
            gate_part.astype(jnp.bfloat16), "fsdp", scatter_dimension=0, tiled=True
        ).astype(jnp.float32),
        lax.psum_scatter(
            up_part.astype(jnp.bfloat16), "fsdp", scatter_dimension=0, tiled=True
        ).astype(jnp.float32),
        lax.psum_scatter(
            down_part.astype(jnp.bfloat16), "fsdp", scatter_dimension=0, tiled=True
        ).astype(jnp.float32),
        lax.psum_scatter(
            attn_part.astype(jnp.bfloat16), "fsdp", scatter_dimension=0, tiled=True
        ).astype(jnp.float32),
        lax.psum_scatter(
            ffn_part.astype(jnp.bfloat16), "fsdp", scatter_dimension=0, tiled=True
        ).astype(jnp.float32),
        lax.psum_scatter(
            qgain_part.astype(jnp.bfloat16), "fsdp", scatter_dimension=0, tiled=True
        ).astype(jnp.float32),
        lax.psum_scatter(
            kgain_part.astype(jnp.bfloat16), "fsdp", scatter_dimension=0, tiled=True
        ).astype(jnp.float32),
    )
    (
        own_query,
        own_key,
        own_value,
        own_output,
        own_gate,
        own_up,
        own_down,
        own_attn,
        own_ffn,
        own_qgain,
        own_kgain,
    ) = owned
    summed = lax.psum(
        (
            own_query,
            own_key,
            own_value,
            own_output,
            own_gate,
            own_up,
            own_down,
            own_attn,
            own_ffn,
            own_qgain,
            own_kgain,
        ),
        "ctx",
    )
    return (
        block_output,
        input_grad,
        summed[0],
        summed[1],
        summed[2],
        summed[3],
        summed[4],
        summed[5],
        summed[6],
        summed[7],
        summed[8],
        summed[9],
        summed[10],
    )


def solution(mesh):
    return jax.shard_map(
        per_device,
        mesh=mesh,
        in_specs=(
            P("fsdp", "ctx", None),
            P("fsdp"),
            P("fsdp", "ctx"),
            P("fsdp", "ctx", None),
            P("fsdp", None),
            P("fsdp", None),
            P("fsdp", None),
            P("fsdp", None),
            P("fsdp", None),
            P("fsdp", None),
            P("fsdp", None),
            P("fsdp"),
            P("fsdp"),
            P("fsdp"),
            P("fsdp"),
        ),
        out_specs=(
            P("fsdp", "ctx", None),
            P("fsdp", "ctx", None),
            P("fsdp", None),
            P("fsdp", None),
            P("fsdp", None),
            P("fsdp", None),
            P("fsdp", None),
            P("fsdp", None),
            P("fsdp", None),
            P("fsdp"),
            P("fsdp"),
            P("fsdp"),
            P("fsdp"),
        ),
        check_vma=False,
    )
```

profile of v0, /device:TPU:0, one launch (start us, length us, event | category | flops | bytes accessed | tf_op | source)
XLA Modules:
  0.0 1645.6 jit_solution(12572242938788006507)
XLA Ops:
  11.0 2.1 convert_element_type.308
  13.3 6.0 all-gather
  21.1 8.0 all-reduce.12
  30.3 2.4 copy.69
  35.6 13.1 all-gather.13.cloned.1.call-done
  51.5 2.1 convert_element_type.311
  53.6 4.0 convert_element_type.316
  57.7 4.3 convert_element_type.315
  62.1 4.2 convert_element_type.318
  69.5 5.5 all-gather.1
  76.1 3.9 copy.72
  80.1 2.3 multiply_reduce_fusion.5
  83.7 67.3 %all-gather.15.cloned.1.call-done = bf16[2,1024,1024]{1,2,0:T(8,128)(2,1)} async-done(((bf16[2,128,1024]{1,2,0:T(8,128)(2,1)}), bf16[2,1024,1024]{1,2,0:T(8,128)(2,1)}) %all-gather.15.cloned.1.call-update) | async-done | bytes 4194320 | tf_op jit(solution)/shard_map/all_gather | solution.py:129
  150.9 4.0 slice_bitcast_fusion.1
  155.0 3.8 while.98
  155.0 3.7 conditional.18
  159.6 6.7 while.99
  159.6 6.7 conditional.19
  159.6 2.2 constant_dynamic-slice_fusion.1
  162.6 3.6 fusion.18
  167.4 2.8 while.100
  167.4 2.7 conditional.20
  171.1 5.5 while.101
  171.1 5.5 conditional.21
  173.0 3.6 fusion.27
  178.4 2.5 multiply_reduce_fusion.4
  182.1 57.9 %all-gather.23.cloned.1.call-done = bf16[1024,4608]{1,0:T(8,128)(2,1)} async-done(((bf16[256,4608]{1,0:T(8,128)(2,1)}), bf16[1024,4608]{1,0:T(8,128)(2,1)}) %all-gather.23.cloned.1.call-update) | async-done | bytes 9437200 | tf_op jit(solution)/shard_map/all_gather | solution.py:99
  240.0 7.9 fusion.100
  247.9 58.5 %all-gather.21.cloned.1.call-done = bf16[1024,4608]{1,0:T(8,128)(2,1)} async-done(((bf16[256,4608]{1,0:T(8,128)(2,1)}), bf16[1024,4608]{1,0:T(8,128)(2,1)}) %all-gather.21.cloned.1.call-update) | async-done | bytes 9437200 | tf_op jit(solution)/shard_map/all_gather | solution.py:98
  306.4 8.1 fusion.99
  314.5 58.3 %all-gather.25.cloned.1.call-done = bf16[4608,1024]{1,0:T(8,128)(2,1)} async-done(((bf16[1152,1024]{1,0:T(8,128)(2,1)}), bf16[4608,1024]{1,0:T(8,128)(2,1)}) %all-gather.25.cloned.1.call-update) | async-done | bytes 9437200 | tf_op jit(solution)/shard_map/all_gather | solution.py:100
  372.8 10.2 multiply_convert_fusion
  383.1 2.6 fusion.101
  385.8 5.6 multiply_reduce_fusion.1
  395.6 2.5 broadcast.374.clone.1
  398.2 9.1 while.102
  398.4 8.9 conditional.22
  407.3 5.4 copy.75
  415.5 2.5 broadcast.374.clone
  418.1 7.8 while.103
  418.2 7.8 conditional.23
  425.9 5.3 copy.76
  431.3 8.4 pad_maximum_fusion
  441.0 3.0 convolution_convert_fusion.3
  445.4 2.1 convolution_convert_fusion.4
  447.5 157.9 %reduce-scatter.9.cloned.1.call-done = f32[2,128,1024]{2,1,0:T(8,128)} async-done(((f32[2,1024,1024]{2,1,0:T(8,128)}), f32[2,128,1024]{2,1,0:T(8,128)}) %reduce-scatter.9.cloned.1.call-update) | async-done | bytes 1048592 | tf_op jit(solution)/shard_map/reduce_scatter | solution.py:302
  607.4 2.0 copy.77
  613.2 2.5 convolution_convert_fusion.5
  615.8 6.8 convolution_convert_fusion.2
  622.7 6.7 convolution_convert_fusion.1
  630.4 7.0 convolution_convert_fusion
  638.7 3.3 fusion.102
  642.1 7.9 fusion.67
  650.0 23.6 %reduce-scatter.11.cloned.1.call-done = bf16[256,1024]{1,0:T(8,128)(2,1)} async-done(((bf16[1024,1024]{1,0:T(8,128)(2,1)}), bf16[256,1024]{1,0:T(8,128)(2,1)}) %reduce-scatter.11.cloned.1.call-update) | async-done | bytes 524304 | tf_op jit(solution)/shard_map/reduce_scatter | solution.py:334
  673.5 2.0 convolution_add_fusion.1
  675.6 3.0 fusion.75
  678.6 5.8 all-reduce.11
  684.6 2.5 fusion.70
  687.1 14.5 reduce-scatter.13.cloned.1.call-done
  701.6 27.4 %reduce-scatter.15.cloned.1.call-done = bf16[256,512]{1,0:T(8,128)(2,1)} async-done(((bf16[1024,512]{1,0:T(8,128)(2,1)}), bf16[256,512]{1,0:T(8,128)(2,1)}) %reduce-scatter.15.cloned.1.call-update) | async-done | bytes 262160 | tf_op jit(solution)/shard_map/reduce_scatter | solution.py:340
  729.0 81.1 %reduce-scatter.19.cloned.1.call-done = bf16[256,4608]{1,0:T(8,128)(2,1)} async-done(((bf16[1024,4608]{1,0:T(8,128)(2,1)}), bf16[256,4608]{1,0:T(8,128)(2,1)}) %reduce-scatter.19.cloned.1.call-update) | async-done | bytes 2359312 | tf_op jit(solution)/shard_map/reduce_scatter | solution.py:346
  810.1 81.1 %reduce-scatter.21.cloned.1.call-done = bf16[256,4608]{1,0:T(8,128)(2,1)} async-done(((bf16[1024,4608]{1,0:T(8,128)(2,1)}), bf16[256,4608]{1,0:T(8,128)(2,1)}) %reduce-scatter.21.cloned.1.call-update) | async-done | bytes 2359312 | tf_op jit(solution)/shard_map/reduce_scatter | solution.py:349
  891.2 81.1 %reduce-scatter.23.cloned.1.call-done = bf16[1152,1024]{1,0:T(8,128)(2,1)} async-done(((bf16[4608,1024]{1,0:T(8,128)(2,1)}), bf16[1152,1024]{1,0:T(8,128)(2,1)}) %reduce-scatter.23.cloned.1.call-update) | async-done | bytes 2359312 | tf_op jit(solution)/shard_map/reduce_scatter | solution.py:352
  972.3 666.3 %all-reduce.14 = (f32[256,1024]{1,0:T(8,128)}, f32[256,512]{1,0:T(8,128)}, f32[256,512]{1,0:T(8,128)}, f32[256,1024]{1,0:T(8,128)}, f32[256,4608]{1,0:T(8,128)},...) all-reduce(bf16[256,1024]{1,0:T(8,128)(2,1)} %reduce-scatter.11.clo, ...), channel_id=1, replica_groups=mesh['ctx'=8,'fsdp'=4] {'ctx'}, use_global_device_ids=true, to_apply=%region_40.41 | all-reduce | flops 4325920 | bytes 25956608 | tf_op jit(solution)/shard_map/psum | solution.py:381
  (318 shorter events, 62.4 us)
Async XLA Ops:
  7.2 12.1 copy-start.62
  7.2 6.0 copy-start.64
  7.2 12.1 copy-start.66
  7.2 12.1 copy-start.67
  7.2 21.9 %copy-start = (bf16[2,128,1024]{2,1,0:T(8,128)(2,1)S(1)}, bf16[2,128,1024]{2,1,0:T(8,128)(2,1)}, u32[]{:S(2)}) copy-start(bf16[2,128,1024]{2,1,0:T(8,128)(2,1)} %param.39) | copy-start | bytes 1572868
  7.2 22.1 %copy-start.63 = (s32[2,128]{1,0:T(2,128)S(1)}, s32[2,128]{1,0:T(2,128)}, u32[]{:S(2)}) copy-start(s32[2,128]{1,0:T(2,128)} %param.41) | copy-start | bytes 3076
  7.2 23.1 %all-gather.11.cloned.1.call-start = ((), (), s32[]{:S(2)}) async-start(), calls=%async_computation.8 | async-start | bytes 1310720 | tf_op jit(solution)/shard_map/all_gather | solution.py:95
  9.1 39.5 %all-gather.13.cloned.1.call-start = ((), (), s32[]{:S(2)}) async-start(), calls=%async_computation.9 | async-start | bytes 1310720 | tf_op jit(solution)/shard_map/all_gather | solution.py:96
  11.0 65.1 %all-gather.17.cloned.1.call-start = ((), (), s32[]{:S(2)}) async-start(), calls=%async_computation.11 | async-start | bytes 2621440 | tf_op jit(solution)/shard_map/all_gather | solution.py:94
  13.2 137.8 %all-gather.15.cloned.1.call-start = ((), (), s32[]{:S(2)}) async-start(), calls=%async_computation.10 | async-start | bytes 4718592 | tf_op jit(solution)/shard_map/all_gather | solution.py:129
  19.3 13.5 copy-start.47
  29.1 5.5 copy-start.57
  29.4 3.4 copy-start.55
  29.6 53.8 %copy-start.38 = (f32[256,32]{0,1:T(8,128)}, f32[256,32]{0,1:T(8,128)S(1)}, u32[]{:S(2)}) copy-start(f32[256,32]{0,1:T(8,128)S(1)} %get-tuple-element.1639) | copy-start | bytes 98308
  29.6 53.8 %copy-start.40 = (f32[256,32]{0,1:T(8,128)}, f32[256,32]{0,1:T(8,128)S(1)}, u32[]{:S(2)}) copy-start(f32[256,32]{0,1:T(8,128)S(1)} %get-tuple-element.1640) | copy-start | bytes 98308
  30.1 50.0 %copy-start.19 = (bf16[2,128,1024]{2,1,0:T(8,128)(2,1)}, bf16[2,128,1024]{2,1,0:T(8,128)(2,1)S(1)}, u32[]{:S(2)}) copy-start(bf16[2,128,1024]{2,1,0:T(8,128)(2,1)S(1)} %fusion.78) | copy-start | bytes 1572868
  30.3 18.4 %copy-start.17 = (bf16[256,1024]{1,0:T(8,128)(2,1)}, bf16[256,1024]{1,0:T(8,128)(2,1)S(1)}, u32[]{:S(2)}) copy-start(bf16[256,1024]{1,0:T(8,128)(2,1)S(1)} %fusion.74) | copy-start | bytes 1572868
  34.5 19.1 %copy-start.22 = (f32[256,8,64]{0,2,1:T(8,128)}, f32[256,8,64]{0,2,1:T(8,128)S(1)}, u32[]{:S(2)}) copy-start(f32[256,8,64]{0,2,1:T(8,128)S(1)} %get-tuple-element.1646) | copy-start | bytes 1572868
  51.4 127.0 %all-gather.19.cloned.1.call-start = ((), (), s32[]{:S(2)}) async-start(), calls=%async_computation.12 | async-start | bytes 2621440 | tf_op jit(solution)/shard_map/all_gather | solution.py:97
  53.6 186.4 %all-gather.23.cloned.1.call-start = ((), (), s32[]{:S(2)}) async-start(), calls=%async_computation.14 | async-start | bytes 11796480 | tf_op jit(solution)/shard_map/all_gather | solution.py:99
  57.6 248.8 %all-gather.21.cloned.1.call-start = ((), (), s32[]{:S(2)}) async-start(), calls=%async_computation.13 | async-start | bytes 11796480 | tf_op jit(solution)/shard_map/all_gather | solution.py:98
  62.0 4.4 copy-start.59
  62.1 7.5 copy-start.65
  62.1 13.1 copy-start.35
  62.1 310.7 %all-gather.25.cloned.1.call-start = ((), (), s32[]{:S(2)}) async-start(), calls=%async_computation.15 | async-start | bytes 11796480 | tf_op jit(solution)/shard_map/all_gather | solution.py:100
  66.3 539.1 %reduce-scatter.9.cloned.1.call-start = ((), (), s32[]{:S(2)}) async-start(), calls=%async_computation.16 | async-start | bytes 9437184 | tf_op jit(solution)/shard_map/reduce_scatter | solution.py:302
  69.5 13.0 copy-start.60
  167.4 11.0 copy-start.28
  182.1 124.3 %copy-start.8 = (bf16[256,1024]{1,0:T(8,128)(2,1)}, bf16[256,1024]{1,0:T(8,128)(2,1)S(1)}, u32[]{:S(2)}) copy-start(bf16[256,1024]{1,0:T(8,128)(2,1)S(1)} %multiply_convert_fusion.2) | copy-start | bytes 1572868
  372.8 10.3 copy-start.13
  383.1 2.7 copy-start.32
  383.1 2.7 copy-start.11
  385.7 5.7 copy-start.36
  385.8 7.0 copy-start.16
  391.4 4.1 copy-start.24
  407.3 7.2 copy-start.25
  439.8 4.6 copy-start.39
  439.8 4.6 copy-start.41
  439.8 4.7 copy-start.15
  439.8 4.7 copy-start.44
  439.8 4.7 copy-start.61
  439.8 5.1 copy-start.50
  439.8 210.1 %reduce-scatter.17.cloned.1.call-start = ((), (), s32[]{:S(2)}) async-start(), calls=%async_computation.20 | async-start | bytes 2621440 | tf_op jit(solution)/shard_map/reduce_scatter | solution.py:343
  444.0 229.5 %reduce-scatter.11.cloned.1.call-start = ((), (), s32[]{:S(2)}) async-start(), calls=%async_computation.17 | async-start | bytes 2621440 | tf_op jit(solution)/shard_map/reduce_scatter | solution.py:334
  445.3 165.2 %copy-start.26 = (bf16[256,16,64]{0,2,1:T(8,128)(2,1)}, bf16[256,16,64]{0,2,1:T(8,128)(2,1)S(1)}, u32[]{:S(2)}) copy-start(bf16[256,16,64]{0,2,1:T(8,128)(2,1)S(1)} %fusion.69) | copy-start | bytes 1572868
  445.4 165.2 %copy-start.23 = (f32[256,8,64]{0,2,1:T(8,128)S(1)}, f32[256,8,64]{0,2,1:T(8,128)}, u32[]{:S(2)}) copy-start(f32[256,8,64]{0,2,1:T(8,128)} %copy-done.22) | copy-start | bytes 1572868
  445.4 165.2 %copy-start.46 = (f32[256,8]{0,1:T(8,128)S(1)}, f32[256,8]{0,1:T(8,128)}, u32[]{:S(2)}) copy-start(f32[256,8]{0,1:T(8,128)} %copy-done.45) | copy-start | bytes 24580
  445.4 165.2 %copy-start.58 = (f32[64]{0:T(128)S(1)}, f32[64]{0:T(128)}, u32[]{:S(2)}) copy-start(f32[64]{0:T(128)} %copy-done.57) | copy-start | bytes 772
  445.4 165.4 %copy-start.52 = (f32[256,8]{0,1:T(8,128)S(1)}, f32[256,8]{0,1:T(8,128)}, u32[]{:S(2)}) copy-start(f32[256,8]{0,1:T(8,128)} %copy-done.51) | copy-start | bytes 24580
  447.5 164.2 %copy-start.21 = (bf16[2,128,1024]{2,1,0:T(8,128)(2,1)S(1)}, bf16[2,128,1024]{2,1,0:T(8,128)(2,1)}, u32[]{:S(2)}) copy-start(bf16[2,128,1024]{2,1,0:T(8,128)(2,1)} %copy-done.19) | copy-start | bytes 1572868
  447.5 254.1 %reduce-scatter.13.cloned.1.call-start = ((), (), s32[]{:S(2)}) async-start(), calls=%async_computation.18 | async-start | bytes 1310720 | tf_op jit(solution)/shard_map/reduce_scatter | solution.py:337
  605.4 7.7 copy-start.18
  610.5 5.2 copy-start.9
  613.1 115.9 %reduce-scatter.15.cloned.1.call-start = ((), (), s32[]{:S(2)}) async-start(), calls=%async_computation.19 | async-start | bytes 1310720 | tf_op jit(solution)/shard_map/reduce_scatter | solution.py:340
  615.7 194.4 %reduce-scatter.19.cloned.1.call-start = ((), (), s32[]{:S(2)}) async-start(), calls=%async_computation.21 | async-start | bytes 11796480 | tf_op jit(solution)/shard_map/reduce_scatter | solution.py:346
  622.6 268.6 %reduce-scatter.21.cloned.1.call-start = ((), (), s32[]{:S(2)}) async-start(), calls=%async_computation.22 | async-start | bytes 11796480 | tf_op jit(solution)/shard_map/reduce_scatter | solution.py:349
  629.4 343.0 %reduce-scatter.23.cloned.1.call-start = ((), (), s32[]{:S(2)}) async-start(), calls=%async_computation.23 | async-start | bytes 11796480 | tf_op jit(solution)/shard_map/reduce_scatter | solution.py:352
  637.4 4.7 copy-start.12
  642.1 31.4 %copy-start.31 = (bf16[256,8,64]{0,2,1:T(8,128)(2,1)S(1)}, bf16[256,8,64]{0,2,1:T(8,128)(2,1)}, u32[]{:S(2)}) copy-start(bf16[256,8,64]{0,2,1:T(8,128)(2,1)} %copy-done.30) | copy-start | bytes 786436
  642.1 33.5 %copy-start.1 = (bf16[2,128,1024]{2,1,0:T(8,128)(2,1)S(1)}, bf16[2,128,1024]{2,1,0:T(8,128)(2,1)}, u32[]{:S(2)}) copy-start(bf16[2,128,1024]{2,1,0:T(8,128)(2,1)} %param.39) | copy-start | bytes 1572868
  642.1 33.5 %copy-start.48 = (f32[4,1,256]{2,1,0:T(1,128)S(1)}, f32[4,1,256]{2,1,0:T(1,128)}, u32[]{:S(2)}) copy-start(f32[4,1,256]{2,1,0:T(1,128)} %copy-done.47) | copy-start | bytes 12292
  642.1 33.5 %copy-start.56 = (f32[256]{0:T(256)S(1)}, f32[256]{0:T(256)}, u32[]{:S(2)}) copy-start(f32[256]{0:T(256)} %copy-done.55) | copy-start | bytes 3076
  650.0 34.6 %copy-start.54 = (f32[2,128]{1,0:T(2,128)S(1)}, f32[2,128]{1,0:T(2,128)}, u32[]{:S(2)}) copy-start(f32[2,128]{1,0:T(2,128)} %copy-done.53) | copy-start | bytes 3076
  675.6 296.8 %copy-start.42 = (bf16[256,1024]{1,0:T(8,128)(2,1)S(1)}, bf16[256,1024]{1,0:T(8,128)(2,1)}, u32[]{:S(2)}) copy-start(bf16[256,1024]{1,0:T(8,128)(2,1)} %reduce-scatter.17.cloned.1.call-done) | copy-start | bytes 1572868
  (20 other events, 25.8 us)
Sparse Core Ops, SparseCore 0:
  10.2 19.5 all-gather.10
  31.9 16.6 all-gather.12
  50.8 22.5 all-gather.16
  75.9 75.0 all-gather.14
  152.9 20.7 all-gather.18
  175.7 64.2 all-gather.22
  242.1 64.2 all-gather.20
  308.5 64.2 all-gather.24
  439.9 165.5 reduce-scatter.8
  608.5 30.3 reduce-scatter.16
  642.1 31.4 reduce-scatter.10
  676.6 24.8 reduce-scatter.12
  704.1 24.8 reduce-scatter.14
  731.6 78.4 reduce-scatter.18
  812.7 78.4 reduce-scatter.20
  893.8 78.4 reduce-scatter.22
where the time goes:
time: 1640 us; the launch traced here: 1650 us
  waiting for transfers between devices  722 us (44%)
  blocking collectives  692 us (42%)
  matrix products  107 us (7%)
  local copies, waits for them, and re-layouts  54.8 us (3%)
  other arithmetic  48.2 us (3%)
  between operations  20 us (1%)
    psum x1, blocking collectives, per_device(): lax.psum((own_query, own_key, own_value, own_output, own_gate, own_up, ow...  666 us
    reduce_scatter x1, waiting for transfers between devices, per_device(): lax.psum_scatter(jnp.stack(kv_terms), 'ctx', scatter_dimension=1, tiled=T...  158 us
    reduce_scatter x1, waiting for transfers between devices, per_device(): lax.psum_scatter(gate_part.astype(jnp.bfloat16), 'fsdp', scatter_dimensio...  81.1 us
    reduce_scatter x1, waiting for transfers between devices, per_device(): lax.psum_scatter(down_part.astype(jnp.bfloat16), 'fsdp', scatter_dimensio...  81.1 us
    reduce_scatter x1, waiting for transfers between devices, per_device(): lax.psum_scatter(up_part.astype(jnp.bfloat16), 'fsdp', scatter_dimension=...  81.1 us
    all_gather x1, waiting for transfers between devices, per_device(): kv_whole = lax.all_gather(kv_local, 'ctx', axis=1, tiled=True)  67.3 us
    all_gather x1, waiting for transfers between devices, per_device(): lax.all_gather(w_gate.astype(jnp.bfloat16), 'fsdp', axis=0, tiled=True)  58.5 us
    all_gather x1, waiting for transfers between devices, per_device(): lax.all_gather(w_down.astype(jnp.bfloat16), 'fsdp', axis=0, tiled=True)  58.3 us
  transfers between devices with their start and end apart: 16, of which 12 were waited for; matrix products, arithmetic and copies ran while one was open for 8% of the time, Pallas kernels for 0%

commit v1 on v0

v1 whole, which is shorter than its diff:
```python
import functools

import jax
import jax.numpy as jnp
from jax import lax
from jax.experimental import pallas as pl
from jax.experimental.pallas import tpu as pltpu
from jax.sharding import PartitionSpec as P

HEADS = 16
KV_HEADS = 8
HEAD = 64
GROUP = HEADS // KV_HEADS


epsilon = 1e-05
rope_base = 1000000.0
masked = -1e30
F32 = jnp.float32
BF16 = jnp.bfloat16


def rms_scale(values, scales):
    return values * lax.rsqrt(jnp.mean(values * values, axis=-1, keepdims=True) + epsilon) * scales


def rotate(values, cosine, sine_part):
    half_width = values.shape[-1] // 2
    first_half = values[..., :half_width]
    second_half = values[..., half_width:]
    return jnp.concatenate(
        [
            first_half * cosine - second_half * sine_part,
            second_half * cosine + first_half * sine_part,
        ],
        axis=-1,
    )


def angles(positions, head_width):
    frequency = rope_base ** (-jnp.arange(0, head_width, 2).astype(F32) / head_width)
    turned = positions.astype(F32)[..., None] * frequency
    return (jnp.cos(turned), jnp.sin(turned))


def prepare(shaped, scales, cosine, sine_part):
    return rotate(rms_scale(shaped, scales), cosine[:, None], sine_part[:, None])


def swiglu(gate_proj, up_proj):
    return gate_proj * jax.nn.sigmoid(gate_proj) * up_proj


def dot_over(left, right, left_dim, right_dim):
    return lax.dot_general(
        left, right, (((left_dim,), (right_dim,)), ((), ())), preferred_element_type=F32
    )


def product(left, right):
    return dot_over(left, right, 1, 0)


def by_transpose(left, right):
    return dot_over(left, right, 1, 1)


def transpose_by(left, right):
    return dot_over(left, right, 0, 0)


def swap(values, axis, step):
    size = lax.axis_size(axis)
    return lax.ppermute(values, axis, [(i, i ^ step) for i in range(size)])


def pick(values, index, axis=0):
    return lax.dynamic_index_in_dim(values, index, axis, keepdims=False)


def gather_near(values):
    far = swap(values, "fsdp", 2)
    near = swap(values, "fsdp", 1)
    return [values, near, far, swap(far, "fsdp", 1)]


def scatter_near(blocks):
    got = swap(jnp.concatenate([blocks[1], blocks[3]], axis=0), "fsdp", 1)
    rows = blocks[0].shape[0]
    mine = blocks[0].astype(F32) + got[:rows].astype(F32)
    far = (blocks[2].astype(F32) + got[rows:].astype(F32)).astype(BF16)
    return mine, swap(far, "fsdp", 2)


def ctx_bits():
    size = lax.axis_size("ctx")
    bits = []
    step = 1
    while step < size:
        bits.append(step)
        step *= 2
    return bits


def ctx_scatter(values, axis):
    me = lax.axis_index("ctx")
    for step in ctx_bits():
        shape = values.shape
        halves = values.reshape(shape[:axis] + (2, shape[axis] // 2) + shape[axis + 1 :])
        mine = (me // step) % 2
        got = swap(pick(halves, 1 - mine, axis), "ctx", step)
        values = (pick(halves, mine, axis).astype(F32) + got.astype(F32)).astype(BF16)
    return values


def ctx_gather(values, axis):
    me = lax.axis_index("ctx")
    for step in reversed(ctx_bits()):
        mine = (me // step) % 2
        got = swap(values, "ctx", step)
        first = jnp.where(mine == 0, values, got)
        second = jnp.where(mine == 0, got, values)
        values = jnp.concatenate([first, second], axis=axis)
    return values


def two_heads(block):
    return jnp.concatenate([block[:, :HEAD], block[:, HEAD:]], axis=0)


def side_by_side(stacked):
    rows = stacked.shape[0] // 2
    return jnp.concatenate([stacked[:rows], stacked[rows:]], axis=1)


def allowed_mask(rows, count, first_query, first_key, seq_len):
    query_slot = first_query + lax.broadcasted_iota(jnp.int32, (rows, count), 0) % (rows // GROUP)
    key_slot = first_key + lax.broadcasted_iota(jnp.int32, (rows, count), 1)
    return (key_slot <= query_slot) & (key_slot < seq_len)


def whole_row(q_ref, kv_ref, index, seq_len):
    slots = q_ref.shape[2]
    count = (index + 1) * slots
    query = two_heads(q_ref[index, 0]) * (HEAD**-0.5)
    both = kv_ref[: index + 1, 0].reshape(count, 2 * HEAD)
    key, value = both[:, :HEAD], both[:, HEAD:]
    scores = by_transpose(query, key)
    scores = jnp.where(
        allowed_mask(GROUP * slots, count, index * slots, 0, seq_len), scores, masked
    )
    exponent = jnp.exp(scores - jnp.max(scores, axis=-1, keepdims=True))
    weights = exponent * (1.0 / jnp.sum(exponent, axis=-1, keepdims=True))
    return query, key, value, weights


def forward_small(info_ref, q_ref, kv_ref, out_ref):
    seq_len = info_ref[pl.program_id(0) + 1]
    slots = q_ref.shape[2]
    for index in range(q_ref.shape[0]):

        @pl.when(index * slots < seq_len)
        def _():
            _, _, value, weights = whole_row(q_ref, kv_ref, index, seq_len)
            out_ref[index, 0] = side_by_side(product(weights.astype(BF16), value)).astype(BF16)

        @pl.when(index * slots >= seq_len)
        def _():
            out_ref[index, 0] = jnp.zeros(out_ref.shape[2:], BF16)


def backward_small(info_ref, q_ref, kv_ref, grad_ref, out_ref, key_acc, value_acc):
    seq_len = info_ref[pl.program_id(0) + 1]
    blocks, _, slots, _ = q_ref.shape
    key_acc[...] = jnp.zeros_like(key_acc)
    value_acc[...] = jnp.zeros_like(value_acc)
    for index in range(blocks):

        @pl.when(index * slots < seq_len)
        def _():
            count = (index + 1) * slots
            query, key, value, weights = whole_row(q_ref, kv_ref, index, seq_len)
            grad = two_heads(grad_ref[index, 0])
            grad_weights = by_transpose(grad, value)
            delta = jnp.sum(weights * grad_weights, axis=-1, keepdims=True)
            grad_scores = (weights * (grad_weights - delta)).astype(BF16)
            out_ref[index, 0, :, : 2 * HEAD] = side_by_side(
                product(grad_scores, key) * (HEAD**-0.5)
            ).astype(BF16)
            key_acc[:count] += transpose_by(grad_scores, query)
            value_acc[:count] += transpose_by(weights.astype(BF16), grad)

        @pl.when(index * slots >= seq_len)
        def _():
            out_ref[index, 0, :, : 2 * HEAD] = jnp.zeros((slots, 2 * HEAD), BF16)

    for index in range(blocks):
        rows = slice(index * slots, (index + 1) * slots)
        out_ref[index, 0, :, 2 * HEAD :] = jnp.concatenate(
            [key_acc[rows], value_acc[rows]], axis=1
        ).astype(BF16)


def row_stats(query, kv_ref, index, first_query, seq_len):
    slots = kv_ref.shape[2]
    rows = query.shape[0]

    def scores_of(block):
        both = kv_ref[block, 0]
        scores = by_transpose(query, both[:, :HEAD])
        allowed = allowed_mask(rows, slots, first_query, block * slots, seq_len)
        return both, jnp.where(allowed, scores, masked)

    def step(block, state):
        top, total = state
        _, scores = scores_of(block)
        new_top = jnp.maximum(top, jnp.max(scores, axis=-1, keepdims=True))
        grown = jnp.sum(jnp.exp(scores - new_top), axis=-1, keepdims=True)
        return new_top, total * jnp.exp(top - new_top) + grown

    start = (jnp.full((rows, 1), masked, F32), jnp.zeros((rows, 1), F32))
    top, total = lax.fori_loop(0, index + 1, step, start)
    inverse = 1.0 / total

    def weights_of(block):
        both, scores = scores_of(block)
        return both, jnp.exp(scores - top) * inverse

    return weights_of


def forward_large(info_ref, q_ref, kv_ref, out_ref):
    seq_len = info_ref[pl.program_id(0) + 1]
    slots = q_ref.shape[2]
    index = info_ref[0] + pl.program_id(1)
    live = index * slots < seq_len

    @pl.when(live)
    def _():
        query = two_heads(q_ref[0, 0]) * (HEAD**-0.5)
        weights_of = row_stats(query, kv_ref, index, index * slots, seq_len)

        def step(block, total):
            both, weights = weights_of(block)
            return total + product(weights.astype(BF16), both[:, HEAD:])

        total = lax.fori_loop(0, index + 1, step, jnp.zeros((GROUP * slots, HEAD), F32))
        out_ref[0, 0] = side_by_side(total).astype(BF16)

    @pl.when(jnp.logical_not(live))
    def _():
        out_ref[0, 0] = jnp.zeros(out_ref.shape[2:], BF16)


def backward_large(info_ref, q_ref, kv_ref, grad_ref, out_ref, kv_out_ref):
    seq_len = info_ref[pl.program_id(0) + 1]
    slots = q_ref.shape[2]
    index = info_ref[0] + pl.program_id(1)
    live = index * slots < seq_len

    @pl.when(pl.program_id(1) == 0)
    def _():
        kv_out_ref[...] = jnp.zeros_like(kv_out_ref)

    @pl.when(live)
    def _():
        query = two_heads(q_ref[0, 0]) * (HEAD**-0.5)
        grad = two_heads(grad_ref[0, 0])
        weights_of = row_stats(query, kv_ref, index, index * slots, seq_len)

        def delta_step(block, total):
            both, weights = weights_of(block)
            grad_weights = by_transpose(grad, both[:, HEAD:])
            return total + jnp.sum(weights * grad_weights, axis=-1, keepdims=True)

        delta = lax.fori_loop(0, index + 1, delta_step, jnp.zeros((GROUP * slots, 1), F32))

        def step(block, total):
            both, weights = weights_of(block)
            grad_weights = by_transpose(grad, both[:, HEAD:])
            grad_scores = (weights * (grad_weights - delta)).astype(BF16)
            kv_out_ref[block, 0] += jnp.concatenate(
                [transpose_by(grad_scores, query), transpose_by(weights.astype(BF16), grad)], axis=1
            )
            return total + product(grad_scores, both[:, :HEAD])

        total = lax.fori_loop(0, index + 1, step, jnp.zeros((GROUP * slots, HEAD), F32))
        out_ref[0, 0] = side_by_side(total * (HEAD**-0.5)).astype(BF16)

    @pl.when(jnp.logical_not(live))
    def _():
        out_ref[0, 0] = jnp.zeros(out_ref.shape[2:], BF16)


def attention_cost(q_blocks, k_blocks, seqs, slots, products):
    pairs = seqs * GROUP * q_blocks * k_blocks * slots * slots // 2
    return pl.CostEstimate(
        flops=pairs * HEAD * 2 * products,
        transcendentals=pairs,
        bytes_accessed=4 * seqs * slots * 4 * HEAD * (q_blocks + k_blocks),
    )


def attention(info, mixed, shared, grad=None):
    blocks, seqs, slots, _ = mixed.shape
    wide = 2 * HEAD
    small = shared is mixed
    k_blocks = shared.shape[0]
    params = dict(vmem_limit_bytes=48 * 1024 * 1024)
    cost = attention_cost(blocks, k_blocks, seqs, slots, 2 if grad is None else 5)
    if small:
        whole = lambda part: pl.BlockSpec(
            (blocks, 1, slots, wide), lambda seq, info: (0, seq, 0, part)
        )
        if grad is None:
            return pl.pallas_call(
                forward_small,
                out_shape=jax.ShapeDtypeStruct((blocks, seqs, slots, wide), BF16),
                grid_spec=pltpu.PrefetchScalarGridSpec(
                    num_scalar_prefetch=1,
                    grid=(seqs,),
                    in_specs=[whole(0), whole(1)],
                    out_specs=whole(0),
                ),
                compiler_params=pltpu.CompilerParams(**params),
                cost_estimate=cost,
            )(info, mixed, mixed)
        return pl.pallas_call(
            backward_small,
            out_shape=jax.ShapeDtypeStruct((blocks, seqs, slots, 2 * wide), BF16),
            grid_spec=pltpu.PrefetchScalarGridSpec(
                num_scalar_prefetch=1,
                grid=(seqs,),
                in_specs=[whole(0), whole(1), whole(0)],
                out_specs=pl.BlockSpec(
                    (blocks, 1, slots, 2 * wide), lambda seq, info: (0, seq, 0, 0)
                ),
                scratch_shapes=[pltpu.VMEM((blocks * slots, HEAD), F32)] * 2,
            ),
            compiler_params=pltpu.CompilerParams(**params),
            cost_estimate=cost,
        )(info, mixed, mixed, grad)
    one = pl.BlockSpec((1, 1, slots, wide), lambda seq, block, info: (block, seq, 0, 0))
    every = pl.BlockSpec((k_blocks, 1, slots, wide), lambda seq, block, info: (0, seq, 0, 0))
    out = jax.ShapeDtypeStruct((blocks, seqs, slots, wide), BF16)
    if grad is None:
        return pl.pallas_call(
            forward_large,
            out_shape=out,
            grid_spec=pltpu.PrefetchScalarGridSpec(
                num_scalar_prefetch=1, grid=(seqs, blocks), in_specs=[one, every], out_specs=one
            ),
            compiler_params=pltpu.CompilerParams(**params),
            cost_estimate=cost,
        )(info, mixed, shared)
    return pl.pallas_call(
        backward_large,
        out_shape=(out, jax.ShapeDtypeStruct((k_blocks, seqs, slots, wide), F32)),
        grid_spec=pltpu.PrefetchScalarGridSpec(
            num_scalar_prefetch=1,
            grid=(seqs, blocks),
            in_specs=[one, every, one],
            out_specs=(one, every),
        ),
        compiler_params=pltpu.CompilerParams(**params),
        cost_estimate=cost,
    )(info, mixed, shared, grad)


def per_device(
    inputs,
    lengths,
    positions,
    cotangent,
    w_query,
    w_key,
    w_value,
    w_output,
    w_gate,
    w_up,
    w_down,
    attn_gain,
    ffn_gain,
    query_gain,
    key_gain,
):
    groups, slot_count, model_width = inputs.shape
    row_count = groups * slot_count
    own_rows = w_query.shape[0]
    ctx_size = lax.axis_size("ctx")
    fsdp_size = lax.axis_size("fsdp")
    me_f = lax.axis_index("fsdp")
    me_c = lax.axis_index("ctx")
    inner = min(ctx_size, KV_HEADS)
    outer = ctx_size // inner
    inner_groups = [[o * inner + i for i in range(inner)] for o in range(outer)]
    outer_groups = [[o * inner + i for o in range(outer)] for i in range(inner)]
    mix = 4 * HEAD
    ff_own = w_down.shape[0]

    slots = me_c * slot_count + jnp.arange(slot_count)
    valid = (slots[None, :] < lengths[:, None]).astype(F32).reshape(row_count, 1)
    info = jnp.concatenate([(me_c // inner * inner)[None].astype(jnp.int32), lengths])

    gains = jnp.concatenate([attn_gain, ffn_gain, query_gain, key_gain]).astype(BF16)
    gains = lax.all_gather(gains, "fsdp", axis=0, tiled=False).astype(F32)
    small = query_gain.shape[0]
    attn_scale = gains[:, :own_rows].reshape(-1)
    ffn_scale = gains[:, own_rows : 2 * own_rows].reshape(-1)
    qgain_scale = gains[:, 2 * own_rows : 2 * own_rows + small].reshape(-1)
    kgain_scale = gains[:, 2 * own_rows + small :].reshape(-1)

    qkv_own = jnp.concatenate(
        [
            w_query.reshape(own_rows, KV_HEADS, GROUP * HEAD),
            w_key.reshape(own_rows, KV_HEADS, HEAD),
            w_value.reshape(own_rows, KV_HEADS, HEAD),
        ],
        axis=-1,
    ).astype(BF16)
    qkv_weight = lax.all_gather(
        qkv_own.reshape(own_rows, KV_HEADS * mix), "fsdp", axis=0, tiled=True
    )
    output_weight = lax.all_gather(w_output.astype(BF16), "fsdp", axis=0, tiled=True)
    down_weight = w_down.astype(BF16)
    gu_own = jnp.concatenate(
        [
            w_gate.reshape(own_rows, fsdp_size, ff_own),
            w_up.reshape(own_rows, fsdp_size, ff_own),
        ],
        axis=-1,
    ).astype(BF16)
    gu_own = gu_own.transpose(1, 0, 2)
    gu_parts = [pick(gu_own, me_f)]
    for step in range(1, fsdp_size):
        gu_parts.append(swap(pick(gu_own, me_f ^ step), "fsdp", step))
    gu_weight = jnp.zeros_like(gu_own)
    for step in range(fsdp_size):
        gu_weight = lax.dynamic_update_index_in_dim(gu_weight, gu_parts[step], me_f ^ step, 0)
    gu_weight = gu_weight.reshape(fsdp_size * own_rows, 2 * ff_own)

    flat = inputs.reshape(row_count, model_width).astype(F32)
    cosine, sine_part = angles(positions.reshape(row_count), HEAD)
    normed_low = rms_scale(flat, attn_scale).astype(BF16)
    projected = product(normed_low, qkv_weight).reshape(row_count, KV_HEADS, mix)
    query_proj = projected[..., : GROUP * HEAD].reshape(row_count, HEADS, HEAD)
    key_proj = projected[..., GROUP * HEAD : GROUP * HEAD + HEAD]
    query_low = prepare(query_proj, qgain_scale, cosine, sine_part).astype(BF16)
    key_low = prepare(key_proj, kgain_scale, cosine, sine_part).astype(BF16)
    value_low = projected[..., GROUP * HEAD + HEAD :].astype(BF16)
    mixed = jnp.concatenate(
        [query_low.reshape(row_count, KV_HEADS, GROUP * HEAD), key_low, value_low], axis=-1
    ).transpose(1, 0, 2)

    def exchange(values):
        shape = values.shape
        return lax.all_to_all(values, "ctx", 0, 0, axis_index_groups=inner_groups, tiled=True)

    heads_each = KV_HEADS // inner
    mixed = exchange(mixed).reshape(inner, heads_each, groups, slot_count, mix)
    mixed = mixed.transpose(0, 1, 2, 3, 4).reshape(inner, heads_each * groups, slot_count, mix)
    if outer == 1:
        shared = mixed
    else:
        shared = lax.all_gather(
            mixed[..., 2 * HEAD :], "ctx", axis=0, axis_index_groups=outer_groups, tiled=True
        )
    attended = attention(info, mixed, shared)
    attended_low = (
        exchange(attended.reshape(KV_HEADS, row_count, 2 * HEAD))
        .transpose(1, 0, 2)
        .reshape(row_count, HEADS * HEAD)
    )
    hidden_res = flat + product(attended_low, output_weight)

    mid_low = rms_scale(hidden_res, ffn_scale).astype(BF16)
    mid_all = jnp.concatenate(gather_near(mid_low), axis=0)
    outer_grad = cotangent.reshape(row_count, model_width).astype(F32) * valid
    outer_low = outer_grad.astype(BF16)
    outer_all = jnp.concatenate(gather_near(outer_low), axis=0)
    gate_up = product(mid_all, gu_weight)
    gate_proj, up_proj = gate_up[:, :ff_own], gate_up[:, ff_own:]
    inner_low = swiglu(gate_proj, up_proj).astype(BF16)
    down_part = transpose_by(inner_low, outer_all).astype(BF16)
    down_sum = ctx_scatter(down_part.reshape(ctx_size, ff_own // ctx_size, model_width), 0)
    grad_inner = by_transpose(outer_all, down_weight)
    _, pull_swiglu = jax.vjp(swiglu, gate_proj, up_proj)
    grad_gate, grad_up = pull_swiglu(grad_inner)
    grad_gu = jnp.concatenate([grad_gate.astype(BF16), grad_up.astype(BF16)], axis=-1)
    grad_mid_part = by_transpose(grad_gu, gu_weight).astype(BF16)
    mine, far = scatter_near(jnp.split(grad_mid_part, fsdp_size, axis=0))
    grad_mid = mine + far.astype(F32)
    gu_part = transpose_by(mid_all, grad_gu).astype(BF16)
    gu_sum = ctx_scatter(
        gu_part.reshape(fsdp_size, ctx_size, own_rows // ctx_size, 2 * ff_own), 1
    )
    result_part = product(inner_low, down_weight).astype(BF16)
    mine, far = scatter_near(jnp.split(result_part, fsdp_size, axis=0))
    result = valid * (hidden_res + (mine + far.astype(F32)))
    block_output = result.astype(BF16).reshape(groups, slot_count, model_width)

    _, pull_mid = jax.vjp(rms_scale, hidden_res, ffn_scale)
    grad_hidden_norm, ffn_part = pull_mid(grad_mid)
    grad_hidden = outer_grad + grad_hidden_norm
    grad_attn_low = grad_hidden.astype(BF16)

    output_part = transpose_by(attended_low, grad_attn_low).astype(BF16)
    grad_heads_low = by_transpose(grad_attn_low, output_weight).astype(BF16)
    grad_heads = exchange(
        grad_heads_low.reshape(row_count, KV_HEADS, 2 * HEAD).transpose(1, 0, 2)
    ).reshape(inner, heads_each * groups, slot_count, 2 * HEAD)
    if outer == 1:
        grad_mixed = attention(info, mixed, shared, grad_heads)
    else:
        grad_q, grad_kv = attention(info, mixed, shared, grad_heads)
        grad_kv = lax.psum_scatter(
            grad_kv, "ctx", scatter_dimension=0, axis_index_groups=outer_groups, tiled=True
        )
        grad_mixed = jnp.concatenate([grad_q, grad_kv.astype(BF16)], axis=-1)
    grad_mixed = exchange(grad_mixed.reshape(KV_HEADS, row_count, mix)).transpose(1, 0, 2)
    grad_query_rot = grad_mixed[..., : GROUP * HEAD].astype(F32).reshape(row_count, HEADS, HEAD)
    grad_key_rot = grad_mixed[..., GROUP * HEAD : GROUP * HEAD + HEAD].astype(F32)
    grad_value_low = grad_mixed[..., GROUP * HEAD + HEAD :]
    _, pull_query = jax.vjp(
        lambda shaped, scales: prepare(shaped, scales, cosine, sine_part), query_proj, qgain_scale
    )
    grad_query_proj, qgain_part = pull_query(grad_query_rot)
    _, pull_key = jax.vjp(
        lambda shaped, scales: prepare(shaped, scales, cosine, sine_part), key_proj, kgain_scale
    )
    grad_key_proj, kgain_part = pull_key(grad_key_rot)
    grad_qkv = jnp.concatenate(
        [
            grad_query_proj.astype(BF16).reshape(row_count, KV_HEADS, GROUP * HEAD),
            grad_key_proj.astype(BF16),
            grad_value_low,
        ],
        axis=-1,
    ).reshape(row_count, KV_HEADS * mix)
    qkv_part = transpose_by(normed_low, grad_qkv).astype(BF16)
    grad_normed = by_transpose(grad_qkv, qkv_weight)
    _, pull_input = jax.vjp(rms_scale, flat, attn_scale)
    grad_flat_norm, attn_part = pull_input(grad_normed)
    input_grad = (grad_hidden + grad_flat_norm).reshape(groups, slot_count, model_width)

    gain_parts = jnp.concatenate(
        [
            attn_part.reshape(fsdp_size, own_rows),
            ffn_part.reshape(fsdp_size, own_rows),
            qgain_part.reshape(fsdp_size, small),
            kgain_part.reshape(fsdp_size, small),
        ],
        axis=-1,
    )
    gain_sum = pick(lax.psum(gain_parts, ("ctx", "fsdp")), me_f)

    def own_block(part):
        blocks = part.reshape(fsdp_size, own_rows, part.shape[1])
        mine, far = scatter_near([pick(blocks, me_f ^ k) for k in range(fsdp_size)])
        return (mine + far.astype(F32)).astype(BF16)

    def ctx_sum(own):
        blocks = own.reshape(ctx_size, own_rows // ctx_size, own.shape[1])
        return ctx_gather(ctx_scatter(blocks, 0), 0).reshape(own.shape)

    output_grad = ctx_sum(own_block(output_part)).astype(F32)
    qkv_grad = ctx_sum(own_block(qkv_part)).reshape(own_rows, KV_HEADS, mix)
    query_grad = qkv_grad[..., : GROUP * HEAD].reshape(own_rows, HEADS * HEAD).astype(F32)
    key_grad = (
        qkv_grad[..., GROUP * HEAD : GROUP * HEAD + HEAD]
        .reshape(own_rows, KV_HEADS * HEAD)
        .astype(F32)
    )
    value_grad = (
        qkv_grad[..., GROUP * HEAD + HEAD :].reshape(own_rows, KV_HEADS * HEAD).astype(F32)
    )
    down_grad = ctx_gather(down_sum, 0).reshape(ff_own, model_width).astype(F32)

    gu_sum = gu_sum.reshape(fsdp_size, own_rows // ctx_size, 2 * ff_own)
    gu_rows = jnp.zeros_like(gu_sum)
    for step in range(fsdp_size):
        block = pick(gu_sum, me_f ^ step)
        if step:
            block = swap(block, "fsdp", step)
        gu_rows = lax.dynamic_update_index_in_dim(gu_rows, block, me_f ^ step, 0)
    gu_all = ctx_gather(gu_rows[None], 0)
    gu_all = gu_all.transpose(0, 2, 1, 3).reshape(own_rows, fsdp_size, 2 * ff_own)
    gate_grad = gu_all[..., :ff_own].reshape(own_rows, fsdp_size * ff_own).astype(F32)
    up_grad = gu_all[..., ff_own:].reshape(own_rows, fsdp_size * ff_own).astype(F32)

    return (
        block_output,
        input_grad,
        query_grad,
        key_grad,
        value_grad,
        output_grad,
        gate_grad,
        up_grad,
        down_grad,
        gain_sum[:own_rows],
        gain_sum[own_rows : 2 * own_rows],
        gain_sum[2 * own_rows : 2 * own_rows + small],
        gain_sum[2 * own_rows + small :],
    )


def solution(mesh):
    return jax.shard_map(
        per_device,
        mesh=mesh,
        in_specs=(
            P("fsdp", "ctx", None),
            P("fsdp"),
            P("fsdp", "ctx"),
            P("fsdp", "ctx", None),
            P("fsdp", None),
            P("fsdp", None),
            P("fsdp", None),
            P("fsdp", None),
            P("fsdp", None),
            P("fsdp", None),
            P("fsdp", None),
            P("fsdp"),
            P("fsdp"),
            P("fsdp"),
            P("fsdp"),
        ),
        out_specs=(
            P("fsdp", "ctx", None),
            P("fsdp", "ctx", None),
            P("fsdp", None),
            P("fsdp", None),
            P("fsdp", None),
            P("fsdp", None),
            P("fsdp", None),
            P("fsdp", None),
            P("fsdp", None),
            P("fsdp"),
            P("fsdp"),
            P("fsdp"),
            P("fsdp"),
        ),
        check_vma=False,
    )
```

time: 1640 us -> 608 us (0.37)
  blocking collectives: 692 us -> 57.2 us
  waiting for transfers between devices: 722 us -> 251 us
  starting transfers between devices: 0.92 us -> 68.4 us
  matrix products: 107 us -> 54.4 us
  local copies, waits for them, and re-layouts: 54.8 us -> 84.8 us
  Pallas kernels: 0 us -> 18.1 us
    psum x1, blocking collectives: 666 us -> 51.1 us  [per_device(): gain_sum = pick(lax.psum(gain_parts, ('ctx', 'fsdp')), me_f)]
    reduce_scatter x8 -> x0, waiting for transfers between devices: 467 us -> none  [the longest x1 158 us: per_device(): lax.psum_scatter(jnp.stack(kv_terms), 'ctx', scatter_dimension=1, tiled=T...]
    all_gather x8 -> x2, waiting for transfers between devices: 255 us -> 30.7 us  [the longest x1 30.7 us: per_device(): lax.all_gather(qkv_own.reshape(own_rows, KV_HEADS * mix), 'fsdp', axis=0,...]
    ppermute x0 -> x44, waiting for transfers between devices: none -> 218 us  [swap(): return lax.ppermute(values, axis, [(i, i ^ step) for i in range(size)])]
    dot_general x35 -> x12, matrix products: 107 us -> 54.4 us  [dot_over(): lax.dot_general(left, right, (((left_dim,), (right_dim,)), ((), ())), pre...]
    ppermute x0 -> x44, starting transfers between devices: none -> 48.1 us  [swap(): return lax.ppermute(values, axis, [(i, i ^ step) for i in range(size)])]
    unnamed x133 -> x135, local copies, waits for them, and re-layouts: 7.73 us -> 32.7 us
    all_to_all x0 -> x4, starting transfers between devices: none -> 20 us  [exchange(): lax.all_to_all(values, 'ctx', 0, 0, axis_index_groups=inner_groups, tiled...]
  transfers between devices with their start and end apart: 16 -> 50, of which waited for: 12 -> 22; matrix products, arithmetic and copies ran while one was open for 8% -> 26% of each run, Pallas kernels for 0% -> 3%
where the time goes in v1:
time: 608 us; the launch traced here: 602 us
  waiting for transfers between devices  251 us (41%)
  local copies, waits for them, and re-layouts  84.8 us (14%)
  starting transfers between devices  68.4 us (11%)
  blocking collectives  57.2 us (9%)
  matrix products  54.4 us (9%)
  other arithmetic  52.6 us (9%)
  Pallas kernels  18.1 us (3%)
  between operations  16 us (3%)
    ppermute x44, waiting for transfers between devices, swap(): return lax.ppermute(values, axis, [(i, i ^ step) for i in range(size)])  218 us
    dot_general x12, matrix products, dot_over(): lax.dot_general(left, right, (((left_dim,), (right_dim,)), ((), ())), pre...  54.4 us
    psum x1, blocking collectives, per_device(): gain_sum = pick(lax.psum(gain_parts, ('ctx', 'fsdp')), me_f)  51.1 us
    ppermute x44, starting transfers between devices, swap(): return lax.ppermute(values, axis, [(i, i ^ step) for i in range(size)])  48.1 us
    unnamed x135, local copies, waits for them, and re-layouts  32.7 us
    all_gather x1, waiting for transfers between devices, per_device(): lax.all_gather(qkv_own.reshape(own_rows, KV_HEADS * mix), 'fsdp', axis=0,...  30.7 us
    all_to_all x4, starting transfers between devices, exchange(): lax.all_to_all(values, 'ctx', 0, 0, axis_index_groups=inner_groups, tiled...  20 us
  transfers between devices with their start and end apart: 50, of which 22 were waited for; matrix products, arithmetic and copies ran while one was open for 26% of the time, Pallas kernels for 3%

profile of v1, /device:TPU:0, one launch (start us, length us, event | category | flops | bytes accessed | tf_op | source)
XLA Modules:
  0.0 602.1 jit_solution(5895848066087796819)
XLA Ops:
  11.8 6.1 %all-gather = bf16[4,1,544]{2,1,0:T(2,128)(2,1)S(1)} all-gather(bf16[1,1,544]{2,1,0:T(2,128)(2,1)S(1)} %maximum_bitcast_fusion.1), channel_id=1, replica_groups=mesh['ctx'=8,'fsdp'=4] {'fsdp'}, dimensions={0}, use_global_device_ids=true | all-gather | bytes 5440 | tf_op jit(solution)/shard_map/all_gather | solution.py:406
  18.9 30.7 %all-gather.4.cloned.1.call-done = bf16[1024,2048]{0,1:T(8,128)(2,1)} async-done(((bf16[256,2048]{0,1:T(8,128)(2,1)}), bf16[1024,2048]{0,1:T(8,128)(2,1)}) %all-gather.4.cloned.1.call-update) | async-done | bytes 4194320 | tf_op jit(solution)/shard_map/all_gather | solution.py:421
  49.5 3.5 fusion.57
  56.1 5.5 all-to-all-start
  62.7 3.4 copy.132
  66.2 4.9 copy.133
  71.0 3.6 fusion.13
  74.7 2.5 copy.135
  79.0 2.5 copy.136
  89.4 7.9 %shard_map.246 = bf16[8,2,128,128]{3,2,1,0:T(8,128)(2,1)S(1)} custom-call(s32[3]{0:T(128)S(1)} %pad_add_fusion.2.info_ref, bf16[8,2,128,256]{3,2,1,0:T(8,128)(2,1)S(1)} %bitcast.228, bf16[8,2,128,256]{3,2,1,0:T(8,128)(2,1)S(1)} %bitcast.229), custom_call_target="tpu_custom_call" | custom-call | flops 536870912 | bytes 4194304 | tf_op jit(solution)/shard_map/pallas_call | solution.py:316
  98.3 4.6 all-to-all-start.1
  102.9 2.5 broadcast_in_dim.65
  106.5 4.9 collective-permute-start.10
  111.4 2.4 bitcast_dynamic-update-slice_fusion.2
  114.2 2.4 multiply_reduce_fusion.4
  116.8 7.8 %collective-permute-start.1 = (bf16[256,1024]{1,0:T(8,128)(2,1)S(1)}, bf16[256,1024]{1,0:T(8,128)(2,1)S(1)}, u32[]{:S(2)}, u32[]{:S(2)}) collective-permute-start(bf16[256,1024]{1,0:T(8,128)(2,1)S(1)} %multiply_convert_fusion.3), channel_id=1, source_target_pairs={{0,2},{1,3},{2,0},{3,1},{4,6},{5,7},{6,4},{7,5},{8,10},{9,11},{10,... | collective-permute-start | bytes 1572872 | tf_op jit(solution)/shard_map/ppermute | solution.py:74
  124.6 2.4 bitcast_dynamic-update-slice_fusion.1
  126.9 32.2 %collective-permute-done.1 = bf16[256,1024]{1,0:T(8,128)(2,1)S(1)} collective-permute-done((bf16[256,1024]{1,0:T(8,128)(2,1)S(1)}, bf16[256,1024]{1,0:T(8,128)(2,1)S(1)}, u32[]{:S(2)}, u32[]{:S(2)}) %collective-permute-start.1) | collective-permute-done | bytes 524320 | tf_op jit(solution)/shard_map/ppermute | solution.py:74
  159.2 2.5 bitcast_dynamic-update-slice_fusion
  161.7 11.9 %fusion.38 = f32[1024,2304]{1,0:T(8,128)} fusion(bf16[1024,2304]{1,0:T(8,128)(2,1)} %bitcast.30, bf16[256,1024]{1,0:T(8,128)(2,1)S(1)} %collective-permute-done.2, bf16[256,1024]{1,0:T(8,128)(2,1)S(1)} %collective-permute-done.1, bf16[256,1024]{1,0:T(8,128)(2,1)S(1)} %collective-permute-done, bf16[256,1024]{1,0:T(8,128)(2,1)S(1)} %multiply_convert_fusion.3), kind=kOutput, calls=%fused_computation.156 | convolution fusion | flops 4840226816 | bytes 16252928 | tf_op jit(solution)/shard_map/dot_general | solution.py:55
  173.7 8.5 %fusion.2 = (bf16[1024,1152]{1,0:T(8,128)(2,1)S(1)}, bf16[1024,1152]{1,0:T(8,128)(2,1)S(1)}, bf16[1024,1152]{1,0:T(8,128)(2,1)S(1)}) fusion(f32[1024,2304]{1,0:T(8,128)} %fusion.38, f32[1152,1024]{1,0:T(8,128)S(1)} %bitcast.301, bf16[256,1024]{1,0:T(8,128)(2,1)S(1)} %collective-permute-done.10, bf16[256,1024]{1,0:T(8,128)(2,1)} %collective-permute-done.9, ...), kind=kOutput, calls=%fused_computation.12 | convolution fusion | flops 2444361728 | bytes 23330816 | tf_op jit(solution)/shard_map/dot_general | solution.py:55
  182.2 3.1 convolution_convert_fusion.3
  186.0 8.1 %fusion.11 = bf16[1024,1024]{1,0:T(8,128)(2,1)S(1)} fusion(bf16[1024,2304]{1,0:T(8,128)(2,1)} %bitcast.30, bf16[1024,1152]{1,0:T(8,128)(2,1)S(1)} %get-tuple-element.87, bf16[1024,1152]{1,0:T(8,128)(2,1)S(1)} %get-tuple-element.86), kind=kOutput, calls=%fused_computation.45 | convolution fusion | flops 4842323968 | bytes 11534336 | tf_op jit(solution)/shard_map/dot_general | solution.py:55
  195.1 4.0 convolution_convert_fusion.1
  200.9 7.8 %convolution_convert_fusion = bf16[1024,2304]{1,0:T(8,128)(2,1)S(1)} fusion(bf16[1024,1152]{1,0:T(8,128)(2,1)} %copy-done.56, bf16[1024,1152]{1,0:T(8,128)(2,1)} %copy-done.55, bf16[256,1024]{1,0:T(8,128)(2,1)S(1)} %copy-done.52, bf16[256,1024]{1,0:T(8,128)(2,1)S(1)} %collective-permute-done.1, bf16[256,1024]{1,0:T(8,128)(2,1)S(1)} %copy-done.50, ...), kind=kOutput, calls=%fused_computation.9 | convolution fusion | flops 4852023296 | bytes 11534336 | tf_op jit(solution)/shard_map/dot_general | solution.py:55
  208.7 1.7 dynamic-slice_bitcast_fusion
  215.1 13.1 %collective-permute-done.38 = bf16[4,144,1024]{2,1,0:T(8,128)(2,1)S(1)} collective-permute-done((bf16[4,144,1024]{2,1,0:T(8,128)(2,1)S(1)}, bf16[4,144,1024]{2,1,0:T(8,128)(2,1)S(1)}, u32[]{:S(2)}, u32[]{:S(2)}) %collective-permute-start.38) | collective-permute-done | bytes 1179680 | tf_op jit(solution)/shard_map/ppermute | solution.py:74
  232.2 5.5 collective-permute-done.7
  245.7 2.5 collective-permute-start.40
  249.6 11.8 %collective-permute-done.40 = bf16[1,144,1024]{2,1,0:T(8,128)(2,1)S(1)} collective-permute-done((bf16[1,144,1024]{2,1,0:T(8,128)(2,1)S(1)}, bf16[1,144,1024]{2,1,0:T(8,128)(2,1)S(1)}, u32[]{:S(2)}, u32[]{:S(2)}) %collective-permute-start.40) | collective-permute-done | bytes 294944 | tf_op jit(solution)/shard_map/ppermute | solution.py:74
  262.5 2.2 fusion.24
  267.0 5.5 all-to-all-start.2
  273.8 11.6 %collective-permute-done.41 = bf16[1,144,1024]{2,1,0:T(8,128)(2,1)} collective-permute-done((bf16[1,144,1024]{2,1,0:T(8,128)(2,1)S(1)}, bf16[1,144,1024]{2,1,0:T(8,128)(2,1)}, u32[]{:S(2)}, u32[]{:S(2)}) %collective-permute-start.41) | collective-permute-done | bytes 294944 | tf_op jit(solution)/shard_map/ppermute | solution.py:74
  289.1 3.0 fusion.3
  292.3 3.2 collective-permute-done.23
  296.2 2.0 collective-permute-start.24
  299.4 10.2 %shard_map.247 = bf16[8,2,128,256]{3,2,1,0:T(8,128)(2,1)S(1)} custom-call(s32[3]{0:T(128)S(1)} %pad_add_fusion.2.info_ref, bf16[8,2,128,256]{3,2,1,0:T(8,128)(2,1)S(1)} %bitcast.230, bf16[8,2,128,256]{3,2,1,0:T(8,128)(2,1)S(1)} %bitcast.231, bf16[8,2,128,128]{3,2,1,0:T(8,128)(2,1)S(1)} %bitcast.233), custom_call_target="tpu_custom_call" | custom-call | flops 1342177280 | bytes 4194304 | tf_op jit(solution)/shard_map/pallas_call | solution.py:328
  310.9 4.5 all-to-all-start.3
  316.4 2.9 collective-permute-start.25
  320.5 21.6 %collective-permute-done.25 = bf16[1,32,1024]{2,1,0:T(8,128)(2,1)S(1)} collective-permute-done((bf16[1,32,1024]{2,1,0:T(8,128)(2,1)S(1)}, bf16[1,32,1024]{2,1,0:T(8,128)(2,1)S(1)}, u32[]{:S(2)}, u32[]{:S(2)}) %collective-permute-start.25) | collective-permute-done | bytes 65568 | tf_op jit(solution)/shard_map/ppermute | solution.py:74
  342.1 3.5 collective-permute-start.26
  347.9 3.5 collective-permute-start.27
  354.4 2.5 collective-permute-start.28
  357.1 17.6 %collective-permute-done.28 = bf16[4,32,1024]{2,1,0:T(8,128)(2,1)S(1)} collective-permute-done((bf16[4,32,1024]{2,1,0:T(8,128)(2,1)S(1)}, bf16[4,32,1024]{2,1,0:T(8,128)(2,1)S(1)}, u32[]{:S(2)}, u32[]{:S(2)}) %collective-permute-start.28) | collective-permute-done | bytes 262176 | tf_op jit(solution)/shard_map/ppermute | solution.py:74
  375.9 5.7 collective-permute-done.31
  383.3 1.9 collective-permute-start.34
  386.2 3.7 collective-permute-done.33
  397.5 1.8 bitcast_dynamic-update-slice_fusion.4
  399.3 2.9 bitcast_convert_fusion
  402.1 26.1 %collective-permute-done.35 = bf16[1,4,32,2304]{3,2,0,1:T(8,128)(2,1)S(1)} collective-permute-done((bf16[1,4,32,2304]{3,2,0,1:T(8,128)(2,1)}, bf16[1,4,32,2304]{3,2,0,1:T(8,128)(2,1)S(1)}, u32[]{:S(2)}, u32[]{:S(2)}) %collective-permute-start.35) | collective-permute-done | bytes 589856 | tf_op jit(solution)/shard_map/ppermute | solution.py:74
  432.8 2.3 fusion.34
  435.4 51.1 %psum.7 = f32[4,544]{1,0:T(4,128)S(1)} all-reduce(f32[4,544]{1,0:T(4,128)S(1)} %pad_maximum_fusion.30), channel_id=1, replica_groups=mesh['ctx'=8,'fsdp'=4] {'ctx','fsdp'}, use_global_device_ids=true, to_apply=%region_12.13 | all-reduce | flops 2176 | bytes 17408 | tf_op jit(solution)/shard_map/psum | solution.py:555
  486.5 2.4 fusion.10
  489.0 2.4 collective-permute-start.15
  493.1 11.1 %collective-permute-done.15 = bf16[4,32,2048]{2,1,0:T(8,128)(2,1)S(1)} collective-permute-done((bf16[4,32,2048]{2,1,0:T(8,128)(2,1)S(1)}, bf16[4,32,2048]{2,1,0:T(8,128)(2,1)S(1)}, u32[]{:S(2)}, u32[]{:S(2)}) %collective-permute-start.15) | collective-permute-done | bytes 524320 | tf_op jit(solution)/shard_map/ppermute | solution.py:74
  505.7 5.6 collective-permute-done.16
  514.0 6.7 %collective-permute-done.17 = bf16[1,32,2048]{2,1,0:T(8,128)(2,1)S(1)} collective-permute-done((bf16[1,32,2048]{2,1,0:T(8,128)(2,1)S(1)}, bf16[1,32,2048]{2,1,0:T(8,128)(2,1)S(1)}, u32[]{:S(2)}, u32[]{:S(2)}) %collective-permute-start.17) | collective-permute-done | bytes 131104 | tf_op jit(solution)/shard_map/ppermute | solution.py:74
  520.9 32.1 %collective-permute-done.37 = bf16[4,4,32,2304]{3,2,0,1:T(8,128)(2,1)S(1)} collective-permute-done((bf16[4,4,32,2304]{3,2,0,1:T(8,128)(2,1)S(1)}, bf16[4,4,32,2304]{3,2,0,1:T(8,128)(2,1)S(1)}, u32[]{:S(2)}, u32[]{:S(2)}) %collective-permute-start.37) | collective-permute-done | bytes 2359328 | tf_op jit(solution)/shard_map/ppermute | solution.py:74
  553.9 6.2 %collective-permute-done.19 = bf16[2,32,2048]{2,1,0:T(8,128)(2,1)S(1)} collective-permute-done((bf16[2,32,2048]{2,1,0:T(8,128)(2,1)S(1)}, bf16[2,32,2048]{2,1,0:T(8,128)(2,1)S(1)}, u32[]{:S(2)}, u32[]{:S(2)}) %collective-permute-start.19) | collective-permute-done | bytes 262176 | tf_op jit(solution)/shard_map/ppermute | solution.py:74
  561.7 4.4 slice_convert_fusion
  566.1 6.0 %copy.146 = f32[256,4,1152]{0,2,1:T(8,128)} copy(f32[256,4,1152]{2,0,1:T(8,128)} %get-tuple-element.90) | data formatting | bytes 9437184 | tf_op jit(solution)/shard_map/convert_element_type | solution.py:588
  572.1 6.0 %copy.150 = f32[256,4608]{1,0:T(8,128)} copy(f32[256,4608]{0,1:T(8,128)} %bitcast.243) | data formatting | bytes 9437184
  578.2 6.0 %copy.147 = f32[256,4,1152]{0,2,1:T(8,128)} copy(f32[256,4,1152]{2,0,1:T(8,128)} %get-tuple-element.89) | data formatting | bytes 9437184 | tf_op jit(solution)/shard_map/convert_element_type | solution.py:589
  584.2 6.0 %copy.151 = f32[256,4608]{1,0:T(8,128)} copy(f32[256,4608]{0,1:T(8,128)} %bitcast.244) | data formatting | bytes 9437184
  (345 shorter events, 91.9 us)
Async XLA Ops:
  7.2 42.4 %all-gather.4.cloned.1.call-start = ((), (), s32[]{:S(2)}) async-start(), calls=%async_computation.4 | async-start | bytes 5242880 | tf_op jit(solution)/shard_map/all_gather | solution.py:421
  18.1 35.3 %copy-start.39 = (f32[64]{0:T(128)}, f32[64]{0:T(128)S(1)}, u32[]{:S(2)}) copy-start(f32[64]{0:T(128)S(1)} %mul.448) | copy-start | bytes 772
  18.2 35.4 %copy-start.37 = (f32[64]{0:T(128)}, f32[64]{0:T(128)S(1)}, u32[]{:S(2)}) copy-start(f32[64]{0:T(128)S(1)} %mul.465) | copy-start | bytes 772
  18.4 34.6 %copy-start.34 = (f32[2,128]{1,0:T(2,128)}, f32[2,128]{1,0:T(2,128)S(1)}, u32[]{:S(2)}) copy-start(f32[2,128]{1,0:T(2,128)S(1)} %fusion.29) | copy-start | bytes 3076
  18.9 34.2 %copy-start.17 = (bf16[2,128,1024]{2,1,0:T(8,128)(2,1)}, bf16[2,128,1024]{2,1,0:T(8,128)(2,1)S(1)}, u32[]{:S(2)}) copy-start(bf16[2,128,1024]{2,1,0:T(8,128)(2,1)S(1)} %fusion.31) | copy-start | bytes 1572868
  56.1 31.8 %all-to-all-start = ((bf16[8,256,256]{1,2,0:T(8,128)(2,1)}), bf16[8,256,256]{1,2,0:T(8,128)(2,1)}, u32[]{:S(2)}, u32[]{:S(2)}) async-start(bf16[8,256,256]{1,2,0:T(8,128)(2,1)} %maximum_bitcast_fusion), calls=%async_computation | async-start | bytes 2097152 | tf_op jit(solution)/shard_map/all_to_all | solution.py:457
  61.6 52.1 %all-gather.6.cloned.1.call-start = ((), (), s32[]{:S(2)}) async-start(), calls=%async_computation.5 | async-start | bytes 2621440 | tf_op jit(solution)/shard_map/all_gather | solution.py:424
  77.2 34.1 %collective-permute-start.3 = (bf16[256,2304]{1,0:T(8,128)(2,1)}, bf16[256,2304]{1,0:T(8,128)(2,1)}, u32[]{:S(2)}, u32[]{:S(2)}) collective-permute-start(bf16[256,2304]{1,0:T(8,128)(2,1)} %bitcast.281), channel_id=1, source_target_pairs={{0,1},{1,0},{2,3},{3,2},{4,5},{5,4},{6,7},{7,6},{8,9},{9,8},{10,11... | collective-permute-start | bytes 3538952 | tf_op jit(solution)/shard_map/ppermute | solution.py:74
  78.3 28.2 %collective-permute-start.9 = (bf16[256,1024]{1,0:T(8,128)(2,1)}, bf16[256,1024]{1,0:T(8,128)(2,1)}, u32[]{:S(2)}, u32[]{:S(2)}) collective-permute-start(bf16[256,1024]{1,0:T(8,128)(2,1)} %fusion.28), channel_id=1, source_target_pairs={{0,2},{1,3},{2,0},{3,1},{4,6},{5,7},{6,4},{7,5},{8,10},{9,11},{10,... | collective-permute-start | bytes 1572872 | tf_op jit(solution)/shard_map/ppermute | solution.py:74
  78.8 94.8 %collective-permute-start.8 = (bf16[256,1024]{1,0:T(8,128)(2,1)}, bf16[256,1024]{1,0:T(8,128)(2,1)}, u32[]{:S(2)}, u32[]{:S(2)}) collective-permute-start(bf16[256,1024]{1,0:T(8,128)(2,1)} %fusion.28), channel_id=1, source_target_pairs={{0,1},{1,0},{2,3},{3,2},{4,5},{5,4},{6,7},{7,6},{8,9},{9,8},{10,11... | collective-permute-start | bytes 1572872 | tf_op jit(solution)/shard_map/ppermute | solution.py:74
  81.5 43.1 %collective-permute-start.4 = (bf16[256,2304]{1,0:T(8,128)(2,1)}, bf16[256,2304]{1,0:T(8,128)(2,1)}, u32[]{:S(2)}, u32[]{:S(2)}) collective-permute-start(bf16[256,2304]{1,0:T(8,128)(2,1)} %bitcast.282), channel_id=1, source_target_pairs={{0,2},{1,3},{2,0},{3,1},{4,6},{5,7},{6,4},{7,5},{8,10},{9,11},{10,... | collective-permute-start | bytes 3538952 | tf_op jit(solution)/shard_map/ppermute | solution.py:74
  84.5 74.6 %collective-permute-start.5 = (bf16[256,2304]{1,0:T(8,128)(2,1)}, bf16[256,2304]{1,0:T(8,128)(2,1)}, u32[]{:S(2)}, u32[]{:S(2)}) collective-permute-start(bf16[256,2304]{1,0:T(8,128)(2,1)} %bitcast.280), channel_id=1, source_target_pairs={{0,3},{1,2},{2,1},{3,0},{4,7},{5,6},{6,5},{7,4},{8,11},{9,10},{10,... | collective-permute-start | bytes 3538952 | tf_op jit(solution)/shard_map/ppermute | solution.py:74
  98.3 15.9 %all-to-all-start.1 = ((bf16[8,256,128]{1,2,0:T(8,128)(2,1)}), bf16[8,256,128]{1,2,0:T(8,128)(2,1)S(1)}, u32[]{:S(2)}, u32[]{:S(2)}) async-start(bf16[8,256,128]{1,2,0:T(8,128)(2,1)} %copy.131), calls=%async_computation.1 | async-start | bytes 1048576 | tf_op jit(solution)/shard_map/all_to_all | solution.py:457
  106.5 67.1 %collective-permute-start.10 = (bf16[256,1024]{1,0:T(8,128)(2,1)}, bf16[256,1024]{1,0:T(8,128)(2,1)S(1)}, u32[]{:S(2)}, u32[]{:S(2)}) collective-permute-start(bf16[256,1024]{1,0:T(8,128)(2,1)} %collective-permute-done.9), channel_id=1, source_target_pairs={{0,1},{1,0},{2,3},{3,2},{4,5},{5,4},{6,7},{7,6},{8,9},{9,8},{10,11... | collective-permute-start | bytes 1572872 | tf_op jit(solution)/shard_map/ppermute | solution.py:74
  116.8 42.4 %collective-permute-start.1 = (bf16[256,1024]{1,0:T(8,128)(2,1)S(1)}, bf16[256,1024]{1,0:T(8,128)(2,1)S(1)}, u32[]{:S(2)}, u32[]{:S(2)}) collective-permute-start(bf16[256,1024]{1,0:T(8,128)(2,1)S(1)} %multiply_convert_fusion.3), channel_id=1, source_target_pairs={{0,2},{1,3},{2,0},{3,1},{4,6},{5,7},{6,4},{7,5},{8,10},{9,11},{10,... | collective-permute-start | bytes 1572872 | tf_op jit(solution)/shard_map/ppermute | solution.py:74
  126.9 34.8 %collective-permute-start = (bf16[256,1024]{1,0:T(8,128)(2,1)S(1)}, bf16[256,1024]{1,0:T(8,128)(2,1)S(1)}, u32[]{:S(2)}, u32[]{:S(2)}) collective-permute-start(bf16[256,1024]{1,0:T(8,128)(2,1)S(1)} %multiply_convert_fusion.3), channel_id=1, source_target_pairs={{0,1},{1,0},{2,3},{3,2},{4,5},{5,4},{6,7},{7,6},{8,9},{9,8},{10,11... | collective-permute-start | bytes 1572872 | tf_op jit(solution)/shard_map/ppermute | solution.py:74
  159.2 2.5 collective-permute-start.2
  159.2 14.5 %slice-start = ((s8[4718592]{0:T(1024)(128)(4,1)}), s8[4194304]{0:T(1024)(128)(4,1)S(1)}, s32[]{:S(2)}) async-start(s8[4718592]{0:T(1024)(128)(4,1)} %bitcast.300), calls=%async_computation.6 | async-start | bytes 8388608
  161.7 11.9 %copy-start.49 = (bf16[256,1024]{1,0:T(8,128)(2,1)}, bf16[256,1024]{1,0:T(8,128)(2,1)S(1)}, u32[]{:S(2)}) copy-start(bf16[256,1024]{1,0:T(8,128)(2,1)S(1)} %collective-permute-done) | copy-start | bytes 1572868
  161.7 11.9 %copy-start.51 = (bf16[256,1024]{1,0:T(8,128)(2,1)}, bf16[256,1024]{1,0:T(8,128)(2,1)S(1)}, u32[]{:S(2)}) copy-start(bf16[256,1024]{1,0:T(8,128)(2,1)S(1)} %collective-permute-done.2) | copy-start | bytes 1572868
  161.7 11.9 %slice-start.1 = ((s8[4718592]{0:T(1024)(128)(4,1)}), s8[524288]{0:T(1024)(128)(4,1)S(1)}, s32[]{:S(2)}) async-start(s8[4718592]{0:T(1024)(128)(4,1)} %bitcast.300), calls=%async_computation.7 | async-start | bytes 1048576
  185.5 27.9 %collective-permute-start.6 = (bf16[512,1024]{1,0:T(8,128)(2,1)S(1)}, bf16[512,1024]{1,0:T(8,128)(2,1)S(1)}, u32[]{:S(2)}, u32[]{:S(2)}) collective-permute-start(bf16[512,1024]{1,0:T(8,128)(2,1)S(1)} %pad_maximum_fusion.14), channel_id=1, source_target_pairs={{0,1},{1,0},{2,3},{3,2},{4,5},{5,4},{6,7},{7,6},{8,9},{9,8},{10,11... | collective-permute-start | bytes 3145736 | tf_op jit(solution)/shard_map/ppermute | solution.py:74
  194.3 18.3 %collective-permute-start.11 = (bf16[512,1024]{1,0:T(8,128)(2,1)S(1)}, bf16[512,1024]{1,0:T(8,128)(2,1)S(1)}, u32[]{:S(2)}, u32[]{:S(2)}) collective-permute-start(bf16[512,1024]{1,0:T(8,128)(2,1)S(1)} %pad_maximum_fusion.15), channel_id=1, source_target_pairs={{0,1},{1,0},{2,3},{3,2},{4,5},{5,4},{6,7},{7,6},{8,9},{9,8},{10,11... | collective-permute-start | bytes 3145736 | tf_op jit(solution)/shard_map/ppermute | solution.py:74
  199.3 28.9 %collective-permute-start.38 = (bf16[4,144,1024]{2,1,0:T(8,128)(2,1)S(1)}, bf16[4,144,1024]{2,1,0:T(8,128)(2,1)S(1)}, u32[]{:S(2)}, u32[]{:S(2)}) collective-permute-start(bf16[4,144,1024]{2,1,0:T(8,128)(2,1)S(1)} %dynamic-slice_bitcast_fusion.1), channel_id=1, source_target_pairs={{0,4},{4,0},{8,12},{12,8},{16,20},{20,16},{24,28},{28,24},{1,5},{5... | collective-permute-start | bytes 3538952 | tf_op jit(solution)/shard_map/ppermute | solution.py:74
  211.5 77.5 %collective-permute-start.29 = (bf16[4,4,32,2304]{3,2,1,0:T(8,128)(2,1)}, bf16[4,4,32,2304]{3,2,1,0:T(8,128)(2,1)}, u32[]{:S(2)}, u32[]{:S(2)}) collective-permute-start(bf16[4,4,32,2304]{3,2,1,0:T(8,128)(2,1)} %dynamic-slice_bitcast_fusion), channel_id=1, source_target_pairs={{0,4},{4,0},{8,12},{12,8},{16,20},{20,16},{24,28},{28,24},{1,5},{5... | collective-permute-start | bytes 7077896 | tf_op jit(solution)/shard_map/ppermute | solution.py:74
  212.8 18.3 %collective-permute-start.12 = (bf16[256,1024]{1,0:T(8,128)(2,1)S(1)}, bf16[256,1024]{1,0:T(8,128)(2,1)S(1)}, u32[]{:S(2)}, u32[]{:S(2)}) collective-permute-start(bf16[256,1024]{1,0:T(8,128)(2,1)S(1)} %add_convert_fusion.1), channel_id=1, source_target_pairs={{0,2},{1,3},{2,0},{3,1},{4,6},{5,7},{6,4},{7,5},{8,10},{9,11},{10,... | collective-permute-start | bytes 1572872 | tf_op jit(solution)/shard_map/ppermute | solution.py:74
  213.6 24.1 %collective-permute-start.7 = (bf16[256,1024]{1,0:T(8,128)(2,1)S(1)}, bf16[256,1024]{1,0:T(8,128)(2,1)S(1)}, u32[]{:S(2)}, u32[]{:S(2)}) collective-permute-start(bf16[256,1024]{1,0:T(8,128)(2,1)S(1)} %add_convert_fusion.2), channel_id=1, source_target_pairs={{0,2},{1,3},{2,0},{3,1},{4,6},{5,7},{6,4},{7,5},{8,10},{9,11},{10,... | collective-permute-start | bytes 1572872 | tf_op jit(solution)/shard_map/ppermute | solution.py:74
  229.6 13.8 %collective-permute-start.39 = (bf16[2,144,1024]{2,1,0:T(8,128)(2,1)}, bf16[2,144,1024]{2,1,0:T(8,128)(2,1)}, u32[]{:S(2)}, u32[]{:S(2)}) collective-permute-start(bf16[2,144,1024]{2,1,0:T(8,128)(2,1)} %dynamic-slice_bitcast_fusion.5), channel_id=1, source_target_pairs={{0,8},{4,12},{8,0},{12,4},{16,24},{20,28},{24,16},{28,20},{1,9},{5... | collective-permute-start | bytes 1769480 | tf_op jit(solution)/shard_map/ppermute | solution.py:74
  239.2 26.1 %copy-start.3 = (f32[256,1024]{1,0:T(8,128)}, f32[256,1024]{1,0:T(8,128)S(1)}, u32[]{:S(2)}) copy-start(f32[256,1024]{1,0:T(8,128)S(1)} %get-tuple-element.117) | copy-start | bytes 3145732
  242.4 20.2 %collective-permute-start.21 = (bf16[512,1024]{1,0:T(8,128)(2,1)}, bf16[512,1024]{1,0:T(8,128)(2,1)}, u32[]{:S(2)}, u32[]{:S(2)}) collective-permute-start(bf16[512,1024]{1,0:T(8,128)(2,1)} %pad_maximum_fusion.18), channel_id=1, source_target_pairs={{0,1},{1,0},{2,3},{3,2},{4,5},{5,4},{6,7},{7,6},{8,9},{9,8},{10,11... | collective-permute-start | bytes 3145736 | tf_op jit(solution)/shard_map/ppermute | solution.py:74
  245.7 15.6 %collective-permute-start.40 = (bf16[1,144,1024]{2,1,0:T(8,128)(2,1)S(1)}, bf16[1,144,1024]{2,1,0:T(8,128)(2,1)S(1)}, u32[]{:S(2)}, u32[]{:S(2)}) collective-permute-start(bf16[1,144,1024]{2,1,0:T(8,128)(2,1)S(1)} %constant_dynamic-slice_fusion), channel_id=1, source_target_pairs={{0,16},{4,20},{8,24},{12,28},{16,0},{20,4},{24,8},{28,12},{1,17},{... | collective-permute-start | bytes 884744 | tf_op jit(solution)/shard_map/ppermute | solution.py:74
  248.2 17.1 %copy-start.7 = (bf16[1024,1024]{1,0:T(8,128)(2,1)S(1)}, bf16[1024,1024]{1,0:T(8,128)(2,1)}, u32[]{:S(2)}) copy-start(bf16[1024,1024]{1,0:T(8,128)(2,1)} %all-gather.6.cloned.1.call-done) | copy-start | bytes 6291460
  262.5 22.9 %collective-permute-start.41 = (bf16[1,144,1024]{2,1,0:T(8,128)(2,1)S(1)}, bf16[1,144,1024]{2,1,0:T(8,128)(2,1)}, u32[]{:S(2)}, u32[]{:S(2)}) collective-permute-start(bf16[1,144,1024]{2,1,0:T(8,128)(2,1)S(1)} %add_convert_fusion.3), channel_id=1, source_target_pairs={{0,16},{4,20},{8,24},{12,28},{16,0},{20,4},{24,8},{28,12},{1,17},{... | collective-permute-start | bytes 884744 | tf_op jit(solution)/shard_map/ppermute | solution.py:74
  264.8 22.6 %collective-permute-start.22 = (bf16[256,1024]{1,0:T(8,128)(2,1)}, bf16[256,1024]{1,0:T(8,128)(2,1)}, u32[]{:S(2)}, u32[]{:S(2)}) collective-permute-start(bf16[256,1024]{1,0:T(8,128)(2,1)} %fusion.24), channel_id=1, source_target_pairs={{0,2},{1,3},{2,0},{3,1},{4,6},{5,7},{6,4},{7,5},{8,10},{9,11},{10,... | collective-permute-start | bytes 1572872 | tf_op jit(solution)/shard_map/ppermute | solution.py:74
  267.0 32.4 %all-to-all-start.2 = ((bf16[8,256,128]{2,1,0:T(8,128)(2,1)}), bf16[8,256,128]{2,1,0:T(8,128)(2,1)S(1)}, u32[]{:S(2)}, u32[]{:S(2)}) async-start(bf16[8,256,128]{2,1,0:T(8,128)(2,1)} %bitcast.226), calls=%async_computation.2 | async-start | bytes 1048576 | tf_op jit(solution)/shard_map/all_to_all | solution.py:457
  287.3 32.0 %collective-permute-start.42 = (bf16[2,144,1024]{2,1,0:T(8,128)(2,1)}, bf16[2,144,1024]{2,1,0:T(8,128)(2,1)}, u32[]{:S(2)}, u32[]{:S(2)}) collective-permute-start(bf16[2,144,1024]{2,1,0:T(8,128)(2,1)} %pad_maximum_fusion.19), channel_id=1, source_target_pairs={{0,8},{4,12},{8,0},{12,4},{16,24},{20,28},{24,16},{28,20},{1,9},{5... | collective-permute-start | bytes 1769480 | tf_op jit(solution)/shard_map/ppermute | solution.py:74
  289.0 6.4 %collective-permute-start.23 = (bf16[4,32,1024]{2,1,0:T(8,128)(2,1)S(1)}, bf16[4,32,1024]{2,1,0:T(8,128)(2,1)S(1)}, u32[]{:S(2)}, u32[]{:S(2)}) collective-permute-start(bf16[4,32,1024]{2,1,0:T(8,128)(2,1)S(1)} %dynamic-slice_bitcast_fusion.9), channel_id=1, source_target_pairs={{0,4},{4,0},{8,12},{12,8},{16,20},{20,16},{24,28},{28,24},{1,5},{5... | collective-permute-start | bytes 786440 | tf_op jit(solution)/shard_map/ppermute | solution.py:74
  296.2 19.1 %collective-permute-start.24 = (bf16[2,32,1024]{2,1,0:T(8,128)(2,1)}, bf16[2,32,1024]{2,1,0:T(8,128)(2,1)}, u32[]{:S(2)}, u32[]{:S(2)}) collective-permute-start(bf16[2,32,1024]{2,1,0:T(8,128)(2,1)} %dynamic-slice_bitcast_fusion.14), channel_id=1, source_target_pairs={{0,8},{4,12},{8,0},{12,4},{16,24},{20,28},{24,16},{28,20},{1,9},{5... | collective-permute-start | bytes 393224 | tf_op jit(solution)/shard_map/ppermute | solution.py:74
  299.4 52.0 %collective-permute-start.30 = (bf16[4,2,32,2304]{3,2,0,1:T(8,128)(2,1)}, bf16[4,2,32,2304]{3,2,0,1:T(8,128)(2,1)}, u32[]{:S(2)}, u32[]{:S(2)}) collective-permute-start(bf16[4,2,32,2304]{3,2,0,1:T(8,128)(2,1)} %dynamic-slice_bitcast_fusion.2), channel_id=1, source_target_pairs={{0,8},{4,12},{8,0},{12,4},{16,24},{20,28},{24,16},{28,20},{1,9},{5... | collective-permute-start | bytes 3538952 | tf_op jit(solution)/shard_map/ppermute | solution.py:74
  310.9 79.7 %all-to-all-start.3 = ((bf16[8,256,256]{1,2,0:T(8,128)(2,1)}), bf16[8,256,256]{1,2,0:T(8,128)(2,1)}, u32[]{:S(2)}, u32[]{:S(2)}) async-start(bf16[8,256,256]{1,2,0:T(8,128)(2,1)} %copy.139), calls=%async_computation.3 | async-start | bytes 2097152 | tf_op jit(solution)/shard_map/all_to_all | solution.py:457
  316.4 35.0 %copy-start.6 = (bf16[4,4,32,2304]{3,2,0,1:T(8,128)(2,1)S(1)}, bf16[4,4,32,2304]{3,2,0,1:T(8,128)(2,1)}, u32[]{:S(2)}) copy-start(bf16[4,4,32,2304]{3,2,0,1:T(8,128)(2,1)} %copy-done.5) | copy-start | bytes 7077892
  316.4 25.7 %collective-permute-start.25 = (bf16[1,32,1024]{2,1,0:T(8,128)(2,1)S(1)}, bf16[1,32,1024]{2,1,0:T(8,128)(2,1)S(1)}, u32[]{:S(2)}, u32[]{:S(2)}) collective-permute-start(bf16[1,32,1024]{2,1,0:T(8,128)(2,1)S(1)} %constant_dynamic-slice_fusion.2), channel_id=1, source_target_pairs={{0,16},{4,20},{8,24},{12,28},{16,0},{20,4},{24,8},{28,12},{1,17},{... | collective-permute-start | bytes 196616 | tf_op jit(solution)/shard_map/ppermute | solution.py:74
  342.1 5.7 collective-permute-start.26
  345.7 39.5 %collective-permute-start.43 = (bf16[4,144,1024]{2,1,0:T(8,128)(2,1)S(1)}, bf16[4,144,1024]{2,1,0:T(8,128)(2,1)S(1)}, u32[]{:S(2)}, u32[]{:S(2)}) collective-permute-start(bf16[4,144,1024]{2,1,0:T(8,128)(2,1)S(1)} %pad_maximum_fusion.12), channel_id=1, source_target_pairs={{0,4},{4,0},{8,12},{12,8},{16,20},{20,16},{24,28},{28,24},{1,5},{5... | collective-permute-start | bytes 3538952 | tf_op jit(solution)/shard_map/ppermute | solution.py:74
  347.9 6.5 %collective-permute-start.27 = (bf16[2,32,1024]{2,1,0:T(8,128)(2,1)S(1)}, bf16[2,32,1024]{2,1,0:T(8,128)(2,1)S(1)}, u32[]{:S(2)}, u32[]{:S(2)}) collective-permute-start(bf16[2,32,1024]{2,1,0:T(8,128)(2,1)S(1)} %pad_maximum_fusion.29), channel_id=1, source_target_pairs={{0,8},{4,12},{8,0},{12,4},{16,24},{20,28},{24,16},{28,20},{1,9},{5... | collective-permute-start | bytes 393224 | tf_op jit(solution)/shard_map/ppermute | solution.py:74
  354.4 20.3 %collective-permute-start.28 = (bf16[4,32,1024]{2,1,0:T(8,128)(2,1)S(1)}, bf16[4,32,1024]{2,1,0:T(8,128)(2,1)S(1)}, u32[]{:S(2)}, u32[]{:S(2)}) collective-permute-start(bf16[4,32,1024]{2,1,0:T(8,128)(2,1)S(1)} %pad_maximum_fusion.28), channel_id=1, source_target_pairs={{0,4},{4,0},{8,12},{12,8},{16,20},{20,16},{24,28},{28,24},{1,5},{5... | collective-permute-start | bytes 786440 | tf_op jit(solution)/shard_map/ppermute | solution.py:74
  356.9 24.7 %collective-permute-start.31 = (bf16[4,1,32,2304]{3,2,0,1:T(8,128)(2,1)S(1)}, bf16[4,1,32,2304]{3,2,0,1:T(8,128)(2,1)S(1)}, u32[]{:S(2)}, u32[]{:S(2)}) collective-permute-start(bf16[4,1,32,2304]{3,2,0,1:T(8,128)(2,1)S(1)} %constant_dynamic-slice_fusion.1), channel_id=1, source_target_pairs={{0,16},{4,20},{8,24},{12,28},{16,0},{20,4},{24,8},{28,12},{1,17},{... | collective-permute-start | bytes 1769480 | tf_op jit(solution)/shard_map/ppermute | solution.py:74
  383.3 2.2 collective-permute-start.32
  383.3 6.6 %collective-permute-start.33 = (bf16[32,2304]{1,0:T(8,128)(2,1)S(1)}, bf16[32,2304]{1,0:T(8,128)(2,1)S(1)}, u32[]{:S(2)}, u32[]{:S(2)}) collective-permute-start(bf16[32,2304]{1,0:T(8,128)(2,1)S(1)} %get-tuple-element.128), channel_id=1, source_target_pairs={{0,2},{1,3},{2,0},{3,1},{4,6},{5,7},{6,4},{7,5},{8,10},{9,11},{10,... | collective-permute-start | bytes 442376 | tf_op jit(solution)/shard_map/ppermute | solution.py:74
  383.3 14.2 %collective-permute-start.34 = (bf16[32,2304]{1,0:T(8,128)(2,1)S(1)}, bf16[32,2304]{1,0:T(8,128)(2,1)}, u32[]{:S(2)}, u32[]{:S(2)}) collective-permute-start(bf16[32,2304]{1,0:T(8,128)(2,1)S(1)} %get-tuple-element.127), channel_id=1, source_target_pairs={{0,3},{1,2},{2,1},{3,0},{4,7},{5,6},{6,5},{7,4},{8,11},{9,10},{10,... | collective-permute-start | bytes 442376 | tf_op jit(solution)/shard_map/ppermute | solution.py:74
  397.0 32.4 %copy-start = (bf16[1024,2048]{1,0:T(8,128)(2,1)}, bf16[1024,2048]{1,0:T(8,128)(2,1)S(1)}, u32[]{:S(2)}) copy-start(bf16[1024,2048]{1,0:T(8,128)(2,1)S(1)} %convolution_convert_fusion.2) | copy-start | bytes 12582916
  397.4 32.0 %collective-permute-start.13 = (bf16[512,2048]{1,0:T(8,128)(2,1)S(1)}, bf16[512,2048]{1,0:T(8,128)(2,1)S(1)}, u32[]{:S(2)}, u32[]{:S(2)}) collective-permute-start(bf16[512,2048]{1,0:T(8,128)(2,1)S(1)} %pad_maximum_fusion.8), channel_id=1, source_target_pairs={{0,1},{1,0},{2,3},{3,2},{4,5},{5,4},{6,7},{7,6},{8,9},{9,8},{10,11... | collective-permute-start | bytes 6291464 | tf_op jit(solution)/shard_map/ppermute | solution.py:74
  399.3 29.0 %collective-permute-start.35 = (bf16[1,4,32,2304]{3,2,0,1:T(8,128)(2,1)}, bf16[1,4,32,2304]{3,2,0,1:T(8,128)(2,1)S(1)}, u32[]{:S(2)}, u32[]{:S(2)}) collective-permute-start(bf16[1,4,32,2304]{3,2,0,1:T(8,128)(2,1)} %bitcast_dynamic-update-slice_fusion.4), channel_id=1, source_target_pairs={{0,16},{4,20},{8,24},{12,28},{16,0},{20,4},{24,8},{28,12},{1,17},{... | collective-permute-start | bytes 1769480 | tf_op jit(solution)/shard_map/ppermute | solution.py:74
  429.9 56.6 %collective-permute-start.14 = (bf16[256,2048]{1,0:T(8,128)(2,1)S(1)}, bf16[256,2048]{1,0:T(8,128)(2,1)}, u32[]{:S(2)}, u32[]{:S(2)}) collective-permute-start(bf16[256,2048]{1,0:T(8,128)(2,1)S(1)} %fusion.8), channel_id=1, source_target_pairs={{0,2},{1,3},{2,0},{3,1},{4,6},{5,7},{6,4},{7,5},{8,10},{9,11},{10,... | collective-permute-start | bytes 3145736 | tf_op jit(solution)/shard_map/ppermute | solution.py:74
  431.3 55.2 %copy-start.35 = (f32[2,128]{1,0:T(2,128)S(1)}, f32[2,128]{1,0:T(2,128)}, u32[]{:S(2)}) copy-start(f32[2,128]{1,0:T(2,128)} %copy-done.34) | copy-start | bytes 3076
  431.3 60.0 %collective-permute-start.36 = (bf16[2,4,32,2304]{3,2,0,1:T(8,128)(2,1)}, bf16[2,4,32,2304]{3,2,0,1:T(8,128)(2,1)}, u32[]{:S(2)}, u32[]{:S(2)}) collective-permute-start(bf16[2,4,32,2304]{3,2,0,1:T(8,128)(2,1)} %pad_maximum_fusion.11), channel_id=1, source_target_pairs={{0,8},{4,12},{8,0},{12,4},{16,24},{20,28},{24,16},{28,20},{1,9},{5... | collective-permute-start | bytes 3538952 | tf_op jit(solution)/shard_map/ppermute | solution.py:74
  489.0 15.2 %collective-permute-start.15 = (bf16[4,32,2048]{2,1,0:T(8,128)(2,1)S(1)}, bf16[4,32,2048]{2,1,0:T(8,128)(2,1)S(1)}, u32[]{:S(2)}, u32[]{:S(2)}) collective-permute-start(bf16[4,32,2048]{2,1,0:T(8,128)(2,1)S(1)} %dynamic-slice_bitcast_fusion.8), channel_id=1, source_target_pairs={{0,4},{4,0},{8,12},{12,8},{16,20},{20,16},{24,28},{28,24},{1,5},{5... | collective-permute-start | bytes 1572872 | tf_op jit(solution)/shard_map/ppermute | solution.py:74
  492.8 11.7 %copy-start.4 = (f32[256,1024]{1,0:T(8,128)S(1)}, f32[256,1024]{1,0:T(8,128)}, u32[]{:S(2)}) copy-start(f32[256,1024]{1,0:T(8,128)} %copy-done.3) | copy-start | bytes 3145732
  493.0 60.0 %collective-permute-start.37 = (bf16[4,4,32,2304]{3,2,0,1:T(8,128)(2,1)S(1)}, bf16[4,4,32,2304]{3,2,0,1:T(8,128)(2,1)S(1)}, u32[]{:S(2)}, u32[]{:S(2)}) collective-permute-start(bf16[4,4,32,2304]{3,2,0,1:T(8,128)(2,1)S(1)} %pad_maximum_fusion.4), channel_id=1, source_target_pairs={{0,4},{4,0},{8,12},{12,8},{16,20},{20,16},{24,28},{28,24},{1,5},{5... | collective-permute-start | bytes 7077896 | tf_op jit(solution)/shard_map/ppermute | solution.py:74
  504.3 7.0 %collective-permute-start.16 = (bf16[2,32,2048]{2,1,0:T(8,128)(2,1)S(1)}, bf16[2,32,2048]{2,1,0:T(8,128)(2,1)S(1)}, u32[]{:S(2)}, u32[]{:S(2)}) collective-permute-start(bf16[2,32,2048]{2,1,0:T(8,128)(2,1)S(1)} %dynamic-slice_bitcast_fusion.10), channel_id=1, source_target_pairs={{0,8},{4,12},{8,0},{12,4},{16,24},{20,28},{24,16},{28,20},{1,9},{5... | collective-permute-start | bytes 786440 | tf_op jit(solution)/shard_map/ppermute | solution.py:74
  511.4 9.3 %collective-permute-start.17 = (bf16[1,32,2048]{2,1,0:T(8,128)(2,1)S(1)}, bf16[1,32,2048]{2,1,0:T(8,128)(2,1)S(1)}, u32[]{:S(2)}, u32[]{:S(2)}) collective-permute-start(bf16[1,32,2048]{2,1,0:T(8,128)(2,1)S(1)} %constant_dynamic-slice_fusion.3), channel_id=1, source_target_pairs={{0,16},{4,20},{8,24},{12,28},{16,0},{20,4},{24,8},{28,12},{1,17},{... | collective-permute-start | bytes 393224 | tf_op jit(solution)/shard_map/ppermute | solution.py:74
  520.8 32.5 %collective-permute-start.18 = (bf16[1,32,2048]{2,1,0:T(8,128)(2,1)S(1)}, bf16[1,32,2048]{2,1,0:T(8,128)(2,1)S(1)}, u32[]{:S(2)}, u32[]{:S(2)}) collective-permute-start(bf16[1,32,2048]{2,1,0:T(8,128)(2,1)S(1)} %add_convert_fusion.5), channel_id=1, source_target_pairs={{0,16},{4,20},{8,24},{12,28},{16,0},{20,4},{24,8},{28,12},{1,17},{... | collective-permute-start | bytes 393224 | tf_op jit(solution)/shard_map/ppermute | solution.py:74
  553.4 6.6 %collective-permute-start.19 = (bf16[2,32,2048]{2,1,0:T(8,128)(2,1)S(1)}, bf16[2,32,2048]{2,1,0:T(8,128)(2,1)S(1)}, u32[]{:S(2)}, u32[]{:S(2)}) collective-permute-start(bf16[2,32,2048]{2,1,0:T(8,128)(2,1)S(1)} %pad_maximum_fusion.27), channel_id=1, source_target_pairs={{0,8},{4,12},{8,0},{12,4},{16,24},{20,28},{24,16},{28,20},{1,9},{5... | collective-permute-start | bytes 786440 | tf_op jit(solution)/shard_map/ppermute | solution.py:74
  560.1 30.2 %collective-permute-start.20 = (bf16[4,32,2048]{2,1,0:T(8,128)(2,1)S(1)}, bf16[4,32,2048]{2,1,0:T(8,128)(2,1)S(1)}, u32[]{:S(2)}, u32[]{:S(2)}) collective-permute-start(bf16[4,32,2048]{2,1,0:T(8,128)(2,1)S(1)} %pad_maximum_fusion.21), channel_id=1, source_target_pairs={{0,4},{4,0},{8,12},{12,8},{16,20},{20,16},{24,28},{28,24},{1,5},{5... | collective-permute-start | bytes 1572872 | tf_op jit(solution)/shard_map/ppermute | solution.py:74
  (45 other events, 174.7 us)
Sparse Core Ops, SparseCore 0:
  11.8 37.7 all-gather.3
  64.6 27.7 all-gather.5

commit v2 on v1

v2 whole, which is shorter than its diff:
```python
import jax
import jax.numpy as jnp
from jax import lax
from jax.experimental import pallas as pl
from jax.experimental.pallas import tpu as pltpu
from jax.sharding import PartitionSpec as P

HEADS = 16
KV_HEADS = 8
HEAD = 64
GROUP = HEADS // KV_HEADS


epsilon = 1e-05
rope_base = 1000000.0
masked = -1e30
F32 = jnp.float32
BF16 = jnp.bfloat16


def dot_over(left, right, left_dim, right_dim):
    return lax.dot_general(
        left, right, (((left_dim,), (right_dim,)), ((), ())), preferred_element_type=F32
    )


def product(left, right):
    return dot_over(left, right, 1, 0)


def by_transpose(left, right):
    return dot_over(left, right, 1, 1)


def transpose_by(left, right):
    return dot_over(left, right, 0, 0)


PLANE = 8


def trade(values, step):
    size = lax.axis_size("ctx") * lax.axis_size("fsdp")
    return lax.ppermute(values, ("ctx", "fsdp"), [(i, i ^ step) for i in range(size)])


def pick(values, index, axis=0):
    return lax.dynamic_index_in_dim(values, index, axis, keepdims=False)


class Line:
    def __init__(self):
        self.last = None

    def __call__(self, step, *operands):
        if self.last is not None:
            operands = lax.optimization_barrier((*operands, self.last))[:-1]
        result = step(*operands)
        self.last = jax.tree.leaves(result)[0]
        return result

    def wait(self, *values):
        *values, self.last = lax.optimization_barrier((*values, self.last))
        return values


def add_low(first, second):
    return (first.astype(F32) + second.astype(F32)).astype(BF16)


def halves(values):
    half = values.shape[0] // 2
    return values[:half], values[half:]


def cut_far(over_x, over_y):
    return halves(over_x)[0], halves(over_y)[1]


def gather_plane(values, over_x, over_y, corner):
    far = [values, over_x, over_y, *corner]
    return [trade(block, 1) for block in far] + far


def plane_groups():
    size = lax.axis_size("ctx") * lax.axis_size("fsdp")
    return [list(range(start, start + PLANE)) for start in range(0, size, PLANE)]


def cut_plane(send_got, keep):
    pair = add_low(keep, send_got).reshape(4, -1, keep.shape[1])
    half = pair.shape[1] // 2
    low, high = pair[:, :half], pair[:, half:]
    return jnp.stack([low[1], low[3]]), jnp.stack([high[2], high[3]]), low[::2], high[:2]


def join_plane(low, high, low_got, high_got):
    low_own = low[0].astype(F32) + low_got[0].astype(F32)
    high_own = high[0].astype(F32) + high_got[0].astype(F32)
    return add_low(low[1], low_got[1]), add_low(high[1], high_got[1]), low_own, high_own


def cut_near(part, me_f):
    blocks = [pick(part, me_f ^ k) for k in range(4)]
    return jnp.stack([blocks[1], blocks[3]]), jnp.stack([blocks[0], blocks[2]])


def gather_near(values):
    far = trade(values, 2)
    near = trade(values, 1)
    return [values, near, far, trade(far, 1)]


def sum_everywhere(values):
    step = 1
    while step < lax.axis_size("ctx") * lax.axis_size("fsdp"):
        values = values + trade(values, step)
        step *= 2
    return values


RING = (0, 1, 3, 2)


def ring_step(values):
    following = {RING[i]: RING[(i + 1) % 4] for i in range(4)}
    pairs = []
    for c in range(lax.axis_size("ctx")):
        outer, place, low = c // 8, c // 2 % 4, c % 2
        pairs.append((c, outer * 8 + following[place] * 2 + low))
    return lax.ppermute(values, "ctx", pairs)


def ring_places(place):
    before = {RING[(i + 1) % 4]: RING[i] for i in range(4)}
    table = []
    for start in range(4):
        row = [start]
        for _ in range(3):
            row.append(before[row[-1]])
        table.append(row)
    return jnp.array(table, jnp.int32)[place]


def plane_step(values, moves):
    size = lax.axis_size("ctx") * lax.axis_size("fsdp")
    pairs = []
    for device in range(size):
        place, rest = device // PLANE, device % PLANE
        pairs += [(device, to * PLANE + rest) for start, to in moves if start == place]
    return lax.ppermute(values, ("ctx", "fsdp"), pairs)


def ctx_bits():
    size = lax.axis_size("ctx")
    bits = []
    step = 1
    while step < size:
        bits.append(step)
        step *= 2
    return bits


def ctx_sum(values):
    me = lax.axis_index("ctx")
    near = lax.axis_size("fsdp")
    for step in ctx_bits():
        shape = values.shape
        halves = values.reshape((2, shape[0] // 2) + shape[1:])
        mine = (me // step) % 2
        got = trade(pick(halves, 1 - mine), step * near)
        values = (pick(halves, mine).astype(F32) + got.astype(F32)).astype(BF16)
    for step in reversed(ctx_bits()):
        mine = (me // step) % 2
        got = trade(values, step * near)
        first = jnp.where(mine == 0, values, got)
        second = jnp.where(mine == 0, got, values)
        values = jnp.concatenate([first, second], axis=0)
    return values


def two_heads(block):
    return jnp.concatenate([block[:, :HEAD], block[:, HEAD:]], axis=0)


def side_by_side(stacked):
    rows = stacked.shape[0] // 2
    return jnp.concatenate([stacked[:rows], stacked[rows:]], axis=1)


def allowed_mask(rows, count, first_query, first_key, seq_len):
    query_slot = first_query + lax.broadcasted_iota(jnp.int32, (rows, count), 0) % (rows // GROUP)
    key_slot = first_key + lax.broadcasted_iota(jnp.int32, (rows, count), 1)
    return (key_slot <= query_slot) & (key_slot < seq_len)


def whole_row(q_ref, kv_ref, index, seq_len):
    slots = q_ref.shape[2]
    count = (index + 1) * slots
    query = two_heads(q_ref[index, 0]) * (HEAD**-0.5)
    both = kv_ref[: index + 1, 0].reshape(count, 2 * HEAD)
    key, value = both[:, :HEAD], both[:, HEAD:]
    scores = by_transpose(query, key)
    scores = jnp.where(
        allowed_mask(GROUP * slots, count, index * slots, 0, seq_len), scores, masked
    )
    exponent = jnp.exp(scores - jnp.max(scores, axis=-1, keepdims=True))
    weights = exponent * (1.0 / jnp.sum(exponent, axis=-1, keepdims=True))
    return query, key, value, weights


def forward_small(info_ref, q_ref, kv_ref, *refs):
    out_ref = refs[-1]
    seq_len = info_ref[pl.program_id(0) + 1]
    slots = q_ref.shape[2]
    for index in range(q_ref.shape[0]):

        @pl.when(index * slots < seq_len)
        def _():
            _, _, value, weights = whole_row(q_ref, kv_ref, index, seq_len)
            out_ref[index, 0] = side_by_side(product(weights.astype(BF16), value)).astype(BF16)

        @pl.when(index * slots >= seq_len)
        def _():
            out_ref[index, 0] = jnp.zeros(out_ref.shape[2:], BF16)


def backward_small(info_ref, q_ref, kv_ref, grad_ref, *refs):
    out_ref, key_acc, value_acc = refs[-3:]
    seq_len = info_ref[pl.program_id(0) + 1]
    blocks, _, slots, _ = q_ref.shape
    key_acc[...] = jnp.zeros_like(key_acc)
    value_acc[...] = jnp.zeros_like(value_acc)
    for index in range(blocks):

        @pl.when(index * slots < seq_len)
        def _():
            count = (index + 1) * slots
            query, key, value, weights = whole_row(q_ref, kv_ref, index, seq_len)
            grad = two_heads(grad_ref[index, 0])
            grad_weights = by_transpose(grad, value)
            delta = jnp.sum(weights * grad_weights, axis=-1, keepdims=True)
            grad_scores = (weights * (grad_weights - delta)).astype(BF16)
            out_ref[index, 0, :, : 2 * HEAD] = side_by_side(
                product(grad_scores, key) * (HEAD**-0.5)
            )
            key_acc[:count] += transpose_by(grad_scores, query)
            value_acc[:count] += transpose_by(weights.astype(BF16), grad)

        @pl.when(index * slots >= seq_len)
        def _():
            out_ref[index, 0, :, : 2 * HEAD] = jnp.zeros((slots, 2 * HEAD), F32)

    for index in range(blocks):
        rows = slice(index * slots, (index + 1) * slots)
        out_ref[index, 0, :, 2 * HEAD :] = jnp.concatenate(
            [key_acc[rows], value_acc[rows]], axis=1
        )


def row_stats(query, kv_ref, index, first_query, seq_len):
    slots = kv_ref.shape[2]
    rows = query.shape[0]

    def scores_of(block):
        both = kv_ref[block, 0]
        scores = by_transpose(query, both[:, :HEAD])
        allowed = allowed_mask(rows, slots, first_query, block * slots, seq_len)
        return both, jnp.where(allowed, scores, masked)

    def step(block, state):
        top, total = state
        _, scores = scores_of(block)
        new_top = jnp.maximum(top, jnp.max(scores, axis=-1, keepdims=True))
        grown = jnp.sum(jnp.exp(scores - new_top), axis=-1, keepdims=True)
        return new_top, total * jnp.exp(top - new_top) + grown

    start = (jnp.full((rows, 1), masked, F32), jnp.zeros((rows, 1), F32))
    top, total = lax.fori_loop(0, index + 1, step, start)
    inverse = 1.0 / total

    def weights_of(block):
        both, scores = scores_of(block)
        return both, jnp.exp(scores - top) * inverse

    return weights_of


def forward_large(info_ref, q_ref, kv_ref, out_ref):
    seq_len = info_ref[pl.program_id(0) + 1]
    slots = q_ref.shape[2]
    index = info_ref[0] + pl.program_id(1)
    live = index * slots < seq_len

    @pl.when(live)
    def _():
        query = two_heads(q_ref[0, 0]) * (HEAD**-0.5)
        weights_of = row_stats(query, kv_ref, index, index * slots, seq_len)

        def step(block, total):
            both, weights = weights_of(block)
            return total + product(weights.astype(BF16), both[:, HEAD:])

        total = lax.fori_loop(0, index + 1, step, jnp.zeros((GROUP * slots, HEAD), F32))
        out_ref[0, 0] = side_by_side(total).astype(BF16)

    @pl.when(jnp.logical_not(live))
    def _():
        out_ref[0, 0] = jnp.zeros(out_ref.shape[2:], BF16)


def backward_large(info_ref, q_ref, kv_ref, grad_ref, out_ref, kv_out_ref):
    seq_len = info_ref[pl.program_id(0) + 1]
    slots = q_ref.shape[2]
    index = info_ref[0] + pl.program_id(1)
    live = index * slots < seq_len

    @pl.when(pl.program_id(1) == 0)
    def _():
        kv_out_ref[...] = jnp.zeros_like(kv_out_ref)

    @pl.when(live)
    def _():
        query = two_heads(q_ref[0, 0]) * (HEAD**-0.5)
        grad = two_heads(grad_ref[0, 0])
        weights_of = row_stats(query, kv_ref, index, index * slots, seq_len)

        def delta_step(block, total):
            both, weights = weights_of(block)
            grad_weights = by_transpose(grad, both[:, HEAD:])
            return total + jnp.sum(weights * grad_weights, axis=-1, keepdims=True)

        delta = lax.fori_loop(0, index + 1, delta_step, jnp.zeros((GROUP * slots, 1), F32))

        def step(block, total):
            both, weights = weights_of(block)
            grad_weights = by_transpose(grad, both[:, HEAD:])
            grad_scores = (weights * (grad_weights - delta)).astype(BF16)
            kv_out_ref[block, 0] += jnp.concatenate(
                [transpose_by(grad_scores, query), transpose_by(weights.astype(BF16), grad)], axis=1
            )
            return total + product(grad_scores, both[:, :HEAD])

        total = lax.fori_loop(0, index + 1, step, jnp.zeros((GROUP * slots, HEAD), F32))
        out_ref[0, 0] = side_by_side(total * (HEAD**-0.5))

    @pl.when(jnp.logical_not(live))
    def _():
        out_ref[0, 0] = jnp.zeros(out_ref.shape[2:], F32)


def attention_cost(q_blocks, k_blocks, seqs, slots, products):
    pairs = seqs * GROUP * q_blocks * k_blocks * slots * slots // 2
    return pl.CostEstimate(
        flops=pairs * HEAD * 2 * products,
        transcendentals=pairs,
        bytes_accessed=4 * seqs * slots * 4 * HEAD * (q_blocks + k_blocks),
    )


def attention(info, mixed, shared, grad=None, awaited=()):
    blocks, seqs, slots, _ = mixed.shape
    wide = 2 * HEAD
    small = shared is mixed
    k_blocks = shared.shape[0]
    params = dict(vmem_limit_bytes=48 * 1024 * 1024)
    cost = attention_cost(blocks, k_blocks, seqs, slots, 2 if grad is None else 5)
    if small:
        whole = lambda part: pl.BlockSpec(
            (blocks, 1, slots, wide), lambda seq, info: (0, seq, 0, part)
        )
        if grad is None:
            return pl.pallas_call(
                forward_small,
                out_shape=jax.ShapeDtypeStruct((blocks, seqs, slots, wide), BF16),
                grid_spec=pltpu.PrefetchScalarGridSpec(
                    num_scalar_prefetch=1,
                    grid=(seqs,),
                    in_specs=[whole(0), whole(1)]
                    + [pl.BlockSpec(memory_space=pl.ANY)] * len(awaited),
                    out_specs=whole(0),
                ),
                compiler_params=pltpu.CompilerParams(**params),
                cost_estimate=cost,
            )(info, mixed, mixed, *awaited)
        return pl.pallas_call(
            backward_small,
            out_shape=jax.ShapeDtypeStruct((blocks, seqs, slots, 2 * wide), F32),
            grid_spec=pltpu.PrefetchScalarGridSpec(
                num_scalar_prefetch=1,
                grid=(seqs,),
                in_specs=[whole(0), whole(1), whole(0)]
                + [pl.BlockSpec(memory_space=pl.ANY)] * len(awaited),
                out_specs=pl.BlockSpec(
                    (blocks, 1, slots, 2 * wide), lambda seq, info: (0, seq, 0, 0)
                ),
                scratch_shapes=[pltpu.VMEM((blocks * slots, HEAD), F32)] * 2,
            ),
            compiler_params=pltpu.CompilerParams(**params),
            cost_estimate=cost,
        )(info, mixed, mixed, grad, *awaited)
    one = pl.BlockSpec((1, 1, slots, wide), lambda seq, block, info: (block, seq, 0, 0))
    every = pl.BlockSpec((k_blocks, 1, slots, wide), lambda seq, block, info: (0, seq, 0, 0))
    out = jax.ShapeDtypeStruct((blocks, seqs, slots, wide), BF16)
    if grad is None:
        return pl.pallas_call(
            forward_large,
            out_shape=out,
            grid_spec=pltpu.PrefetchScalarGridSpec(
                num_scalar_prefetch=1, grid=(seqs, blocks), in_specs=[one, every], out_specs=one
            ),
            compiler_params=pltpu.CompilerParams(**params),
            cost_estimate=cost,
        )(info, mixed, shared)
    return pl.pallas_call(
        backward_large,
        out_shape=(
            jax.ShapeDtypeStruct((blocks, seqs, slots, wide), F32),
            jax.ShapeDtypeStruct((k_blocks, seqs, slots, wide), F32),
        ),
        grid_spec=pltpu.PrefetchScalarGridSpec(
            num_scalar_prefetch=1,
            grid=(seqs, blocks),
            in_specs=[one, every, one],
            out_specs=(one, every),
        ),
        compiler_params=pltpu.CompilerParams(**params),
        cost_estimate=cost,
    )(info, mixed, shared, grad)


POSITION_ROWS = 16
POSITION_BASE = 256


def lane_of(shape):
    return lax.broadcasted_iota(jnp.int32, shape, 1)


def head_mean(values):
    lanes = values.shape[1]
    same = (
        lax.broadcasted_iota(jnp.int32, (lanes, lanes), 0) // HEAD
        == lax.broadcasted_iota(jnp.int32, (lanes, lanes), 1) // HEAD
    )
    ones = jnp.where(same, 1.0, 0.0).astype(BF16)
    high = values.astype(BF16)
    rest = values - high.astype(F32)
    middle = rest.astype(BF16)
    low = (rest - middle.astype(F32)).astype(BF16)
    return (product(high, ones) + product(middle, ones) + product(low, ones)) * (1.0 / HEAD)


def turn(values):
    lanes = values.shape[1]
    first = lane_of(values.shape) % HEAD < HEAD // 2
    return jnp.where(
        first,
        -pltpu.roll(values, lanes - HEAD // 2, 1),
        pltpu.roll(values, HEAD // 2, 1),
    )


def project_kernel(info_ref, near_ref, far_ref, weight_ref, gain_ref, head_gain_ref, freq_ref, *rest):
    normed_ref, projected_ref, mixed_ref, cosine_ref, sine_ref = rest[-5:]
    my_row, my_place = info_ref[0], info_ref[1]
    depth = weight_ref.shape[1]
    rows = normed_ref.shape[1]
    wide = 2 * HEAD
    for which, ref in enumerate((near_ref, far_ref)):
        place = my_place if which == 0 else 1 - my_place
        values = ref[:rows].astype(F32)
        scale = lax.rsqrt(jnp.mean(values * values, axis=-1, keepdims=True) + epsilon)
        normed = (values * scale * gain_ref[...]).astype(BF16)
        normed_ref[place] = normed
        total = jnp.zeros((rows, weight_ref.shape[2]), F32)
        for block in range(weight_ref.shape[0]):
            weight = weight_ref[block ^ my_row]
            total = total + product(normed[:, block * depth : (block + 1) * depth], weight)
        projected_ref[place] = total
        digits = ref[rows : rows + POSITION_ROWS, :rows].astype(F32)
        position = digits[0:1] * POSITION_BASE + digits[1:2]
        angle = jnp.broadcast_to(position, (wide, rows)).T * freq_ref[...]
        cosine, sine = jnp.cos(angle), jnp.sin(angle)
        cosine_ref[place] = cosine
        sine_ref[place] = sine
        for part in range(2):
            lanes = slice(part * wide, (part + 1) * wide)
            piece = total[:, lanes]
            scaled = piece * lax.rsqrt(head_mean(piece * piece) + epsilon) * head_gain_ref[:, lanes]
            turned = scaled * cosine + turn(scaled) * sine
            if part == 1:
                turned = jnp.where(lane_of(turned.shape) < HEAD, turned, piece)
            mixed_ref[place, :, lanes] = turned.astype(BF16)


def project(info, near, far, weight, gain, head_gain, frequency, blocks, earlier):
    rows, width = near.shape
    rows -= POSITION_ROWS
    mix = weight.shape[2]
    wide = 2 * HEAD
    whole = lambda *shape: pl.BlockSpec(shape, lambda step, info: (0,) * len(shape))
    pair = lambda last: pl.BlockSpec((2, rows, last), lambda step, info: (info[2], 0, 0))
    outs = ((width, BF16), (mix, F32), (mix, BF16), (wide, F32), (wide, F32))
    in_specs = [
        whole(*near.shape),
        whole(*near.shape),
        whole(*weight.shape),
        whole(1, width),
        whole(1, mix),
        whole(1, wide),
    ]
    aliases = {}
    operands = [near, far, weight, gain, head_gain, frequency]
    if earlier is not None:
        aliases = {1 + len(operands) + i: i for i in range(len(outs))}
        in_specs += [pl.BlockSpec(memory_space=pl.ANY)] * len(outs)
        operands += list(earlier)
    return pl.pallas_call(
        project_kernel,
        out_shape=tuple(jax.ShapeDtypeStruct((blocks, rows, last), kind) for last, kind in outs),
        grid_spec=pltpu.PrefetchScalarGridSpec(
            num_scalar_prefetch=1,
            grid=(1,),
            in_specs=in_specs,
            out_specs=tuple(pair(last) for last, _ in outs),
        ),
        input_output_aliases=aliases,
        compiler_params=pltpu.CompilerParams(vmem_limit_bytes=32 * 1024 * 1024),
        cost_estimate=pl.CostEstimate(
            flops=4 * rows * width * mix, transcendentals=0, bytes_accessed=8 * rows * width
        ),
    )(info, *operands)


def unproject_kernel(
    grad_ref, projected_ref, head_gain_ref, cosine_ref, sine_ref, *refs
):
    out_ref, gain_ref = refs[-2:]
    wide = 2 * HEAD

    @pl.when(pl.program_id(0) == 0)
    def _():
        gain_ref[...] = jnp.zeros_like(gain_ref)

    cosine, sine = cosine_ref[0], sine_ref[0]
    for part in range(2):
        lanes = slice(part * wide, (part + 1) * wide)
        grad = grad_ref[0, :, lanes]
        piece = projected_ref[0, :, lanes]
        back = grad * cosine - turn(grad) * sine
        scale = lax.rsqrt(head_mean(piece * piece) + epsilon)
        hat = piece * scale
        gain_ref[:, lanes] += jnp.sum(back * hat, axis=0, keepdims=True)
        back = back * head_gain_ref[:, lanes]
        back = scale * (back - hat * head_mean(back * hat))
        if part == 1:
            back = jnp.where(lane_of(back.shape) < HEAD, back, grad)
        out_ref[0, :, lanes] = back.astype(BF16)


def unproject(grad, projected, head_gain, cosine, sine, awaited=()):
    blocks, rows, mix = grad.shape
    one = lambda last: pl.BlockSpec((1, rows, last), lambda step: (step, 0, 0))
    flat = pl.BlockSpec((1, mix), lambda step: (0, 0))
    return pl.pallas_call(
        unproject_kernel,
        out_shape=(
            jax.ShapeDtypeStruct((blocks, rows, mix), BF16),
            jax.ShapeDtypeStruct((1, mix), F32),
        ),
        grid=(blocks,),
        in_specs=[one(mix), one(mix), flat, one(cosine.shape[2]), one(cosine.shape[2])]
        + [pl.BlockSpec(memory_space=pl.ANY)] * len(awaited),
        out_specs=(one(mix), flat),
        compiler_params=pltpu.CompilerParams(vmem_limit_bytes=32 * 1024 * 1024),
        cost_estimate=pl.CostEstimate(
            flops=100 * blocks * rows * mix, transcendentals=0, bytes_accessed=12 * blocks * rows * mix
        ),
    )(grad, projected, head_gain, cosine, sine, *awaited)


TAIL = 64


def half_tile(low, tile, keep_low):
    rolled = pltpu.roll(tile, TAIL, 1)
    return jnp.where(low, tile, rolled) if keep_low else jnp.where(low, rolled, tile)


def pack_kernel(info_ref, gate_ref, up_ref, *out_refs):
    low = info_ref[1] == 0
    main = (gate_ref.shape[1] - 2 * TAIL) // 2
    for index, out_ref in enumerate(out_refs):

        @pl.when(pl.program_id(0) == index)
        def _():
            for place in range(2):

                @pl.when(info_ref[1] == place)
                def _():
                    lanes = slice(place * main, (place + 1) * main)
                    out_ref[:, :main] = gate_ref[:, lanes].astype(BF16)
                    out_ref[:, main : 2 * main] = up_ref[:, lanes].astype(BF16)

            gate = half_tile(low, gate_ref[:, 2 * main :], True)
            up = half_tile(low, up_ref[:, 2 * main :], False)
            both = jnp.where(lane_of(gate.shape) < TAIL, gate, up)
            out_ref[:, 2 * main :] = both.astype(BF16)


def pack(info, gate, up, near):
    rows, width = gate.shape
    shard = width // near
    block = pl.BlockSpec((rows, shard), lambda step, info: (0, info[0] ^ step))
    out = pl.BlockSpec((rows, shard), lambda step, info: (0, 0))
    return pl.pallas_call(
        pack_kernel,
        out_shape=(jax.ShapeDtypeStruct((rows, shard), BF16),) * near,
        grid_spec=pltpu.PrefetchScalarGridSpec(
            num_scalar_prefetch=1, grid=(near,), in_specs=[block, block], out_specs=(out,) * near
        ),
        compiler_params=pltpu.CompilerParams(vmem_limit_bytes=32 * 1024 * 1024),
        cost_estimate=pl.CostEstimate(
            flops=0, transcendentals=0, bytes_accessed=10 * rows * width
        ),
    )(info, gate, up)


def spread_kernel(info_ref, *refs):
    pieces = (len(refs) - 2) // 2
    gate_ref, up_ref = refs[2 * pieces :]
    rows, shard = gate_ref.shape
    main = (shard - 2 * TAIL) // 2
    low = info_ref[1] == 0

    def whole(parts):
        parts = [ref[:, 0] for ref in parts]
        return jnp.concatenate(parts, axis=1).reshape(rows, shard).astype(F32)

    mine, other = whole(refs[:pieces]), whole(refs[pieces : 2 * pieces])
    first = jnp.where(low, mine, other)
    second = jnp.where(low, other, mine)
    gate_ref[:, :main] = first[:, :main]
    gate_ref[:, main : 2 * main] = second[:, :main]
    up_ref[:, :main] = first[:, main : 2 * main]
    up_ref[:, main : 2 * main] = second[:, main : 2 * main]
    first, second = first[:, 2 * main :], second[:, 2 * main :]
    lower = lane_of(first.shape) < TAIL
    gate_ref[:, 2 * main :] = jnp.where(lower, first, pltpu.roll(second, TAIL, 1))
    up_ref[:, 2 * main :] = jnp.where(lower, pltpu.roll(first, TAIL, 1), second)


def spread(info, mine, other):
    planes, near, _, width = mine[0].shape
    rows = planes * sum(piece.shape[2] for piece in mine)
    block = lambda piece: pl.BlockSpec(
        (planes, 1, piece.shape[2], width), lambda step, info: (0, step, 0, 0)
    )
    out = pl.BlockSpec((rows, width), lambda step, info: (0, info[0] ^ step))
    shape = jax.ShapeDtypeStruct((rows, near * width), F32)
    return pl.pallas_call(
        spread_kernel,
        out_shape=(shape, shape),
        grid_spec=pltpu.PrefetchScalarGridSpec(
            num_scalar_prefetch=1,
            grid=(near,),
            in_specs=[block(piece) for piece in (*mine, *other)],
            out_specs=(out, out),
        ),
        compiler_params=pltpu.CompilerParams(vmem_limit_bytes=40 * 1024 * 1024),
        cost_estimate=pl.CostEstimate(
            flops=0, transcendentals=0, bytes_accessed=12 * near * rows * width
        ),
    )(info, *mine, *other)


def mix_heads_kernel(query_ref, key_ref, value_ref, out_ref):
    wide = 2 * HEAD
    for head in range(KV_HEADS):
        out_ref[:, 2 * head * wide : (2 * head + 1) * wide] = query_ref[
            :, head * wide : (head + 1) * wide
        ].astype(BF16)
        tile = slice(head // 2 * wide, (head // 2 + 1) * wide)
        key, value = key_ref[:, tile], value_ref[:, tile]
        if head % 2 == 0:
            value = pltpu.roll(value, HEAD, 1)
        else:
            key = pltpu.roll(key, HEAD, 1)
        both = jnp.where(lane_of(key.shape) < HEAD, key, value)
        out_ref[:, (2 * head + 1) * wide : (2 * head + 2) * wide] = both.astype(BF16)


def mix_heads(query, key, value):
    rows = query.shape[0]
    width = query.shape[1] + key.shape[1] + value.shape[1]
    return pl.pallas_call(
        mix_heads_kernel,
        out_shape=jax.ShapeDtypeStruct((rows, width), BF16),
        compiler_params=pltpu.CompilerParams(vmem_limit_bytes=32 * 1024 * 1024),
        cost_estimate=pl.CostEstimate(flops=0, transcendentals=0, bytes_accessed=6 * rows * width),
    )(query, key, value)


def part_heads_kernel(mixed_ref, query_ref, key_ref, value_ref):
    wide = 2 * HEAD
    for pair in range(KV_HEADS // 2):
        tile = slice(pair * wide, (pair + 1) * wide)
        for head in (2 * pair, 2 * pair + 1):
            query_ref[:, head * wide : (head + 1) * wide] = mixed_ref[head, :, :wide].astype(F32)
        first = mixed_ref[2 * pair, :, wide:].astype(F32)
        second = mixed_ref[2 * pair + 1, :, wide:].astype(F32)
        lower = lane_of(first.shape) < HEAD
        key_ref[:, tile] = jnp.where(lower, first, pltpu.roll(second, HEAD, 1))
        value_ref[:, tile] = jnp.where(lower, pltpu.roll(first, HEAD, 1), second)


def part_heads(mixed, rows):
    heads, _, mix = mixed.shape
    block = pl.BlockSpec((heads, rows, mix), lambda step: (0, 0, 0))
    out = lambda count: pl.BlockSpec((rows, count * HEAD), lambda step: (0, 0))
    shape = lambda count: jax.ShapeDtypeStruct((rows, count * HEAD), F32)
    return pl.pallas_call(
        part_heads_kernel,
        out_shape=(shape(GROUP * heads), shape(heads), shape(heads)),
        grid=(1,),
        in_specs=[block],
        out_specs=(out(GROUP * heads), out(heads), out(heads)),
        compiler_params=pltpu.CompilerParams(vmem_limit_bytes=32 * 1024 * 1024),
        cost_estimate=pl.CostEstimate(
            flops=0, transcendentals=0, bytes_accessed=6 * rows * heads * 4 * HEAD
        ),
    )(mixed)


def row_scale(values):
    return lax.rsqrt(jnp.mean(values * values, axis=-1, keepdims=True) + epsilon)


def norm_back(grad, values, gain):
    scale = row_scale(values)
    gain_grad = jnp.sum(grad * values * scale, axis=0, keepdims=True)
    grad = grad * gain
    mean = jnp.mean(grad * values, axis=-1, keepdims=True)
    return scale * grad - values * (scale * scale * scale) * mean, gain_grad


def row_call(kernel, outs, flops, *operands, awaited=()):
    moved = sum(a.size * a.dtype.itemsize for a in operands)
    count = len(operands)

    def body(*refs):
        kernel(*refs[:count], *refs[count + len(awaited) :])

    return pl.pallas_call(
        body,
        grid=(1,),
        in_specs=[whole_spec(a.shape) for a in operands] + awaiting(len(awaited)),
        out_specs=tuple(whole_spec(shape) for shape, _ in outs),
        out_shape=tuple(jax.ShapeDtypeStruct(shape, kind) for shape, kind in outs),
        compiler_params=pltpu.CompilerParams(vmem_limit_bytes=40 * 1024 * 1024),
        cost_estimate=pl.CostEstimate(flops=flops, transcendentals=0, bytes_accessed=moved),
    )(*operands, *awaited)


def join_kernel(heads_ref, weight_ref, input_ref, gain_ref, hidden_ref, mid_ref):
    wide = heads_ref.shape[2]
    total = input_ref[...].astype(F32)
    for head in range(0, heads_ref.shape[0], 2):
        both = jnp.concatenate([heads_ref[head], heads_ref[head + 1]], axis=1)
        total = total + product(both, weight_ref[head * wide : (head + 2) * wide])
    hidden_ref[...] = total
    mid_ref[...] = (total * row_scale(total) * gain_ref[...]).astype(BF16)


def middle_kernel(
    low_own, low_got, high_own, high_got, hidden_ref, outer_ref, gain_ref, weight_ref,
    grad_ref, low_ref, heads_ref, part_ref,
):
    grad_mid = jnp.concatenate(
        [
            low_own[...] + low_got[...].astype(F32),
            high_own[...] + high_got[...].astype(F32),
        ],
        axis=0,
    )
    through, gain_grad = norm_back(grad_mid, hidden_ref[...], gain_ref[...])
    part_ref[...] = gain_grad
    grad = outer_ref[...].astype(F32) + through
    grad_ref[...] = grad
    low = grad.astype(BF16)
    low_ref[...] = low
    wide = heads_ref.shape[2]
    for head in range(0, heads_ref.shape[0], 2):
        both = by_transpose(low, weight_ref[head * wide : (head + 2) * wide]).astype(BF16)
        heads_ref[head] = both[:, :wide]
        heads_ref[head + 1] = both[:, wide:]


def output_weight_kernel(heads_ref, grad_ref, out_ref):
    wide = heads_ref.shape[2]
    for head in range(heads_ref.shape[0]):
        out_ref[head * wide : (head + 1) * wide] = transpose_by(
            heads_ref[head], grad_ref[...]
        ).astype(BF16)


def input_kernel(heads_ref, weight_ref, input_ref, hidden_ref, gain_ref, grad_ref, part_ref):
    mix = heads_ref.shape[2]
    total = jnp.zeros(grad_ref.shape, F32)
    for head in range(heads_ref.shape[0]):
        total = total + by_transpose(
            heads_ref[head], weight_ref[:, head * mix : (head + 1) * mix]
        )
    through, gain_grad = norm_back(total, input_ref[...].astype(F32), gain_ref[...])
    part_ref[...] = gain_grad
    grad_ref[...] = hidden_ref[...] + through


def feed_kernel(info_ref, *refs):
    mids, outers, weights = refs[:10], refs[10], refs[11:15]
    down_ref = refs[15]
    mid_ref, outer_ref, inner_ref, grads_ref, send_ref, keep_ref = refs[-12:-6]
    mid_all, outer_all, weight_all, mid_sem, outer_sem, weight_sem = refs[-6:]
    step = pl.program_id(0)
    main = inner_ref.shape[1] - TAIL

    def weight_copy(block):
        return pltpu.make_async_copy(
            weights[block], weight_all.at[info_ref[0] ^ block], weight_sem.at[block]
        )

    @pl.when(step == 0)
    def _():
        for block in range(len(weights)):
            weight_copy(block).start()
        for block in range(PLANE):
            change = 2 * block + 1 if block < 4 else 2 * block - 8
            pltpu.make_async_copy(
                outers.at[change ^ info_ref[2]], outer_all.at[block], outer_sem.at[block]
            ).start()
            first = 5 * (block // 4) + block % 4
            if block % 4 < 3:
                pltpu.make_async_copy(mids[first], mid_all.at[block], mid_sem.at[block]).start()
            else:
                half = mids[first].shape[0]
                for part in range(2):
                    target = mid_all.at[block].at[pl.ds(part * half, half)]
                    pltpu.make_async_copy(mids[first + part], target, mid_sem.at[block]).start()
        for block in range(len(weights)):
            weight_copy(block).wait()

    for which in range(2):
        block = 2 * step + which
        pltpu.make_async_copy(mids[0], mid_all.at[block], mid_sem.at[block]).wait()
        pltpu.make_async_copy(outers.at[0], outer_all.at[block], outer_sem.at[block]).wait()
    fsdp, depth, width = weight_all.shape
    weight = weight_all[...].reshape(fsdp * depth, width)
    rows = mid_all.shape[1]

    def unit(gate, up, back):
        share = jax.nn.sigmoid(gate)
        silu = gate * share
        inner = (silu * up).astype(BF16)
        grad_gate = (back * up * (share + silu * (1.0 - share))).astype(BF16)
        return inner, grad_gate, (back * silu).astype(BF16)

    tail = slice(2 * main, 2 * main + TAIL)
    last = slice(2 * main + TAIL, 2 * main + 2 * TAIL)
    parts = []
    for which in range(2):
        mine = slice(which * rows, (which + 1) * rows)
        mid, outer = mid_all[2 * step + which], outer_all[2 * step + which]
        mid_ref[mine] = mid
        outer_ref[mine] = outer
        both = product(mid, weight)
        back = by_transpose(outer, down_ref[...])
        inner, gate, up = unit(both[:, :main], both[:, main : 2 * main], back[:, :main])
        inner_ref[mine, :main] = inner
        inner, gate_tail, up_tail = unit(both[:, tail], both[:, last], back[:, main:])
        inner_ref[mine, main:] = inner
        grads = jnp.concatenate([gate, up, gate_tail, up_tail], axis=1)
        grads_ref[mine] = grads
        parts.append(by_transpose(grads, weight).astype(BF16))

    @pl.when(step < 2)
    def _():
        send_ref[:rows] = parts[0]
        send_ref[rows:] = parts[1]

    @pl.when(step >= 2)
    def _():
        keep_ref[:rows] = parts[0]
        keep_ref[rows:] = parts[1]


def feed(info, mids, outers, weights, down, awaited=()):
    rows, width = mids[0].shape
    depth, units2 = weights[0].shape
    units = units2 // 2
    count = PLANE
    anywhere = pl.BlockSpec(memory_space=pl.ANY)
    flat = lambda last: pl.BlockSpec((2 * rows, last), lambda step, info: (step, 0))
    send = pl.BlockSpec((2 * rows, width), lambda step, info: (jnp.minimum(step, 1), 0))
    keep = pl.BlockSpec((2 * rows, width), lambda step, info: (jnp.maximum(step - 2, 0), 0))
    shape = lambda tall, last: jax.ShapeDtypeStruct((tall * rows, last), BF16)
    return pl.pallas_call(
        feed_kernel,
        out_shape=(
            shape(count, width),
            shape(count, width),
            shape(count, units),
            shape(count, units2),
            shape(count // 2, width),
            shape(count // 2, width),
        ),
        grid_spec=pltpu.PrefetchScalarGridSpec(
            num_scalar_prefetch=1,
            grid=(count // 2,),
            in_specs=[anywhere] * (len(mids) + 1 + len(weights))
            + [pl.BlockSpec(down.shape, lambda step, info: (0, 0))]
            + [anywhere] * len(awaited),
            out_specs=(flat(width), flat(width), flat(units), flat(units2), send, keep),
            scratch_shapes=[
                pltpu.VMEM((count, rows, width), BF16),
                pltpu.VMEM((count, rows, width), BF16),
                pltpu.VMEM((len(weights), depth, units2), BF16),
                pltpu.SemaphoreType.DMA((count,)),
                pltpu.SemaphoreType.DMA((count,)),
                pltpu.SemaphoreType.DMA((len(weights),)),
            ],
        ),
        compiler_params=pltpu.CompilerParams(vmem_limit_bytes=56 * 1024 * 1024),
        cost_estimate=pl.CostEstimate(
            flops=10 * count * rows * width * units,
            transcendentals=count * rows * units,
            bytes_accessed=12 * count * rows * width,
        ),
    )(info, *mids, outers, *weights, down, *awaited)


def hidden_weight_kernel(mid_ref, grads_ref, out_ref):
    planes, _, rows, width = out_ref.shape
    total = transpose_by(mid_ref[...], grads_ref[...])
    out_ref[:, 0] = total.reshape(planes, rows, width).astype(BF16)


def hidden_weight(mid, grads, near, planes):
    count, width = mid.shape
    units2 = grads.shape[1]
    rows = width // near // planes
    return pl.pallas_call(
        hidden_weight_kernel,
        out_shape=jax.ShapeDtypeStruct((planes, near, rows, units2), BF16),
        grid=(near,),
        in_specs=[
            pl.BlockSpec((count, width // near), lambda step: (0, step)),
            pl.BlockSpec((count, units2), lambda step: (0, 0)),
        ],
        out_specs=pl.BlockSpec((planes, 1, rows, units2), lambda step: (0, step, 0, 0)),
        compiler_params=pltpu.CompilerParams(vmem_limit_bytes=48 * 1024 * 1024),
        cost_estimate=pl.CostEstimate(
            flops=2 * count * width * units2,
            transcendentals=0,
            bytes_accessed=2 * count * (width + units2) + 2 * width * units2,
        ),
    )(mid, grads)


def awaiting(count):
    return [pl.BlockSpec(memory_space=pl.ANY)] * count


def whole_spec(shape):
    return pl.BlockSpec(shape, lambda *_: (0,) * len(shape))


def split_rows(blocks, cut, awaited):
    rows, width = blocks[0].shape
    count = len(blocks)

    def kernel(*refs):
        for index in range(count):
            refs[-2][index] = refs[index][:cut]
            refs[-1][index] = refs[index][cut:]

    return pl.pallas_call(
        kernel,
        out_shape=(
            jax.ShapeDtypeStruct((count, cut, width), BF16),
            jax.ShapeDtypeStruct((count, rows - cut, width), BF16),
        ),
        grid=(1,),
        in_specs=[whole_spec((rows, width))] * count + awaiting(len(awaited)),
        out_specs=(whole_spec((count, cut, width)), whole_spec((count, rows - cut, width))),
        cost_estimate=pl.CostEstimate(
            flops=0, transcendentals=0, bytes_accessed=4 * count * rows * width
        ),
    )(*blocks, *awaited)


def head_message(first, second, rest, awaited):
    def kernel(first_ref, second_ref, rest_ref, *refs):
        rows = first_ref.shape[0]
        refs[-1][:rows] = (first_ref[...].astype(F32) + second_ref[...].astype(F32)).astype(BF16)
        refs[-1][rows:] = rest_ref[...].astype(BF16)

    rows, width = first.shape
    shape = (rows + rest.shape[0], width)
    return pl.pallas_call(
        kernel,
        out_shape=jax.ShapeDtypeStruct(shape, BF16),
        grid=(1,),
        in_specs=[whole_spec(a.shape) for a in (first, second, rest)] + awaiting(len(awaited)),
        out_specs=whole_spec(shape),
        cost_estimate=pl.CostEstimate(
            flops=0, transcendentals=0, bytes_accessed=6 * rows * width
        ),
    )(first, second, rest, *awaited)


def per_device(
    inputs,
    lengths,
    positions,
    cotangent,
    w_query,
    w_key,
    w_value,
    w_output,
    w_gate,
    w_up,
    w_down,
    attn_gain,
    ffn_gain,
    query_gain,
    key_gain,
):
    groups, slot_count, model_width = inputs.shape
    row_count = groups * slot_count
    own_rows = w_query.shape[0]
    ctx_size = lax.axis_size("ctx")
    fsdp_size = lax.axis_size("fsdp")
    me_f = lax.axis_index("fsdp")
    me_c = lax.axis_index("ctx")
    inner = KV_HEADS
    outer = ctx_size // inner
    inner_groups = [[o * inner + i for i in range(inner)] for o in range(outer)]
    outer_groups = [[o * inner + i for o in range(outer)] for i in range(inner)]
    planes = ctx_size // 2
    plane_groups_z = [[2 * i + low for i in range(planes)] for low in range(2)]
    low_bit = me_c % 2
    my_head = me_c % inner
    mix = 4 * HEAD
    wide = GROUP * HEAD
    ff_shard = w_down.shape[0]
    ff_own = ff_shard // 2
    ff_main = ff_own - TAIL

    slots = me_c * slot_count + jnp.arange(slot_count)
    valid = (slots[None, :] < lengths[:, None]).astype(F32).reshape(row_count, 1)
    info = jnp.concatenate([(me_c // inner * inner)[None].astype(jnp.int32), lengths])
    device_info = jnp.stack([me_f, low_bit]).astype(jnp.int32)
    plane_info = jnp.stack([me_f, low_bit, low_bit * fsdp_size + me_f]).astype(jnp.int32)

    small = query_gain.shape[0]
    gains = jnp.concatenate([attn_gain, ffn_gain, query_gain, key_gain]).astype(BF16)[None]
    gains = jnp.concatenate(gather_near(gains), axis=0).astype(F32)
    gains = jnp.stack([pick(gains, me_f ^ k) for k in range(fsdp_size)])
    attn_scale = gains[:, :own_rows].reshape(1, model_width)
    ffn_scale = gains[:, own_rows : 2 * own_rows].reshape(1, model_width)
    qgain_scale = gains[:, 2 * own_rows : 2 * own_rows + small].reshape(-1)
    kgain_scale = gains[:, 2 * own_rows + small :].reshape(-1)
    head_gain = jnp.concatenate(
        [qgain_scale] * GROUP + [kgain_scale, jnp.ones((HEAD,), F32)]
    ).reshape(1, mix)

    line = Line()
    rows_shape = (row_count, model_width)

    line = Line()
    rows_shape = (row_count, model_width)
    rows_flops = 2 * row_count * model_width * model_width

    flat_low = inputs.reshape(row_count, model_width)
    place_row = positions.reshape(1, row_count)
    digits = jnp.concatenate([place_row // POSITION_BASE, place_row % POSITION_BASE], axis=0)
    digits = jnp.pad(
        digits.astype(BF16), ((0, POSITION_ROWS - 2), (0, model_width - row_count))
    )
    near = line(lambda a, b: jnp.concatenate([a, b], axis=0), flat_low, digits)
    far, following = trade(near, 4), ring_step(near)
    places = ring_places(my_head // 2)
    frequency = rope_base ** (-jnp.arange(0, HEAD, 2).astype(F32) / HEAD)
    frequency = jnp.concatenate([frequency] * (2 * GROUP)).reshape(1, wide)

    qkv_own = line(mix_heads, w_query, w_key, w_value)
    head_weight = lax.dynamic_slice_in_dim(qkv_own, my_head * mix, mix, 1)
    head_weight = jnp.stack(gather_near(head_weight))
    output_own = line(lambda a: a.astype(BF16), w_output)
    output_weight = lax.all_gather(output_own, "fsdp", axis=0, tiled=True)
    gu_own = line(lambda a, b: pack(device_info, a, b, fsdp_size), w_gate, w_up)
    gu_parts = [gu_own[0]] + [trade(gu_own[k], k) for k in range(1, fsdp_size)]

    earlier = ()
    for step in range(4):
        if step < 3:
            far, following = line.wait(far, following)
            next_far = trade(following, 4)
            after_next = ring_step(following) if step < 2 else None
        else:
            gu_parts = line.wait(*gu_parts)
        project_info = jnp.stack([me_f, low_bit, places[step]]).astype(jnp.int32)
        earlier = line(
            lambda a, b, c, *rest: project(
                project_info, a, b, c, attn_scale, head_gain, frequency, inner, rest or None
            ),
            near,
            far,
            head_weight,
            *earlier,
        )
        near, far, following = following, next_far, after_next
    normed_all, projected, mixed, cosine, sine = earlier
    mixed = mixed.reshape(inner, groups, slot_count, mix)

    qkv_weight = lax.all_gather(qkv_own, "fsdp", axis=0, tiled=True)
    if outer == 1:
        attended = line(lambda a: attention(info, a, a, None, (qkv_weight,)), mixed)
    else:
        shared = lax.all_gather(
            mixed[..., 2 * HEAD :], "ctx", axis=0, axis_index_groups=outer_groups, tiled=True
        )
        attended = line(lambda a, b: attention(info, a, b), mixed, shared)

    def exchange(values):
        return lax.all_to_all(values, "ctx", 0, 0, axis_index_groups=inner_groups, tiled=True)

    attended = exchange(attended.reshape(inner, row_count, wide))
    outer_low = line(
        lambda a: (a.reshape(rows_shape).astype(F32) * valid).astype(BF16), cotangent
    )
    outer_all = lax.all_gather(
        outer_low, ("ctx", "fsdp"), axis=0, axis_index_groups=plane_groups(), tiled=False
    )
    down_weight = line(
        lambda a: jnp.concatenate(
            [
                lax.dynamic_slice_in_dim(a, low_bit * ff_main, ff_main, 0),
                lax.dynamic_slice_in_dim(a, 2 * ff_main + low_bit * TAIL, TAIL, 0),
            ],
            axis=0,
        ).astype(BF16),
        w_down,
    )
    hidden_res, mid_low = line(
        lambda *a: row_call(
            join_kernel, ((rows_shape, F32), (rows_shape, BF16)), rows_flops, *a
        ),
        attended,
        output_weight,
        flat_low,
        ffn_scale,
    )
    mid_x, mid_y = trade(mid_low, 2), trade(mid_low, 4)
    mid_cut = line(cut_far, mid_x, mid_y)
    mid_corner = trade(mid_cut[0], 4), trade(mid_cut[1], 2)
    mid_all = gather_plane(mid_low, mid_x, mid_y, mid_corner)

    mid_all, outer_all, inner_low, grad_gu, send, keep = line(
        lambda *a: feed(plane_info, a[:10], a[10], a[11:15], a[15]),
        *mid_all,
        outer_all,
        *gu_parts,
        down_weight,
    )
    got = trade(send, 1)
    gu_part = line(lambda a, b: hidden_weight(a, b, fsdp_size, planes), mid_all, grad_gu)
    gu_sum = lax.psum_scatter(
        gu_part.reshape(-1, 2 * ff_own),
        "ctx",
        scatter_dimension=0,
        axis_index_groups=plane_groups_z,
        tiled=True,
    )
    low_send, high_send, low, high = line(cut_plane, got, keep)
    low_got, high_got = trade(low_send, 2), trade(high_send, 4)
    down_part = line(lambda a, b: transpose_by(a, b).astype(BF16), inner_low, outer_all)
    down_sum = lax.psum(down_part, "ctx", axis_index_groups=plane_groups_z)
    result_part = line(lambda a, b: product(a, b).astype(BF16), inner_low, down_weight)
    low_far, high_far, low_own, high_own = line(join_plane, low, high, low_got, high_got)
    low_got, high_got = trade(low_far, 4), trade(high_far, 2)
    (qkv_weight,) = line.wait(qkv_weight)
    grad_hidden, grad_attn_low, grad_heads, ffn_part = line(
        lambda *a: row_call(
            middle_kernel,
            (
                (rows_shape, F32),
                (rows_shape, BF16),
                ((inner, row_count, wide), BF16),
                ((1, model_width), F32),
            ),
            rows_flops,
            *a,
        ),
        low_own,
        low_got,
        high_own,
        high_got,
        hidden_res,
        outer_low,
        ffn_scale,
        output_weight,
    )

    grad_heads = exchange(grad_heads).reshape(inner, groups, slot_count, wide)
    (output_part,) = line(
        lambda *a: row_call(
            output_weight_kernel, (((model_width, model_width), BF16),), rows_flops, *a
        ),
        attended,
        grad_attn_low,
    )
    gu_own = line(
        lambda a: tuple(
            pick(a.reshape(fsdp_size, own_rows // planes, 2 * ff_own), me_f ^ k)
            for k in range(fsdp_size)
        ),
        gu_sum,
    )
    gu_blocks = [gu_own[0]] + [trade(gu_own[k], k) for k in range(1, fsdp_size)]
    if outer == 1:
        grad_mixed = line(
            lambda a, b: attention(info, a, a, b, gu_own[1:]), mixed, grad_heads
        )
    else:
        grad_q, grad_kv = line(
            lambda a, b, c: attention(info, a, b, c), mixed, shared, grad_heads
        )
        grad_kv = lax.psum_scatter(
            grad_kv, "ctx", scatter_dimension=0, axis_index_groups=outer_groups, tiled=True
        )
        grad_mixed = jnp.concatenate([grad_q, grad_kv], axis=-1)
    grad_head, head_part = line(
        lambda *a: unproject(*a, gu_blocks[1:]),
        grad_mixed.reshape(inner, row_count, mix),
        projected,
        head_gain,
        cosine,
        sine,
    )
    grad_qkv = exchange(grad_head)
    head_rows = line(
        lambda a, b: transpose_by(
            a.reshape(inner * row_count, model_width), b.reshape(-1, mix)
        ).astype(BF16),
        normed_all,
        grad_head,
    )
    head_send, head_keep = line(
        lambda a: cut_near(a.reshape(fsdp_size, own_rows, mix), me_f), head_rows
    )
    head_got = trade(head_send, 1)
    cut = own_rows // planes // 2
    first_half, second_half = split_rows(gu_blocks, cut, (down_sum,))
    gu_mine = [
        lax.all_gather(piece, "ctx", axis=0, axis_index_groups=plane_groups_z, tiled=False)
        for piece in (first_half, second_half)
    ]
    gu_other = [trade(piece, fsdp_size) for piece in gu_mine]

    head_pair = line(add_low, head_keep, head_got)
    head_far = trade(head_pair[1], 2)
    output_send, output_keep = line(
        lambda a: cut_near(a.reshape(fsdp_size, own_rows, model_width), me_f), output_part
    )
    output_got = trade(output_send, 1)
    output_pair = line(add_low, output_keep, output_got)
    output_far = trade(output_pair[1], 2)
    down_other = trade(down_sum, fsdp_size)
    input_grad, attn_part = line(
        lambda *a: row_call(
            input_kernel,
            ((rows_shape, F32), ((1, model_width), F32)),
            rows_flops * KV_HEADS * mix // model_width,
            *a,
            awaited=(gu_mine[0],),
        ),
        grad_qkv,
        qkv_weight,
        flat_low,
        grad_hidden,
        attn_scale,
    )
    input_grad = input_grad.reshape(groups, slot_count, model_width)
    qgain_part = sum(head_part[0, i * HEAD : (i + 1) * HEAD] for i in range(GROUP))
    kgain_part = head_part[0, GROUP * HEAD : (GROUP + 1) * HEAD]
    gain_parts = jnp.concatenate(
        [
            attn_part.reshape(fsdp_size, own_rows),
            ffn_part.reshape(fsdp_size, own_rows),
            qgain_part.reshape(fsdp_size, small),
            kgain_part.reshape(fsdp_size, small),
        ],
        axis=-1,
    )
    output_own = line(add_low, output_pair[0], output_far)
    output_grad = (
        ctx_sum(output_own.reshape(ctx_size, own_rows // ctx_size, model_width))
        .reshape(own_rows, model_width)
        .astype(F32)
    )
    result_send, result_keep = halves(result_part)
    got = trade(result_send, 1)
    gain_count = gain_parts.size
    gain_near = gain_parts + trade(gain_parts, 1)
    gain_near = gain_near + trade(gain_near, 2)
    gain_rows = -(-gain_count // (16 * mix)) * 16
    gain_near = jnp.pad(gain_near.reshape(-1), (0, gain_rows * mix - gain_count))
    gain_near = gain_near.reshape(gain_rows, mix)
    head_first, head_second = head_pair[0], head_far
    if outer > 1:
        gain_near = lax.psum(gain_near, "ctx", axis_index_groups=outer_groups)
        head_first = lax.psum(
            add_low(head_first, head_second).astype(F32), "ctx", axis_index_groups=outer_groups
        ).astype(BF16)
        head_second = jnp.zeros_like(head_first)
    head_own = head_message(head_first, head_second, gain_near, (gu_other[0],))
    head_blocks = lax.all_gather(
        head_own, "ctx", axis=0, axis_index_groups=inner_groups, tiled=False
    )
    gain_sum = jnp.sum(head_blocks[:, own_rows:].astype(F32), axis=0)
    gain_sum = pick(gain_sum.reshape(-1)[:gain_count].reshape(gain_parts.shape), me_f)
    low_send, high_send, result_low, result_high = line(cut_plane, got, result_keep)
    result_low_got, result_high_got = trade(low_send, 2), trade(high_send, 4)
    low_far, high_far, low_own, high_own = line(
        join_plane, result_low, result_high, result_low_got, result_high_got
    )
    low_got, high_got = trade(low_far, 4), trade(high_far, 2)
    result = line(
        lambda a, b, c, d, e: (
            valid * (e + jnp.concatenate([a + b.astype(F32), c + d.astype(F32)], axis=0))
        ).astype(BF16),
        low_own,
        low_got,
        high_own,
        high_got,
        hidden_res,
    )
    block_output = result.reshape(groups, slot_count, model_width)

    query_grad, key_grad, value_grad = part_heads(head_blocks, own_rows)
    first = jnp.where(low_bit == 0, down_sum, down_other)
    second = jnp.where(low_bit == 0, down_other, down_sum)
    down_grad = jnp.concatenate(
        [first[:ff_main], second[:ff_main], first[ff_main:], second[ff_main:]], axis=0
    ).astype(F32)
    gate_grad, up_grad = spread(device_info, gu_mine, gu_other)

    return (
        block_output,
        input_grad,
        query_grad,
        key_grad,
        value_grad,
        output_grad,
        gate_grad,
        up_grad,
        down_grad,
        gain_sum[:own_rows],
        gain_sum[own_rows : 2 * own_rows],
        gain_sum[2 * own_rows : 2 * own_rows + small],
        gain_sum[2 * own_rows + small :],
    )


def solution(mesh):
    return jax.shard_map(
        per_device,
        mesh=mesh,
        in_specs=(
            P("fsdp", "ctx", None),
            P("fsdp"),
            P("fsdp", "ctx"),
            P("fsdp", "ctx", None),
            P("fsdp", None),
            P("fsdp", None),
            P("fsdp", None),
            P("fsdp", None),
            P("fsdp", None),
            P("fsdp", None),
            P("fsdp", None),
            P("fsdp"),
            P("fsdp"),
            P("fsdp"),
            P("fsdp"),
        ),
        out_specs=(
            P("fsdp", "ctx", None),
            P("fsdp", "ctx", None),
            P("fsdp", None),
            P("fsdp", None),
            P("fsdp", None),
            P("fsdp", None),
            P("fsdp", None),
            P("fsdp", None),
            P("fsdp", None),
            P("fsdp"),
            P("fsdp"),
            P("fsdp"),
            P("fsdp"),
        ),
        check_vma=False,
    )
```

time: 608 us -> 495 us (0.81)
  Pallas kernels: 18.1 us -> 94.1 us
  waiting for transfers between devices: 251 us -> 193 us
  blocking collectives: 57.2 us -> 0 us
  matrix products: 54.4 us -> 13 us
  other arithmetic: 52.6 us -> 38.7 us
  local copies, waits for them, and re-layouts: 84.8 us -> 72.6 us
    ppermute x44 -> x53, waiting for transfers between devices: 218 us -> 141 us  [the longest x50 138 us: trade(): lax.ppermute(values, ('ctx', 'fsdp'), [(i, i ^ step) for i in range(size)])]
    pallas_call x0 -> x17, Pallas kernels: none -> 75 us  [the longest x1 25.2 us: feed(): pl.pallas_call(feed_kernel, out_shape=(shape(count, width), shape(count,...]
    psum x1 -> x0, blocking collectives: 51.1 us -> none  [per_device(): gain_sum = pick(lax.psum(gain_parts, ('ctx', 'fsdp')), me_f)]
    dot_general x12 -> x3, matrix products: 54.4 us -> 13 us  [dot_over(): lax.dot_general(left, right, (((left_dim,), (right_dim,)), ((), ())), pre...]
    psum x0 -> x1, waiting for transfers between devices: none -> 24.6 us  [per_device(): down_sum = lax.psum(down_part, 'ctx', axis_index_groups=plane_groups_z)]
    all_gather x2 -> x6, waiting for transfers between devices: 30.7 us -> 8.63 us  [the longest x2 5.96 us: per_device(): lax.all_gather(piece, 'ctx', axis=0, axis_index_groups=plane_groups_z, ti...]
    unnamed x135 -> x164, local copies, waits for them, and re-layouts: 32.7 us -> 50.3 us
    all_to_all x4 -> x3, waiting for transfers between devices: 2.06 us -> 17.9 us  [exchange(): lax.all_to_all(values, 'ctx', 0, 0, axis_index_groups=inner_groups, tiled...]
  transfers between devices with their start and end apart: 50 -> 64, of which waited for: 22 -> 28; matrix products, arithmetic and copies ran while one was open for 26% -> 14% of each run, Pallas kernels for 3% -> 13%
where the time goes in v2:
time: 495 us; the launch traced here: 490 us
  waiting for transfers between devices  193 us (39%)
  Pallas kernels  94.1 us (19%)
  local copies, waits for them, and re-layouts  72.6 us (15%)
  starting transfers between devices  62.5 us (13%)
  other arithmetic  38.7 us (8%)
  between operations  15.7 us (3%)
  matrix products  13 us (3%)
    ppermute x50, waiting for transfers between devices, trade(): lax.ppermute(values, ('ctx', 'fsdp'), [(i, i ^ step) for i in range(size)])  138 us
    unnamed x164, local copies, waits for them, and re-layouts  50.3 us
    ppermute x50, starting transfers between devices, trade(): lax.ppermute(values, ('ctx', 'fsdp'), [(i, i ^ step) for i in range(size)])  42.8 us
    pallas_call x1, Pallas kernels, feed(): pl.pallas_call(feed_kernel, out_shape=(shape(count, width), shape(count,...  25.2 us
    psum x1, waiting for transfers between devices, per_device(): down_sum = lax.psum(down_part, 'ctx', axis_index_groups=plane_groups_z)  24.6 us
    all_to_all x3, waiting for transfers between devices, exchange(): lax.all_to_all(values, 'ctx', 0, 0, axis_index_groups=inner_groups, tiled...  17.9 us
    pallas_call x4, Pallas kernels, project(): pl.pallas_call(project_kernel, out_shape=tuple((jax.ShapeDtypeStruct((blo...  14.3 us
    convert_element_type x9, other arithmetic, add_low(): return (first.astype(F32) + second.astype(F32)).astype(BF16)  14.2 us
  transfers between devices with their start and end apart: 64, of which 28 were waited for; matrix products, arithmetic and copies ran while one was open for 14% of the time, Pallas kernels for 13%

profile of v2, /device:TPU:0, one launch (start us, length us, event | category | flops | bytes accessed | tf_op | source)
XLA Modules:
  0.0 489.5 jit_solution(17053382712210950985)
XLA Ops:
  13.7 3.0 collective-permute-start
  25.5 2.5 pad_add_fusion.6
  28.4 2.3 copy-done.24
  30.7 2.3 copy-done.25
  33.1 2.0 shard_map.256
  37.0 2.6 collective-permute-start.3
  43.4 2.7 shard_map.257
  46.1 5.5 %collective-permute-done.2.far_ref = bf16[272,1024]{1,0:T(8,128)(2,1)} collective-permute-done((bf16[272,1024]{1,0:T(8,128)(2,1)}, bf16[272,1024]{1,0:T(8,128)(2,1)}, u32[]{:S(2)}, u32[]{:S(2)}) %collective-permute-start.2) | collective-permute-done | bytes 557088 | tf_op jit(solution)/shard_map/ppermute | solution.py:44
  54.2 2.1 collective-permute-start.11
  58.2 4.0 shard_map.258
  62.2 2.0 copy-done
  67.4 1.7 collective-permute-done.11.near_ref
  70.0 2.2 copy-done.1
  76.7 3.7 shard_map.259
  80.5 2.2 collective-permute-done.23.refs_13_
  82.7 13.2 %collective-permute-done.24.refs_14_ = bf16[256,1152]{1,0:T(8,128)(2,1)} collective-permute-done((bf16[256,1152]{1,0:T(8,128)(2,1)}, bf16[256,1152]{1,0:T(8,128)(2,1)}, u32[]{:S(2)}, u32[]{:S(2)}) %collective-permute-start.24) | collective-permute-done | bytes 589856 | tf_op jit(solution)/shard_map/ppermute | solution.py:44
  95.9 3.9 shard_map.260
  99.8 2.1 copy-done.2
  103.9 2.2 copy-done.4
  106.1 7.9 %shard_map.261 = bf16[8,2,128,128]{3,2,1,0:T(8,128)(2,1)S(1)} custom-call(s32[3]{0:T(128)S(1)} %pad_add_fusion.2.info_ref, bf16[8,2,128,256]{3,2,1,0:T(8,128)(2,1)S(1)} %bitcast.121, bf16[8,2,128,256]{3,2,1,0:T(8,128)(2,1)S(1)} %bitcast.122, bf16[1024,2048]{1,0:T(8,128)(2,1)S(1)} %copy-done.4), custom_call_target="tpu_custom_call" | custom-call | flops 536870912 | bytes 4194304 | tf_op jit(solution)/shard_map/pallas_call | solution.py:373
  115.9 4.2 all-to-all-start
  120.1 2.0 fusion.4.refs_5_
  123.1 1.7 dynamic-slice_convert_fusion
  126.1 10.0 %all-to-all-done.refs_0_ = bf16[8,256,128]{2,1,0:T(8,128)(2,1)} async-done(((bf16[8,256,128]{2,1,0:T(8,128)(2,1)}), bf16[8,256,128]{2,1,0:T(8,128)(2,1)}, u32[]{:S(2)}, u32[]{:S(2)}) %all-to-all-start) | async-done | bytes 524320 | tf_op jit(solution)/shard_map/all_to_all | solution.py:1137
  136.1 1.6 copy-done.16
  138.7 1.9 shard_map.262
  141.6 3.3 collective-permute-start.14
  146.6 21.7 %collective-permute-done.14.refs_6_ = bf16[256,1024]{1,0:T(8,128)(2,1)S(1)} collective-permute-done((bf16[256,1024]{1,0:T(8,128)(2,1)S(1)}, bf16[256,1024]{1,0:T(8,128)(2,1)S(1)}, u32[]{:S(2)}, u32[]{:S(2)}) %collective-permute-start.14) | collective-permute-done | bytes 524320 | tf_op jit(solution)/shard_map/ppermute | solution.py:44
  171.0 5.8 %collective-permute-done.18.refs_8_ = bf16[128,1024]{1,0:T(8,128)(2,1)S(1)} collective-permute-done((bf16[128,1024]{1,0:T(8,128)(2,1)S(1)}, bf16[128,1024]{1,0:T(8,128)(2,1)S(1)}, u32[]{:S(2)}, u32[]{:S(2)}) %collective-permute-start.18) | collective-permute-done | bytes 262176 | tf_op jit(solution)/shard_map/ppermute | solution.py:44
  181.1 25.2 %shard_map.263 = (bf16[2048,1024]{1,0:T(8,128)(2,1)}, bf16[2048,1024]{1,0:T(8,128)(2,1)}, bf16[2048,576]{1,0:T(8,128)(2,1)}, bf16[2048,1152]{1,0:T(8,128)(2,1)},...) custom-call(s32[3]{0:T(128)} %get-tuple-element.416.info_ref, bf16[256,1024]{1,0:T(8,128)(2,1)} %copy-done.70, ...), custom_call_target="tpu_custom_call" | custom-call | flops 12079595520 | bytes 25165824 | tf_op jit(solution)/shard_map/pallas_call | solution.py:907
  206.5 9.1 %shard_map.264 = bf16[4,4,64,1152]{3,2,1,0:T(8,128)(2,1)S(1)} custom-call(bf16[2048,1024]{1,0:T(8,128)(2,1)} %get-tuple-element.281.mid_ref, bf16[2048,1152]{1,0:T(8,128)(2,1)} %get-tuple-element.282.grads_ref), custom_call_target="tpu_custom_call" | custom-call | flops 4831838208 | bytes 11272192 | tf_op jit(solution)/shard_map/pallas_call | solution.py:952
  217.1 3.3 add_convert_fusion.1
  224.0 3.8 convolution_convert_fusion.1
  230.2 6.7 %convolution_convert_fusion = bf16[2048,1024]{1,0:T(8,128)(2,1)} fusion(bf16[2048,576]{1,0:T(8,128)(2,1)} %get-tuple-element.287, bf16[576,1024]{1,0:T(8,128)(2,1)S(1)} %copy-done.63), kind=kOutput, calls=%fused_computation.2 | convolution fusion | flops 2418016256 | bytes 7733248 | tf_op jit(solution)/shard_map/dot_general | solution.py:22
  237.4 6.0 %collective-permute-done.28 = bf16[2,128,1024]{2,1,0:T(8,128)(2,1)S(1)} collective-permute-done((bf16[2,128,1024]{2,1,0:T(8,128)(2,1)S(1)}, bf16[2,128,1024]{2,1,0:T(8,128)(2,1)S(1)}, u32[]{:S(2)}, u32[]{:S(2)}) %collective-permute-start.28) | collective-permute-done | bytes 524320 | tf_op jit(solution)/shard_map/ppermute | solution.py:44
  247.1 4.4 collective-permute-done.30.refs_3_
  256.8 4.9 all-to-all-start.1
  263.3 1.8 shard_map.266
  266.5 1.9 dynamic-slice_bitcast_fusion.1
  270.3 7.9 %all-to-all-done.1 = bf16[8,256,128]{2,1,0:T(8,128)(2,1)} async-done(((bf16[8,256,128]{2,1,0:T(8,128)(2,1)}), bf16[8,256,128]{2,1,0:T(8,128)(2,1)}, u32[]{:S(2)}, u32[]{:S(2)}) %all-to-all-start.1) | async-done | bytes 524320 | tf_op jit(solution)/shard_map/all_to_all | solution.py:1137
  278.2 11.2 %shard_map.267 = f32[8,2,128,256]{3,2,1,0:T(8,128)S(1)} custom-call(s32[3]{0:T(128)S(1)} %pad_add_fusion.2.info_ref, bf16[8,2,128,256]{3,2,1,0:T(8,128)(2,1)S(1)} %bitcast.123, bf16[8,2,128,256]{3,2,1,0:T(8,128)(2,1)S(1)} %bitcast.124, bf16[8,2,128,128]{3,2,1,0:T(8,128)(2,1)} %bitcast.28.grad_ref, bf16[64,1152]{1,0:T(8,128)(2,1)} %get-tuple-element.389.refs_0_, ...), custom_call_target="tpu_custom_call" | custom-call | flops 1342177280 | bytes 4194304 | tf_op jit(solution)/shard_map/pallas_call | solution.py:386
  289.5 5.6 %shard_map.268 = (bf16[8,256,256]{2,1,0:T(8,128)(2,1)}, f32[1,256]{1,0:T(1,128)S(1)}) custom-call(f32[8,256,256]{2,1,0:T(8,128)S(1)} %bitcast.126, f32[8,256,256]{2,1,0:T(8,128)S(1)} %get-tuple-element.313.projected_ref, f32[1,256]{1,0:T(1,128)S(1)} %bitcast.150, f32[8,256,128]{2,1,0:T(8,128)S(1)} %copy-done.9, f32[8,256,128]{2,1,0:T(8,128)S(1)} %copy-done.13, ...), custom_call_target="tpu_custom_call" | custom-call | flops 52428800 | bytes 6291456 | tf_op jit(solution)/shard_map/pallas_call | solution.py:566
  295.0 2.5 fusion
  297.8 24.6 %all-reduce.4.cloned.1.call-done.refs_4_ = bf16[576,1024]{1,0:T(8,128)(2,1)} async-done(((bf16[576,1024]{1,0:T(8,128)(2,1)}), bf16[576,1024]{1,0:T(8,128)(2,1)}) %all-reduce.4.cloned.1.call-update) | async-done | bytes 1179664 | tf_op jit(solution)/shard_map/psum | solution.py:1189
  326.2 3.6 all-to-all-start.2
  329.8 2.0 shard_map.269
  332.2 4.7 fusion.20
  338.6 21.4 %collective-permute-done.52 = bf16[576,1024]{1,0:T(8,128)(2,1)} collective-permute-done((bf16[576,1024]{1,0:T(8,128)(2,1)}, bf16[576,1024]{1,0:T(8,128)(2,1)}, u32[]{:S(2)}, u32[]{:S(2)}) %collective-permute-start.52) | collective-permute-done | bytes 1179680 | tf_op jit(solution)/shard_map/ppermute | solution.py:44
  366.8 2.7 maximum_convert_fusion
  369.8 6.0 %all-gather.16.cloned.1.call-done = bf16[16,32,1152]{2,1,0:T(8,128)(2,1)} async-done(((bf16[4,32,1152]{2,1,0:T(8,128)(2,1)}), bf16[16,32,1152]{2,1,0:T(8,128)(2,1)}) %all-gather.16.cloned.1.call-update) | async-done | bytes 1179664 | tf_op jit(solution)/shard_map/all_gather | solution.py:1267
  377.3 2.2 copy-done.5
  382.0 2.6 shard_map.270
  387.4 3.2 add_convert_fusion
  391.6 17.9 %collective-permute-done.45 = bf16[4,32,1024]{2,1,0:T(8,128)(2,1)S(1)} collective-permute-done((bf16[4,32,1024]{2,1,0:T(8,128)(2,1)S(1)}, bf16[4,32,1024]{2,1,0:T(8,128)(2,1)S(1)}, u32[]{:S(2)}, u32[]{:S(2)}) %collective-permute-start.45) | collective-permute-done | bytes 262176 | tf_op jit(solution)/shard_map/ppermute | solution.py:44
  412.8 1.7 collective-permute-start.38
  417.1 3.8 collective-permute-done.47
  421.8 2.6 collective-permute-done.43
  426.6 1.6 collective-permute-start.51
  430.2 2.1 fusion.9
  433.8 1.7 shard_map.271
  439.9 22.3 %collective-permute-done.39 = bf16[128,1024]{1,0:T(8,128)(2,1)S(1)} collective-permute-done((bf16[128,1024]{1,0:T(8,128)(2,1)S(1)}, bf16[128,1024]{1,0:T(8,128)(2,1)S(1)}, u32[]{:S(2)}, u32[]{:S(2)}) %collective-permute-start.39) | collective-permute-done | bytes 262176 | tf_op jit(solution)/shard_map/ppermute | solution.py:44
  464.3 5.1 %collective-permute-done.50 = bf16[4,32,1024]{2,1,0:T(8,128)(2,1)S(1)} collective-permute-done((bf16[4,32,1024]{2,1,0:T(8,128)(2,1)S(1)}, bf16[4,32,1024]{2,1,0:T(8,128)(2,1)S(1)}, u32[]{:S(2)}, u32[]{:S(2)}) %collective-permute-start.50) | collective-permute-done | bytes 262176 | tf_op jit(solution)/shard_map/ppermute | solution.py:44
  470.6 4.8 shard_map.273
  475.4 2.7 all-gather.18.cloned.1.call-done
  (369 shorter events, 117.8 us)
Async XLA Ops:
  7.2 96.7 %all-gather.10.cloned.1.call-start = ((), (), s32[]{:S(2)}) async-start(), calls=%async_computation.4 | async-start | bytes 5242880 | tf_op jit(solution)/shard_map/all_gather | solution.py:1127
  13.7 112.4 %all-gather.12.cloned.1.call-start = ((), (), s32[]{:S(2)}) async-start(), calls=%async_computation.5 | async-start | bytes 2621440 | tf_op jit(solution)/shard_map/all_gather | solution.py:1101
  13.7 22.7 %collective-permute-start = (bf16[272,1024]{1,0:T(8,128)(2,1)S(1)}, bf16[272,1024]{1,0:T(8,128)(2,1)S(1)}, u32[]{:S(2)}, u32[]{:S(2)}) collective-permute-start(bf16[272,1024]{1,0:T(8,128)(2,1)S(1)} %pad_maximum_fusion.3.near_ref), channel_id=1, source_target_pairs={{0,4},{1,5},{2,6},{3,7},{4,0},{5,1},{6,2},{7,3},{8,12},{9,13},{10,... | collective-permute-start | bytes 1671176 | tf_op jit(solution)/shard_map/ppermute | solution.py:44
  16.8 19.7 %collective-permute-start.1 = (bf16[272,1024]{1,0:T(8,128)(2,1)S(1)}, bf16[272,1024]{1,0:T(8,128)(2,1)}, u32[]{:S(2)}, u32[]{:S(2)}) collective-permute-start(bf16[272,1024]{1,0:T(8,128)(2,1)S(1)} %pad_maximum_fusion.3.near_ref), channel_id=1, source_target_pairs={{0,8},{4,12},{8,24},{12,28},{16,0},{20,4},{24,16},{28,20},{1,9},{5... | collective-permute-start | bytes 1671176 | tf_op jit(solution)/shard_map/ppermute | solution.py:131
  18.5 9.6 %collective-permute-start.8 = (bf16[1,544]{1,0:T(2,128)(2,1)S(1)}, bf16[1,544]{1,0:T(2,128)(2,1)S(1)}, u32[]{:S(2)}, u32[]{:S(2)}) collective-permute-start(bf16[1,544]{1,0:T(2,128)(2,1)S(1)} %pad_maximum_fusion.14), channel_id=1, source_target_pairs={{0,2},{1,3},{2,0},{3,1},{4,6},{5,7},{6,4},{7,5},{8,10},{9,11},{10,... | collective-permute-start | bytes 3272 | tf_op jit(solution)/shard_map/ppermute | solution.py:44
  20.0 15.9 %collective-permute-start.7 = (bf16[1,544]{1,0:T(2,128)(2,1)S(1)}, bf16[1,544]{1,0:T(2,128)(2,1)S(1)}, u32[]{:S(2)}, u32[]{:S(2)}) collective-permute-start(bf16[1,544]{1,0:T(2,128)(2,1)S(1)} %pad_maximum_fusion.14), channel_id=1, source_target_pairs={{0,1},{1,0},{2,3},{3,2},{4,5},{5,4},{6,7},{7,6},{8,9},{9,8},{10,11... | collective-permute-start | bytes 3272 | tf_op jit(solution)/shard_map/ppermute | solution.py:44
  20.9 18.7 %collective-permute-start.5 = (bf16[256,256]{1,0:T(8,128)(2,1)S(1)}, bf16[256,256]{1,0:T(8,128)(2,1)S(1)}, u32[]{:S(2)}, u32[]{:S(2)}) collective-permute-start(bf16[256,256]{1,0:T(8,128)(2,1)S(1)} %constant_dynamic-slice_fusion.14), channel_id=1, source_target_pairs={{0,2},{1,3},{2,0},{3,1},{4,6},{5,7},{6,4},{7,5},{8,10},{9,11},{10,... | collective-permute-start | bytes 393224 | tf_op jit(solution)/shard_map/ppermute | solution.py:44
  22.4 158.7 %all-gather.14.cloned.1.call-start = ((), (), s32[]{:S(2)}) async-start(), calls=%async_computation.6 | async-start | bytes 4718592 | tf_op jit(solution)/shard_map/all_gather | solution.py:1143
  28.1 8.2 %collective-permute-start.9 = (bf16[1,544]{1,0:T(2,128)(2,1)S(1)}, bf16[1,544]{1,0:T(2,128)(2,1)S(1)}, u32[]{:S(2)}, u32[]{:S(2)}) collective-permute-start(bf16[1,544]{1,0:T(2,128)(2,1)S(1)} %collective-permute-done.8), channel_id=1, source_target_pairs={{0,1},{1,0},{2,3},{3,2},{4,5},{5,4},{6,7},{7,6},{8,9},{9,8},{10,11... | collective-permute-start | bytes 3272 | tf_op jit(solution)/shard_map/ppermute | solution.py:44
  35.9 4.1 collective-permute-start.4
  36.5 15.1 %collective-permute-start.2 = (bf16[272,1024]{1,0:T(8,128)(2,1)}, bf16[272,1024]{1,0:T(8,128)(2,1)}, u32[]{:S(2)}, u32[]{:S(2)}) collective-permute-start(bf16[272,1024]{1,0:T(8,128)(2,1)} %collective-permute-done.1.near_ref), channel_id=1, source_target_pairs={{0,4},{1,5},{2,6},{3,7},{4,0},{5,1},{6,2},{7,3},{8,12},{9,13},{10,... | collective-permute-start | bytes 1671176 | tf_op jit(solution)/shard_map/ppermute | solution.py:44
  37.0 15.7 %collective-permute-start.3 = (bf16[272,1024]{1,0:T(8,128)(2,1)}, bf16[272,1024]{1,0:T(8,128)(2,1)}, u32[]{:S(2)}, u32[]{:S(2)}) collective-permute-start(bf16[272,1024]{1,0:T(8,128)(2,1)} %collective-permute-done.1.near_ref), channel_id=1, source_target_pairs={{0,8},{4,12},{8,24},{12,28},{16,0},{20,4},{24,16},{28,20},{1,9},{5... | collective-permute-start | bytes 1671176 | tf_op jit(solution)/shard_map/ppermute | solution.py:131
  39.6 1.3 collective-permute-start.6
  52.8 13.9 %collective-permute-start.10 = (bf16[272,1024]{1,0:T(8,128)(2,1)}, bf16[272,1024]{1,0:T(8,128)(2,1)S(1)}, u32[]{:S(2)}, u32[]{:S(2)}) collective-permute-start(bf16[272,1024]{1,0:T(8,128)(2,1)} %collective-permute-done.3.near_ref), channel_id=1, source_target_pairs={{0,4},{1,5},{2,6},{3,7},{4,0},{5,1},{6,2},{7,3},{8,12},{9,13},{10,... | collective-permute-start | bytes 1671176 | tf_op jit(solution)/shard_map/ppermute | solution.py:44
  54.2 15.0 %collective-permute-start.11 = (bf16[272,1024]{1,0:T(8,128)(2,1)}, bf16[272,1024]{1,0:T(8,128)(2,1)}, u32[]{:S(2)}, u32[]{:S(2)}) collective-permute-start(bf16[272,1024]{1,0:T(8,128)(2,1)} %collective-permute-done.3.near_ref), channel_id=1, source_target_pairs={{0,8},{4,12},{8,24},{12,28},{16,0},{20,4},{24,16},{28,20},{1,9},{5... | collective-permute-start | bytes 1671176 | tf_op jit(solution)/shard_map/ppermute | solution.py:131
  56.3 24.1 %collective-permute-start.22 = (bf16[256,1152]{1,0:T(8,128)(2,1)}, bf16[256,1152]{1,0:T(8,128)(2,1)}, u32[]{:S(2)}, u32[]{:S(2)}) collective-permute-start(bf16[256,1152]{1,0:T(8,128)(2,1)} %copy-done.55), channel_id=1, source_target_pairs={{0,1},{1,0},{2,3},{3,2},{4,5},{5,4},{6,7},{7,6},{8,9},{9,8},{10,11... | collective-permute-start | bytes 1769480 | tf_op jit(solution)/shard_map/ppermute | solution.py:44
  56.3 26.3 %collective-permute-start.23 = (bf16[256,1152]{1,0:T(8,128)(2,1)}, bf16[256,1152]{1,0:T(8,128)(2,1)}, u32[]{:S(2)}, u32[]{:S(2)}) collective-permute-start(bf16[256,1152]{1,0:T(8,128)(2,1)} %copy-done.54), channel_id=1, source_target_pairs={{0,2},{1,3},{2,0},{3,1},{4,6},{5,7},{6,4},{7,5},{8,10},{9,11},{10,... | collective-permute-start | bytes 1769480 | tf_op jit(solution)/shard_map/ppermute | solution.py:44
  57.9 38.0 %collective-permute-start.24 = (bf16[256,1152]{1,0:T(8,128)(2,1)}, bf16[256,1152]{1,0:T(8,128)(2,1)}, u32[]{:S(2)}, u32[]{:S(2)}) collective-permute-start(bf16[256,1152]{1,0:T(8,128)(2,1)} %copy-done.53), channel_id=1, source_target_pairs={{0,3},{1,2},{2,1},{3,0},{4,7},{5,6},{6,5},{7,4},{8,11},{9,10},{10,... | collective-permute-start | bytes 1769480 | tf_op jit(solution)/shard_map/ppermute | solution.py:44
  69.2 26.7 %collective-permute-start.12 = (bf16[272,1024]{1,0:T(8,128)(2,1)}, bf16[272,1024]{1,0:T(8,128)(2,1)}, u32[]{:S(2)}, u32[]{:S(2)}) collective-permute-start(bf16[272,1024]{1,0:T(8,128)(2,1)} %collective-permute-done.11.near_ref), channel_id=1, source_target_pairs={{0,4},{1,5},{2,6},{3,7},{4,0},{5,1},{6,2},{7,3},{8,12},{9,13},{10,... | collective-permute-start | bytes 1671176 | tf_op jit(solution)/shard_map/ppermute | solution.py:44
  115.9 20.2 %all-to-all-start = ((bf16[8,256,128]{2,1,0:T(8,128)(2,1)}), bf16[8,256,128]{2,1,0:T(8,128)(2,1)}, u32[]{:S(2)}, u32[]{:S(2)}) async-start(bf16[8,256,128]{2,1,0:T(8,128)(2,1)} %bitcast.134), calls=%async_computation | async-start | bytes 1048576 | tf_op jit(solution)/shard_map/all_to_all | solution.py:1137
  120.0 146.4 %reduce-scatter.2.cloned.1.call-start = ((), (), s32[]{:S(2)}) async-start(), calls=%async_computation.7 | async-start | bytes 2949120 | tf_op jit(solution)/shard_map/reduce_scatter | solution.py:1179
  141.6 26.7 %collective-permute-start.14 = (bf16[256,1024]{1,0:T(8,128)(2,1)S(1)}, bf16[256,1024]{1,0:T(8,128)(2,1)S(1)}, u32[]{:S(2)}, u32[]{:S(2)}) collective-permute-start(bf16[256,1024]{1,0:T(8,128)(2,1)S(1)} %get-tuple-element.264.refs_5_), channel_id=1, source_target_pairs={{0,2},{1,3},{2,0},{3,1},{4,6},{5,7},{6,4},{7,5},{8,10},{9,11},{10,... | collective-permute-start | bytes 1572872 | tf_op jit(solution)/shard_map/ppermute | solution.py:44
  144.8 23.4 %collective-permute-start.16 = (bf16[256,1024]{1,0:T(8,128)(2,1)S(1)}, bf16[256,1024]{1,0:T(8,128)(2,1)S(1)}, u32[]{:S(2)}, u32[]{:S(2)}) collective-permute-start(bf16[256,1024]{1,0:T(8,128)(2,1)S(1)} %get-tuple-element.264.refs_5_), channel_id=1, source_target_pairs={{0,4},{1,5},{2,6},{3,7},{4,0},{5,1},{6,2},{7,3},{8,12},{9,13},{10,... | collective-permute-start | bytes 1572872 | tf_op jit(solution)/shard_map/ppermute | solution.py:44
  146.3 31.7 %collective-permute-start.13 = (bf16[256,1024]{1,0:T(8,128)(2,1)S(1)}, bf16[256,1024]{1,0:T(8,128)(2,1)S(1)}, u32[]{:S(2)}, u32[]{:S(2)}) collective-permute-start(bf16[256,1024]{1,0:T(8,128)(2,1)S(1)} %get-tuple-element.264.refs_5_), channel_id=1, source_target_pairs={{0,1},{1,0},{2,3},{3,2},{4,5},{5,4},{6,7},{7,6},{8,9},{9,8},{10,11... | collective-permute-start | bytes 1572872 | tf_op jit(solution)/shard_map/ppermute | solution.py:44
  168.3 8.5 %collective-permute-start.18 = (bf16[128,1024]{1,0:T(8,128)(2,1)S(1)}, bf16[128,1024]{1,0:T(8,128)(2,1)S(1)}, u32[]{:S(2)}, u32[]{:S(2)}) collective-permute-start(bf16[128,1024]{1,0:T(8,128)(2,1)S(1)} %slice.219), channel_id=1, source_target_pairs={{0,4},{1,5},{2,6},{3,7},{4,0},{5,1},{6,2},{7,3},{8,12},{9,13},{10,... | collective-permute-start | bytes 786440 | tf_op jit(solution)/shard_map/ppermute | solution.py:44
  169.8 8.2 %collective-permute-start.20 = (bf16[128,1024]{1,0:T(8,128)(2,1)S(1)}, bf16[128,1024]{1,0:T(8,128)(2,1)S(1)}, u32[]{:S(2)}, u32[]{:S(2)}) collective-permute-start(bf16[128,1024]{1,0:T(8,128)(2,1)S(1)} %slice.220), channel_id=1, source_target_pairs={{0,2},{1,3},{2,0},{3,1},{4,6},{5,7},{6,4},{7,5},{8,10},{9,11},{10,... | collective-permute-start | bytes 786440 | tf_op jit(solution)/shard_map/ppermute | solution.py:44
  170.5 9.1 %collective-permute-start.15 = (bf16[256,1024]{1,0:T(8,128)(2,1)S(1)}, bf16[256,1024]{1,0:T(8,128)(2,1)S(1)}, u32[]{:S(2)}, u32[]{:S(2)}) collective-permute-start(bf16[256,1024]{1,0:T(8,128)(2,1)S(1)} %collective-permute-done.14.refs_6_), channel_id=1, source_target_pairs={{0,1},{1,0},{2,3},{3,2},{4,5},{5,4},{6,7},{7,6},{8,9},{9,8},{10,11... | collective-permute-start | bytes 1572872 | tf_op jit(solution)/shard_map/ppermute | solution.py:44
  170.5 10.6 %collective-permute-start.17 = (bf16[256,1024]{1,0:T(8,128)(2,1)S(1)}, bf16[256,1024]{1,0:T(8,128)(2,1)}, u32[]{:S(2)}, u32[]{:S(2)}) collective-permute-start(bf16[256,1024]{1,0:T(8,128)(2,1)S(1)} %collective-permute-done.16.refs_7_), channel_id=1, source_target_pairs={{0,1},{1,0},{2,3},{3,2},{4,5},{5,4},{6,7},{7,6},{8,9},{9,8},{10,11... | collective-permute-start | bytes 1572872 | tf_op jit(solution)/shard_map/ppermute | solution.py:44
  176.8 1.5 collective-permute-start.19
  178.1 1.5 collective-permute-start.21
  206.3 10.7 %collective-permute-start.25 = (bf16[1024,1024]{1,0:T(8,128)(2,1)}, bf16[1024,1024]{1,0:T(8,128)(2,1)}, u32[]{:S(2)}, u32[]{:S(2)}) collective-permute-start(bf16[1024,1024]{1,0:T(8,128)(2,1)} %get-tuple-element.277), channel_id=1, source_target_pairs={{0,1},{1,0},{2,3},{3,2},{4,5},{5,4},{6,7},{7,6},{8,9},{9,8},{10,11... | collective-permute-start | bytes 6291464 | tf_op jit(solution)/shard_map/ppermute | solution.py:44
  222.9 14.5 %collective-permute-start.27 = (bf16[2,128,1024]{2,1,0:T(8,128)(2,1)}, bf16[2,128,1024]{2,1,0:T(8,128)(2,1)}, u32[]{:S(2)}, u32[]{:S(2)}) collective-permute-start(bf16[2,128,1024]{2,1,0:T(8,128)(2,1)} %pad_maximum_fusion.5), channel_id=1, source_target_pairs={{0,2},{1,3},{2,0},{3,1},{4,6},{5,7},{6,4},{7,5},{8,10},{9,11},{10,... | collective-permute-start | bytes 1572872 | tf_op jit(solution)/shard_map/ppermute | solution.py:44
  229.2 14.3 %collective-permute-start.28 = (bf16[2,128,1024]{2,1,0:T(8,128)(2,1)S(1)}, bf16[2,128,1024]{2,1,0:T(8,128)(2,1)S(1)}, u32[]{:S(2)}, u32[]{:S(2)}) collective-permute-start(bf16[2,128,1024]{2,1,0:T(8,128)(2,1)S(1)} %get-tuple-element.373), channel_id=1, source_target_pairs={{0,4},{1,5},{2,6},{3,7},{4,0},{5,1},{6,2},{7,3},{8,12},{9,13},{10,... | collective-permute-start | bytes 1572872 | tf_op jit(solution)/shard_map/ppermute | solution.py:44
  243.6 7.9 %collective-permute-start.30 = (bf16[128,1024]{1,0:T(8,128)(2,1)S(1)}, bf16[128,1024]{1,0:T(8,128)(2,1)S(1)}, u32[]{:S(2)}, u32[]{:S(2)}) collective-permute-start(bf16[128,1024]{1,0:T(8,128)(2,1)S(1)} %get-tuple-element.383), channel_id=1, source_target_pairs={{0,2},{1,3},{2,0},{3,1},{4,6},{5,7},{6,4},{7,5},{8,10},{9,11},{10,... | collective-permute-start | bytes 786440 | tf_op jit(solution)/shard_map/ppermute | solution.py:44
  245.6 7.4 %collective-permute-start.29 = (bf16[128,1024]{1,0:T(8,128)(2,1)S(1)}, bf16[128,1024]{1,0:T(8,128)(2,1)S(1)}, u32[]{:S(2)}, u32[]{:S(2)}) collective-permute-start(bf16[128,1024]{1,0:T(8,128)(2,1)S(1)} %get-tuple-element.385), channel_id=1, source_target_pairs={{0,4},{1,5},{2,6},{3,7},{4,0},{5,1},{6,2},{7,3},{8,12},{9,13},{10,... | collective-permute-start | bytes 786440 | tf_op jit(solution)/shard_map/ppermute | solution.py:44
  256.8 21.4 %all-to-all-start.1 = ((bf16[8,256,128]{2,1,0:T(8,128)(2,1)}), bf16[8,256,128]{2,1,0:T(8,128)(2,1)}, u32[]{:S(2)}, u32[]{:S(2)}) async-start(bf16[8,256,128]{2,1,0:T(8,128)(2,1)} %copy-done.47), calls=%async_computation.1 | async-start | bytes 1048576 | tf_op jit(solution)/shard_map/all_to_all | solution.py:1137
  261.7 60.7 %all-reduce.4.cloned.1.call-start = ((), (), s32[]{:S(2)}) async-start(), calls=%async_computation.8 | async-start | bytes 2359296 | tf_op jit(solution)/shard_map/psum | solution.py:1189
  268.4 21.0 %collective-permute-start.31 = (bf16[64,1152]{1,0:T(8,128)(2,1)}, bf16[64,1152]{1,0:T(8,128)(2,1)S(1)}, u32[]{:S(2)}, u32[]{:S(2)}) collective-permute-start(bf16[64,1152]{1,0:T(8,128)(2,1)} %get-tuple-element.389.refs_0_), channel_id=1, source_target_pairs={{0,1},{1,0},{2,3},{3,2},{4,5},{5,4},{6,7},{7,6},{8,9},{9,8},{10,11... | collective-permute-start | bytes 442376 | tf_op jit(solution)/shard_map/ppermute | solution.py:44
  268.4 21.0 %collective-permute-start.32 = (bf16[64,1152]{1,0:T(8,128)(2,1)}, bf16[64,1152]{1,0:T(8,128)(2,1)S(1)}, u32[]{:S(2)}, u32[]{:S(2)}) collective-permute-start(bf16[64,1152]{1,0:T(8,128)(2,1)} %get-tuple-element.388.refs_1_), channel_id=1, source_target_pairs={{0,2},{1,3},{2,0},{3,1},{4,6},{5,7},{6,4},{7,5},{8,10},{9,11},{10,... | collective-permute-start | bytes 442376 | tf_op jit(solution)/shard_map/ppermute | solution.py:44
  269.7 19.7 %collective-permute-start.33 = (bf16[64,1152]{1,0:T(8,128)(2,1)}, bf16[64,1152]{1,0:T(8,128)(2,1)}, u32[]{:S(2)}, u32[]{:S(2)}) collective-permute-start(bf16[64,1152]{1,0:T(8,128)(2,1)} %get-tuple-element.387.refs_2_), channel_id=1, source_target_pairs={{0,3},{1,2},{2,1},{3,0},{4,7},{5,6},{6,5},{7,4},{8,11},{9,10},{10,... | collective-permute-start | bytes 442376 | tf_op jit(solution)/shard_map/ppermute | solution.py:44
  297.7 26.2 %collective-permute-start.34 = (bf16[2,256,256]{2,1,0:T(8,128)(2,1)S(1)}, bf16[2,256,256]{2,1,0:T(8,128)(2,1)S(1)}, u32[]{:S(2)}, u32[]{:S(2)}) collective-permute-start(bf16[2,256,256]{2,1,0:T(8,128)(2,1)S(1)} %pad_maximum_fusion.9), channel_id=1, source_target_pairs={{0,1},{1,0},{2,3},{3,2},{4,5},{5,4},{6,7},{7,6},{8,9},{9,8},{10,11... | collective-permute-start | bytes 786440 | tf_op jit(solution)/shard_map/ppermute | solution.py:44
  322.4 37.6 %collective-permute-start.52 = (bf16[576,1024]{1,0:T(8,128)(2,1)}, bf16[576,1024]{1,0:T(8,128)(2,1)}, u32[]{:S(2)}, u32[]{:S(2)}) collective-permute-start(bf16[576,1024]{1,0:T(8,128)(2,1)} %all-reduce.4.cloned.1.call-done.refs_4_), channel_id=1, source_target_pairs={{0,4},{1,5},{2,6},{3,7},{4,0},{5,1},{6,2},{7,3},{8,12},{9,13},{10,... | collective-permute-start | bytes 3538952 | tf_op jit(solution)/shard_map/ppermute | solution.py:44
  326.2 36.5 %collective-permute-start.35 = (bf16[2,256,1024]{2,1,0:T(8,128)(2,1)}, bf16[2,256,1024]{2,1,0:T(8,128)(2,1)}, u32[]{:S(2)}, u32[]{:S(2)}) collective-permute-start(bf16[2,256,1024]{2,1,0:T(8,128)(2,1)} %pad_maximum_fusion.2), channel_id=1, source_target_pairs={{0,1},{1,0},{2,3},{3,2},{4,5},{5,4},{6,7},{7,6},{8,9},{9,8},{10,11... | collective-permute-start | bytes 3145736 | tf_op jit(solution)/shard_map/ppermute | solution.py:44
  326.2 51.1 %all-to-all-start.2 = ((bf16[8,256,256]{2,1,0:T(8,128)(2,1)}), bf16[8,256,256]{2,1,0:T(8,128)(2,1)S(1)}, u32[]{:S(2)}, u32[]{:S(2)}) async-start(bf16[8,256,256]{2,1,0:T(8,128)(2,1)} %get-tuple-element.319), calls=%async_computation.3 | async-start | bytes 2097152 | tf_op jit(solution)/shard_map/all_to_all | solution.py:1137
  329.8 46.0 %all-gather.16.cloned.1.call-start = ((), (), s32[]{:S(2)}) async-start(), calls=%async_computation.9 | async-start | bytes 1474560 | tf_op jit(solution)/shard_map/all_gather | solution.py:1267
  331.9 94.7 %all-gather.20.cloned.1.call-start = ((), (), s32[]{:S(2)}) async-start(), calls=%async_computation.11 | async-start | bytes 1474560 | tf_op jit(solution)/shard_map/all_gather | solution.py:1267
  336.9 50.5 %collective-permute-start.26 = (bf16[1024,1024]{1,0:T(8,128)(2,1)}, bf16[1024,1024]{1,0:T(8,128)(2,1)}, u32[]{:S(2)}, u32[]{:S(2)}) collective-permute-start(bf16[1024,1024]{1,0:T(8,128)(2,1)} %get-tuple-element.362), channel_id=1, source_target_pairs={{0,1},{1,0},{2,3},{3,2},{4,5},{5,4},{6,7},{7,6},{8,9},{9,8},{10,11... | collective-permute-start | bytes 6291464 | tf_op jit(solution)/shard_map/ppermute | solution.py:44
  365.3 20.1 %collective-permute-start.36 = (bf16[256,1024]{1,0:T(8,128)(2,1)}, bf16[256,1024]{1,0:T(8,128)(2,1)}, u32[]{:S(2)}, u32[]{:S(2)}) collective-permute-start(bf16[256,1024]{1,0:T(8,128)(2,1)} %get-tuple-element.381), channel_id=1, source_target_pairs={{0,2},{1,3},{2,0},{3,1},{4,6},{5,7},{6,4},{7,5},{8,10},{9,11},{10,... | collective-permute-start | bytes 1572872 | tf_op jit(solution)/shard_map/ppermute | solution.py:44
  369.8 108.3 %all-gather.18.cloned.1.call-start = ((), (), s32[]{:S(2)}) async-start(), calls=%async_computation.10 | async-start | bytes 1253376 | tf_op jit(solution)/shard_map/all_gather | solution.py:1329
  375.8 57.0 %collective-permute-start.44 = (bf16[4,4,32,1152]{3,2,1,0:T(8,128)(2,1)}, bf16[4,4,32,1152]{3,2,1,0:T(8,128)(2,1)S(1)}, u32[]{:S(2)}, u32[]{:S(2)}) collective-permute-start(bf16[4,4,32,1152]{3,2,1,0:T(8,128)(2,1)} %bitcast.127), channel_id=1, source_target_pairs={{0,4},{1,5},{2,6},{3,7},{4,0},{5,1},{6,2},{7,3},{8,12},{9,13},{10,... | collective-permute-start | bytes 3538952 | tf_op jit(solution)/shard_map/ppermute | solution.py:44
  385.3 30.2 %collective-permute-start.42 = (f32[4,544]{1,0:T(4,128)S(1)}, f32[4,544]{1,0:T(4,128)S(1)}, u32[]{:S(2)}, u32[]{:S(2)}) collective-permute-start(f32[4,544]{1,0:T(4,128)S(1)} %pad_maximum_fusion.13), channel_id=1, source_target_pairs={{0,1},{1,0},{2,3},{3,2},{4,5},{5,4},{6,7},{7,6},{8,9},{9,8},{10,11... | collective-permute-start | bytes 26120 | tf_op jit(solution)/shard_map/ppermute | solution.py:44
  386.8 22.8 %collective-permute-start.45 = (bf16[4,32,1024]{2,1,0:T(8,128)(2,1)S(1)}, bf16[4,32,1024]{2,1,0:T(8,128)(2,1)S(1)}, u32[]{:S(2)}, u32[]{:S(2)}) collective-permute-start(bf16[4,32,1024]{2,1,0:T(8,128)(2,1)S(1)} %dynamic-slice_bitcast_fusion), channel_id=1, source_target_pairs={{0,4},{1,5},{2,6},{3,7},{4,0},{5,1},{6,2},{7,3},{8,12},{9,13},{10,... | collective-permute-start | bytes 786440 | tf_op jit(solution)/shard_map/ppermute | solution.py:44
  409.7 5.0 %collective-permute-start.46 = (bf16[2,32,1024]{2,1,0:T(8,128)(2,1)S(1)}, bf16[2,32,1024]{2,1,0:T(8,128)(2,1)S(1)}, u32[]{:S(2)}, u32[]{:S(2)}) collective-permute-start(bf16[2,32,1024]{2,1,0:T(8,128)(2,1)S(1)} %dynamic-slice_bitcast_fusion.5), channel_id=1, source_target_pairs={{0,8},{1,9},{2,10},{3,11},{4,12},{5,13},{6,14},{7,15},{8,0},{9,1},... | collective-permute-start | bytes 393224 | tf_op jit(solution)/shard_map/ppermute | solution.py:44
  411.4 17.5 %collective-permute-start.37 = (bf16[2,128,1024]{2,1,0:T(8,128)(2,1)}, bf16[2,128,1024]{2,1,0:T(8,128)(2,1)}, u32[]{:S(2)}, u32[]{:S(2)}) collective-permute-start(bf16[2,128,1024]{2,1,0:T(8,128)(2,1)} %pad_maximum_fusion.6), channel_id=1, source_target_pairs={{0,2},{1,3},{2,0},{3,1},{4,6},{5,7},{6,4},{7,5},{8,10},{9,11},{10,... | collective-permute-start | bytes 1572872 | tf_op jit(solution)/shard_map/ppermute | solution.py:44
  412.8 17.3 %collective-permute-start.38 = (bf16[2,128,1024]{2,1,0:T(8,128)(2,1)}, bf16[2,128,1024]{2,1,0:T(8,128)(2,1)}, u32[]{:S(2)}, u32[]{:S(2)}) collective-permute-start(bf16[2,128,1024]{2,1,0:T(8,128)(2,1)} %get-tuple-element.365), channel_id=1, source_target_pairs={{0,4},{1,5},{2,6},{3,7},{4,0},{5,1},{6,2},{7,3},{8,12},{9,13},{10,... | collective-permute-start | bytes 1572872 | tf_op jit(solution)/shard_map/ppermute | solution.py:44
  414.8 6.1 %collective-permute-start.47 = (bf16[1,32,1024]{2,1,0:T(8,128)(2,1)S(1)}, bf16[1,32,1024]{2,1,0:T(8,128)(2,1)S(1)}, u32[]{:S(2)}, u32[]{:S(2)}) collective-permute-start(bf16[1,32,1024]{2,1,0:T(8,128)(2,1)S(1)} %constant_dynamic-slice_fusion.1), channel_id=1, source_target_pairs={{0,16},{1,17},{2,18},{3,19},{4,20},{5,21},{6,22},{7,23},{8,24},{9,... | collective-permute-start | bytes 196616 | tf_op jit(solution)/shard_map/ppermute | solution.py:44
  415.6 8.8 %collective-permute-start.43 = (f32[4,544]{1,0:T(4,128)S(1)}, f32[4,544]{1,0:T(4,128)S(1)}, u32[]{:S(2)}, u32[]{:S(2)}) collective-permute-start(f32[4,544]{1,0:T(4,128)S(1)} %fusion.33), channel_id=1, source_target_pairs={{0,2},{1,3},{2,0},{3,1},{4,6},{5,7},{6,4},{7,5},{8,10},{9,11},{10,... | collective-permute-start | bytes 26120 | tf_op jit(solution)/shard_map/ppermute | solution.py:44
  420.9 5.7 %collective-permute-start.48 = (bf16[1,32,1024]{2,1,0:T(8,128)(2,1)S(1)}, bf16[1,32,1024]{2,1,0:T(8,128)(2,1)S(1)}, u32[]{:S(2)}, u32[]{:S(2)}) collective-permute-start(bf16[1,32,1024]{2,1,0:T(8,128)(2,1)S(1)} %add_convert_fusion.9), channel_id=1, source_target_pairs={{0,16},{1,17},{2,18},{3,19},{4,20},{5,21},{6,22},{7,23},{8,24},{9,... | collective-permute-start | bytes 196616 | tf_op jit(solution)/shard_map/ppermute | solution.py:44
  424.4 8.4 %collective-permute-start.41 = (bf16[256,256]{1,0:T(8,128)(2,1)}, bf16[256,256]{1,0:T(8,128)(2,1)}, u32[]{:S(2)}, u32[]{:S(2)}) collective-permute-start(bf16[256,256]{1,0:T(8,128)(2,1)} %get-tuple-element.399), channel_id=1, source_target_pairs={{0,2},{1,3},{2,0},{3,1},{4,6},{5,7},{6,4},{7,5},{8,10},{9,11},{10,... | collective-permute-start | bytes 393224 | tf_op jit(solution)/shard_map/ppermute | solution.py:44
  426.6 44.1 %collective-permute-start.51 = (bf16[4,4,32,1152]{3,2,1,0:T(8,128)(2,1)}, bf16[4,4,32,1152]{3,2,1,0:T(8,128)(2,1)S(1)}, u32[]{:S(2)}, u32[]{:S(2)}) collective-permute-start(bf16[4,4,32,1152]{3,2,1,0:T(8,128)(2,1)} %bitcast.137), channel_id=1, source_target_pairs={{0,4},{1,5},{2,6},{3,7},{4,0},{5,1},{6,2},{7,3},{8,12},{9,13},{10,... | collective-permute-start | bytes 3538952 | tf_op jit(solution)/shard_map/ppermute | solution.py:44
  428.9 8.5 %collective-permute-start.49 = (bf16[2,32,1024]{2,1,0:T(8,128)(2,1)}, bf16[2,32,1024]{2,1,0:T(8,128)(2,1)}, u32[]{:S(2)}, u32[]{:S(2)}) collective-permute-start(bf16[2,32,1024]{2,1,0:T(8,128)(2,1)} %pad_maximum_fusion.11), channel_id=1, source_target_pairs={{0,8},{1,9},{2,10},{3,11},{4,12},{5,13},{6,14},{7,15},{8,0},{9,1},... | collective-permute-start | bytes 393224 | tf_op jit(solution)/shard_map/ppermute | solution.py:44
  432.2 7.6 %collective-permute-start.40 = (bf16[128,1024]{1,0:T(8,128)(2,1)}, bf16[128,1024]{1,0:T(8,128)(2,1)}, u32[]{:S(2)}, u32[]{:S(2)}) collective-permute-start(bf16[128,1024]{1,0:T(8,128)(2,1)} %get-tuple-element.377), channel_id=1, source_target_pairs={{0,2},{1,3},{2,0},{3,1},{4,6},{5,7},{6,4},{7,5},{8,10},{9,11},{10,... | collective-permute-start | bytes 786440 | tf_op jit(solution)/shard_map/ppermute | solution.py:44
  436.7 25.4 %collective-permute-start.39 = (bf16[128,1024]{1,0:T(8,128)(2,1)S(1)}, bf16[128,1024]{1,0:T(8,128)(2,1)S(1)}, u32[]{:S(2)}, u32[]{:S(2)}) collective-permute-start(bf16[128,1024]{1,0:T(8,128)(2,1)S(1)} %get-tuple-element.379), channel_id=1, source_target_pairs={{0,4},{1,5},{2,6},{3,7},{4,0},{5,1},{6,2},{7,3},{8,12},{9,13},{10,... | collective-permute-start | bytes 786440 | tf_op jit(solution)/shard_map/ppermute | solution.py:44
  438.3 31.1 %collective-permute-start.50 = (bf16[4,32,1024]{2,1,0:T(8,128)(2,1)S(1)}, bf16[4,32,1024]{2,1,0:T(8,128)(2,1)S(1)}, u32[]{:S(2)}, u32[]{:S(2)}) collective-permute-start(bf16[4,32,1024]{2,1,0:T(8,128)(2,1)S(1)} %pad_maximum_fusion.10), channel_id=1, source_target_pairs={{0,4},{1,5},{2,6},{3,7},{4,0},{5,1},{6,2},{7,3},{8,12},{9,13},{10,... | collective-permute-start | bytes 786440 | tf_op jit(solution)/shard_map/ppermute | solution.py:44
  (80 other events, 407.4 us)
Sparse Core Ops, SparseCore 0:
  13.8 37.1 all-gather.9
  53.1 33.9 all-gather.11
  116.0 53.7 all-gather.13
  217.2 46.9 reduce-scatter.1
  266.4 55.9 all-reduce.3
  332.5 43.2 all-gather.15
  377.4 30.0 all-gather.19
  435.6 42.4 all-gather.17

commit v3 on v2

--- a/solution.py
+++ b/solution.py
@@ -967,6 +967,17 @@
     )(mid, grads)
 
 
+def down_spread_kernel(low_ref, mine_ref, other_ref, out_ref):
+    main = mine_ref.shape[0] - TAIL
+    low = low_ref[...] == 0
+    mine, other = mine_ref[...].astype(F32), other_ref[...].astype(F32)
+    first, second = jnp.where(low, mine, other), jnp.where(low, other, mine)
+    out_ref[:main] = first[:main]
+    out_ref[main : 2 * main] = second[:main]
+    out_ref[2 * main : 2 * main + TAIL] = first[main:]
+    out_ref[2 * main + TAIL :] = second[main:]
+
+
 def awaiting(count):
     return [pl.BlockSpec(memory_space=pl.ANY)] * count
 
@@ -1262,7 +1273,7 @@
     )
     head_got = trade(head_send, 1)
     cut = own_rows // planes // 2
-    first_half, second_half = split_rows(gu_blocks, cut, (down_sum,))
+    first_half, second_half = split_rows(gu_blocks, cut, (down_sum, grad_head))
     gu_mine = [
         lax.all_gather(piece, "ctx", axis=0, axis_index_groups=plane_groups_z, tiled=False)
         for piece in (first_half, second_half)
@@ -1325,7 +1336,7 @@
             add_low(head_first, head_second).astype(F32), "ctx", axis_index_groups=outer_groups
         ).astype(BF16)
         head_second = jnp.zeros_like(head_first)
-    head_own = head_message(head_first, head_second, gain_near, (gu_other[0],))
+    head_own = head_message(head_first, head_second, gain_near, ())
     head_blocks = lax.all_gather(
         head_own, "ctx", axis=0, axis_index_groups=inner_groups, tiled=False
     )
@@ -1350,11 +1361,15 @@
     block_output = result.reshape(groups, slot_count, model_width)
 
     query_grad, key_grad, value_grad = part_heads(head_blocks, own_rows)
-    first = jnp.where(low_bit == 0, down_sum, down_other)
-    second = jnp.where(low_bit == 0, down_other, down_sum)
-    down_grad = jnp.concatenate(
-        [first[:ff_main], second[:ff_main], first[ff_main:], second[ff_main:]], axis=0
-    ).astype(F32)
+    (down_grad,) = row_call(
+        down_spread_kernel,
+        (((2 * ff_own, model_width), F32),),
+        0,
+        low_bit.reshape(1, 1),
+        down_sum,
+        down_other,
+        awaited=(gu_mine[1], head_own),
+    )
     gate_grad, up_grad = spread(device_info, gu_mine, gu_other)
 
     return (

time: 495 us -> 513 us (1.036)
  waiting for transfers between devices: 193 us -> 208 us
    all_to_all x3, waiting for transfers between devices: 17.9 us -> 47.1 us  [exchange(): lax.all_to_all(values, 'ctx', 0, 0, axis_index_groups=inner_groups, tiled...]
    ppermute x50, waiting for transfers between devices: 138 us -> 132 us  [trade(): lax.ppermute(values, ('ctx', 'fsdp'), [(i, i ^ step) for i in range(size)])]
    all_gather x2, waiting for transfers between devices: 5.96 us -> 0.02 us  [per_device(): lax.all_gather(piece, 'ctx', axis=0, axis_index_groups=plane_groups_z, ti...]
    pallas_call x4 -> x5, Pallas kernels: 7.55 us -> 11.7 us  [row_call(): pl.pallas_call(body, grid=(1,), in_specs=[whole_spec(a.shape) for a in op...]
    unnamed x164 -> x168, local copies, waits for them, and re-layouts: 50.3 us -> 49.6 us
  transfers between devices with their start and end apart: 64 -> 64, of which waited for: 28 -> 27; matrix products, arithmetic and copies ran while one was open for 14% -> 13% of each run, Pallas kernels for 13% -> 14%
where the time goes in v3:
time: 513 us; the launch traced here: 507 us
  waiting for transfers between devices  208 us (41%)
  Pallas kernels  98.4 us (19%)
  local copies, waits for them, and re-layouts  74.1 us (14%)
  starting transfers between devices  65.2 us (13%)
  other arithmetic  33.7 us (7%)
  between operations  15.7 us (3%)
  matrix products  12.9 us (3%)
    ppermute x50, waiting for transfers between devices, trade(): lax.ppermute(values, ('ctx', 'fsdp'), [(i, i ^ step) for i in range(size)])  132 us
    unnamed x168, local copies, waits for them, and re-layouts  49.6 us
    all_to_all x3, waiting for transfers between devices, exchange(): lax.all_to_all(values, 'ctx', 0, 0, axis_index_groups=inner_groups, tiled...  47.1 us
    ppermute x50, starting transfers between devices, trade(): lax.ppermute(values, ('ctx', 'fsdp'), [(i, i ^ step) for i in range(size)])  45.4 us
    pallas_call x1, Pallas kernels, feed(): pl.pallas_call(feed_kernel, out_shape=(shape(count, width), shape(count,...  25.3 us
    psum x1, waiting for transfers between devices, per_device(): down_sum = lax.psum(down_part, 'ctx', axis_index_groups=plane_groups_z)  24.7 us
    pallas_call x4, Pallas kernels, project(): pl.pallas_call(project_kernel, out_shape=tuple((jax.ShapeDtypeStruct((blo...  14.4 us
    convert_element_type x9, other arithmetic, add_low(): return (first.astype(F32) + second.astype(F32)).astype(BF16)  13.2 us
  transfers between devices with their start and end apart: 64, of which 27 were waited for; matrix products, arithmetic and copies ran while one was open for 13% of the time, Pallas kernels for 14%

profile of v3, /device:TPU:0, one launch (start us, length us, event | category | flops | bytes accessed | tf_op | source)
XLA Modules:
  0.0 507.5 jit_solution(15109806742902210830)
XLA Ops:
  13.7 3.0 collective-permute-start
  25.5 2.5 pad_add_fusion.6
  28.4 2.3 copy-done.25
  30.7 2.3 copy-done.26
  33.1 2.0 shard_map.256
  37.0 2.6 collective-permute-start.3
  43.4 2.7 shard_map.257
  46.1 5.5 %collective-permute-done.2.far_ref = bf16[272,1024]{1,0:T(8,128)(2,1)} collective-permute-done((bf16[272,1024]{1,0:T(8,128)(2,1)}, bf16[272,1024]{1,0:T(8,128)(2,1)}, u32[]{:S(2)}, u32[]{:S(2)}) %collective-permute-start.2) | collective-permute-done | bytes 557088 | tf_op jit(solution)/shard_map/ppermute | solution.py:44
  54.2 2.1 collective-permute-start.11
  58.2 4.0 shard_map.258
  62.2 2.0 copy-done
  67.4 1.7 collective-permute-done.11.near_ref
  70.0 2.2 copy-done.1
  76.7 3.8 shard_map.259
  80.5 2.2 collective-permute-done.23.refs_13_
  82.7 13.2 %collective-permute-done.24.refs_14_ = bf16[256,1152]{1,0:T(8,128)(2,1)} collective-permute-done((bf16[256,1152]{1,0:T(8,128)(2,1)}, bf16[256,1152]{1,0:T(8,128)(2,1)}, u32[]{:S(2)}, u32[]{:S(2)}) %collective-permute-start.24) | collective-permute-done | bytes 589856 | tf_op jit(solution)/shard_map/ppermute | solution.py:44
  95.9 3.9 shard_map.260
  99.8 2.1 copy-done.2
  103.9 2.2 copy-done.4
  106.1 7.9 %shard_map.261 = bf16[8,2,128,128]{3,2,1,0:T(8,128)(2,1)S(1)} custom-call(s32[3]{0:T(128)S(1)} %pad_add_fusion.2.info_ref, bf16[8,2,128,256]{3,2,1,0:T(8,128)(2,1)S(1)} %bitcast.122, bf16[8,2,128,256]{3,2,1,0:T(8,128)(2,1)S(1)} %bitcast.123, bf16[1024,2048]{1,0:T(8,128)(2,1)S(1)} %copy-done.4), custom_call_target="tpu_custom_call" | custom-call | flops 536870912 | bytes 4194304 | tf_op jit(solution)/shard_map/pallas_call | solution.py:373
  115.9 4.2 all-to-all-start
  120.1 2.0 fusion.4.refs_5_
  123.2 1.7 dynamic-slice_convert_fusion
  126.1 9.4 %all-to-all-done.refs_0_ = bf16[8,256,128]{2,1,0:T(8,128)(2,1)} async-done(((bf16[8,256,128]{2,1,0:T(8,128)(2,1)}), bf16[8,256,128]{2,1,0:T(8,128)(2,1)}, u32[]{:S(2)}, u32[]{:S(2)}) %all-to-all-start) | async-done | bytes 524320 | tf_op jit(solution)/shard_map/all_to_all | solution.py:1148
  138.1 1.9 shard_map.262
  141.0 5.0 collective-permute-start.14
  147.5 20.3 %collective-permute-done.14.refs_6_ = bf16[256,1024]{1,0:T(8,128)(2,1)S(1)} collective-permute-done((bf16[256,1024]{1,0:T(8,128)(2,1)S(1)}, bf16[256,1024]{1,0:T(8,128)(2,1)S(1)}, u32[]{:S(2)}, u32[]{:S(2)}) %collective-permute-start.14) | collective-permute-done | bytes 524320 | tf_op jit(solution)/shard_map/ppermute | solution.py:44
  171.5 4.7 collective-permute-done.18.refs_8_
  179.8 25.3 %shard_map.263 = (bf16[2048,1024]{1,0:T(8,128)(2,1)}, bf16[2048,1024]{1,0:T(8,128)(2,1)}, bf16[2048,576]{1,0:T(8,128)(2,1)}, bf16[2048,1152]{1,0:T(8,128)(2,1)},...) custom-call(s32[3]{0:T(128)} %get-tuple-element.414.info_ref, bf16[256,1024]{1,0:T(8,128)(2,1)} %copy-done.72, ...), custom_call_target="tpu_custom_call" | custom-call | flops 12079595520 | bytes 25165824 | tf_op jit(solution)/shard_map/pallas_call | solution.py:907
  205.2 9.1 %shard_map.264 = bf16[4,4,64,1152]{3,2,1,0:T(8,128)(2,1)S(1)} custom-call(bf16[2048,1024]{1,0:T(8,128)(2,1)} %get-tuple-element.281.mid_ref, bf16[2048,1152]{1,0:T(8,128)(2,1)} %get-tuple-element.282.grads_ref), custom_call_target="tpu_custom_call" | custom-call | flops 4831838208 | bytes 11272192 | tf_op jit(solution)/shard_map/pallas_call | solution.py:952
  215.7 3.3 add_convert_fusion.1
  222.9 3.7 convolution_convert_fusion.1
  229.6 6.7 %convolution_convert_fusion = bf16[2048,1024]{1,0:T(8,128)(2,1)} fusion(bf16[2048,576]{1,0:T(8,128)(2,1)} %get-tuple-element.287, bf16[576,1024]{1,0:T(8,128)(2,1)S(1)} %copy-done.65), kind=kOutput, calls=%fused_computation.2 | convolution fusion | flops 2418016256 | bytes 7733248 | tf_op jit(solution)/shard_map/dot_general | solution.py:22
  236.3 6.0 %collective-permute-done.28 = bf16[2,128,1024]{2,1,0:T(8,128)(2,1)S(1)} collective-permute-done((bf16[2,128,1024]{2,1,0:T(8,128)(2,1)S(1)}, bf16[2,128,1024]{2,1,0:T(8,128)(2,1)S(1)}, u32[]{:S(2)}, u32[]{:S(2)}) %collective-permute-start.28) | collective-permute-done | bytes 524320 | tf_op jit(solution)/shard_map/ppermute | solution.py:44
  242.4 1.7 collective-permute-start.30
  245.8 4.6 collective-permute-done.30.refs_3_
  250.4 2.6 collective-permute-done.29.refs_1_
  256.8 4.4 all-to-all-start.1
  263.1 1.8 shard_map.266
  266.2 1.9 dynamic-slice_bitcast_fusion.1
  270.0 7.7 %all-to-all-done.1 = bf16[8,256,128]{2,1,0:T(8,128)(2,1)} async-done(((bf16[8,256,128]{2,1,0:T(8,128)(2,1)}), bf16[8,256,128]{2,1,0:T(8,128)(2,1)}, u32[]{:S(2)}, u32[]{:S(2)}) %all-to-all-start.1) | async-done | bytes 524320 | tf_op jit(solution)/shard_map/all_to_all | solution.py:1148
  277.7 11.2 %shard_map.267 = f32[8,2,128,256]{3,2,1,0:T(8,128)S(1)} custom-call(s32[3]{0:T(128)S(1)} %pad_add_fusion.2.info_ref, bf16[8,2,128,256]{3,2,1,0:T(8,128)(2,1)S(1)} %bitcast.124, bf16[8,2,128,256]{3,2,1,0:T(8,128)(2,1)S(1)} %bitcast.125, bf16[8,2,128,128]{3,2,1,0:T(8,128)(2,1)} %bitcast.28.grad_ref, bf16[64,1152]{1,0:T(8,128)(2,1)} %get-tuple-element.387.refs_0_, ...), custom_call_target="tpu_custom_call" | custom-call | flops 1342177280 | bytes 4194304 | tf_op jit(solution)/shard_map/pallas_call | solution.py:386
  288.9 5.6 %shard_map.268 = (bf16[8,256,256]{2,1,0:T(8,128)(2,1)}, f32[1,256]{1,0:T(1,128)S(1)}) custom-call(f32[8,256,256]{2,1,0:T(8,128)S(1)} %bitcast.127, f32[8,256,256]{2,1,0:T(8,128)S(1)} %get-tuple-element.313.projected_ref, f32[1,256]{1,0:T(1,128)S(1)} %bitcast.152, f32[8,256,128]{2,1,0:T(8,128)S(1)} %copy-done.9, f32[8,256,128]{2,1,0:T(8,128)S(1)} %copy-done.13, ...), custom_call_target="tpu_custom_call" | custom-call | flops 52428800 | bytes 6291456 | tf_op jit(solution)/shard_map/pallas_call | solution.py:566
  294.5 2.6 fusion
  297.3 24.7 %all-reduce.4.cloned.1.call-done.refs_4_.refs_1_ = bf16[576,1024]{1,0:T(8,128)(2,1)} async-done(((bf16[576,1024]{1,0:T(8,128)(2,1)}), bf16[576,1024]{1,0:T(8,128)(2,1)}) %all-reduce.4.cloned.1.call-update) | async-done | bytes 1179664 | tf_op jit(solution)/shard_map/psum | solution.py:1200
  321.9 2.0 shard_map.269
  326.3 4.1 all-to-all-start.2
  330.7 5.0 fusion.20
  337.2 1.8 collective-permute-start.52
  345.8 30.0 %all-to-all-done.2.refs_0_ = bf16[8,256,256]{2,1,0:T(8,128)(2,1)S(1)} async-done(((bf16[8,256,256]{2,1,0:T(8,128)(2,1)}), bf16[8,256,256]{2,1,0:T(8,128)(2,1)S(1)}, u32[]{:S(2)}, u32[]{:S(2)}) %all-to-all-start.2) | async-done | bytes 1048608 | tf_op jit(solution)/shard_map/all_to_all | solution.py:1148
  375.8 2.2 copy-done.5
  380.5 2.6 shard_map.270
  386.9 3.2 add_convert_fusion
  391.2 2.9 collective-permute-done.44
  396.6 9.9 %collective-permute-done.45 = bf16[2,32,1024]{2,1,0:T(8,128)(2,1)S(1)} collective-permute-done((bf16[2,32,1024]{2,1,0:T(8,128)(2,1)S(1)}, bf16[2,32,1024]{2,1,0:T(8,128)(2,1)S(1)}, u32[]{:S(2)}, u32[]{:S(2)}) %collective-permute-start.45) | collective-permute-done | bytes 131104 | tf_op jit(solution)/shard_map/ppermute | solution.py:44
  408.3 5.1 collective-permute-done.46
  420.4 1.6 shard_map.271.refs_4_
  422.1 1.7 collective-permute-start.51
  426.0 4.2 shard_map.274
  431.1 2.4 collective-permute-start.48
  438.1 1.6 collective-permute-start.49
  441.2 46.1 %collective-permute-done.39 = bf16[128,1024]{1,0:T(8,128)(2,1)S(1)} collective-permute-done((bf16[128,1024]{1,0:T(8,128)(2,1)S(1)}, bf16[128,1024]{1,0:T(8,128)(2,1)S(1)}, u32[]{:S(2)}, u32[]{:S(2)}) %collective-permute-start.39) | collective-permute-done | bytes 262176 | tf_op jit(solution)/shard_map/ppermute | solution.py:44
  488.3 1.7 collective-permute-done.49
  491.3 4.8 shard_map.273
  (368 shorter events, 116.6 us)
Async XLA Ops:
  7.2 96.7 %all-gather.10.cloned.1.call-start = ((), (), s32[]{:S(2)}) async-start(), calls=%async_computation.4 | async-start | bytes 5242880 | tf_op jit(solution)/shard_map/all_gather | solution.py:1138
  13.7 112.4 %all-gather.12.cloned.1.call-start = ((), (), s32[]{:S(2)}) async-start(), calls=%async_computation.5 | async-start | bytes 2621440 | tf_op jit(solution)/shard_map/all_gather | solution.py:1112
  13.7 22.7 %collective-permute-start = (bf16[272,1024]{1,0:T(8,128)(2,1)S(1)}, bf16[272,1024]{1,0:T(8,128)(2,1)S(1)}, u32[]{:S(2)}, u32[]{:S(2)}) collective-permute-start(bf16[272,1024]{1,0:T(8,128)(2,1)S(1)} %pad_maximum_fusion.3.near_ref), channel_id=1, source_target_pairs={{0,4},{1,5},{2,6},{3,7},{4,0},{5,1},{6,2},{7,3},{8,12},{9,13},{10,... | collective-permute-start | bytes 1671176 | tf_op jit(solution)/shard_map/ppermute | solution.py:44
  16.8 19.7 %collective-permute-start.1 = (bf16[272,1024]{1,0:T(8,128)(2,1)S(1)}, bf16[272,1024]{1,0:T(8,128)(2,1)}, u32[]{:S(2)}, u32[]{:S(2)}) collective-permute-start(bf16[272,1024]{1,0:T(8,128)(2,1)S(1)} %pad_maximum_fusion.3.near_ref), channel_id=1, source_target_pairs={{0,8},{4,12},{8,24},{12,28},{16,0},{20,4},{24,16},{28,20},{1,9},{5... | collective-permute-start | bytes 1671176 | tf_op jit(solution)/shard_map/ppermute | solution.py:131
  18.5 9.6 %collective-permute-start.8 = (bf16[1,544]{1,0:T(2,128)(2,1)S(1)}, bf16[1,544]{1,0:T(2,128)(2,1)S(1)}, u32[]{:S(2)}, u32[]{:S(2)}) collective-permute-start(bf16[1,544]{1,0:T(2,128)(2,1)S(1)} %pad_maximum_fusion.14), channel_id=1, source_target_pairs={{0,2},{1,3},{2,0},{3,1},{4,6},{5,7},{6,4},{7,5},{8,10},{9,11},{10,... | collective-permute-start | bytes 3272 | tf_op jit(solution)/shard_map/ppermute | solution.py:44
  20.0 15.9 %collective-permute-start.7 = (bf16[1,544]{1,0:T(2,128)(2,1)S(1)}, bf16[1,544]{1,0:T(2,128)(2,1)S(1)}, u32[]{:S(2)}, u32[]{:S(2)}) collective-permute-start(bf16[1,544]{1,0:T(2,128)(2,1)S(1)} %pad_maximum_fusion.14), channel_id=1, source_target_pairs={{0,1},{1,0},{2,3},{3,2},{4,5},{5,4},{6,7},{7,6},{8,9},{9,8},{10,11... | collective-permute-start | bytes 3272 | tf_op jit(solution)/shard_map/ppermute | solution.py:44
  20.9 18.7 %collective-permute-start.5 = (bf16[256,256]{1,0:T(8,128)(2,1)S(1)}, bf16[256,256]{1,0:T(8,128)(2,1)S(1)}, u32[]{:S(2)}, u32[]{:S(2)}) collective-permute-start(bf16[256,256]{1,0:T(8,128)(2,1)S(1)} %constant_dynamic-slice_fusion.14), channel_id=1, source_target_pairs={{0,2},{1,3},{2,0},{3,1},{4,6},{5,7},{6,4},{7,5},{8,10},{9,11},{10,... | collective-permute-start | bytes 393224 | tf_op jit(solution)/shard_map/ppermute | solution.py:44
  22.4 157.3 %all-gather.14.cloned.1.call-start = ((), (), s32[]{:S(2)}) async-start(), calls=%async_computation.6 | async-start | bytes 4718592 | tf_op jit(solution)/shard_map/all_gather | solution.py:1154
  28.1 8.1 %collective-permute-start.9 = (bf16[1,544]{1,0:T(2,128)(2,1)S(1)}, bf16[1,544]{1,0:T(2,128)(2,1)S(1)}, u32[]{:S(2)}, u32[]{:S(2)}) collective-permute-start(bf16[1,544]{1,0:T(2,128)(2,1)S(1)} %collective-permute-done.8), channel_id=1, source_target_pairs={{0,1},{1,0},{2,3},{3,2},{4,5},{5,4},{6,7},{7,6},{8,9},{9,8},{10,11... | collective-permute-start | bytes 3272 | tf_op jit(solution)/shard_map/ppermute | solution.py:44
  35.9 4.1 collective-permute-start.4
  36.5 15.1 %collective-permute-start.2 = (bf16[272,1024]{1,0:T(8,128)(2,1)}, bf16[272,1024]{1,0:T(8,128)(2,1)}, u32[]{:S(2)}, u32[]{:S(2)}) collective-permute-start(bf16[272,1024]{1,0:T(8,128)(2,1)} %collective-permute-done.1.near_ref), channel_id=1, source_target_pairs={{0,4},{1,5},{2,6},{3,7},{4,0},{5,1},{6,2},{7,3},{8,12},{9,13},{10,... | collective-permute-start | bytes 1671176 | tf_op jit(solution)/shard_map/ppermute | solution.py:44
  37.0 15.7 %collective-permute-start.3 = (bf16[272,1024]{1,0:T(8,128)(2,1)}, bf16[272,1024]{1,0:T(8,128)(2,1)}, u32[]{:S(2)}, u32[]{:S(2)}) collective-permute-start(bf16[272,1024]{1,0:T(8,128)(2,1)} %collective-permute-done.1.near_ref), channel_id=1, source_target_pairs={{0,8},{4,12},{8,24},{12,28},{16,0},{20,4},{24,16},{28,20},{1,9},{5... | collective-permute-start | bytes 1671176 | tf_op jit(solution)/shard_map/ppermute | solution.py:131
  39.6 1.3 collective-permute-start.6
  52.8 13.9 %collective-permute-start.10 = (bf16[272,1024]{1,0:T(8,128)(2,1)}, bf16[272,1024]{1,0:T(8,128)(2,1)S(1)}, u32[]{:S(2)}, u32[]{:S(2)}) collective-permute-start(bf16[272,1024]{1,0:T(8,128)(2,1)} %collective-permute-done.3.near_ref), channel_id=1, source_target_pairs={{0,4},{1,5},{2,6},{3,7},{4,0},{5,1},{6,2},{7,3},{8,12},{9,13},{10,... | collective-permute-start | bytes 1671176 | tf_op jit(solution)/shard_map/ppermute | solution.py:44
  54.2 15.0 %collective-permute-start.11 = (bf16[272,1024]{1,0:T(8,128)(2,1)}, bf16[272,1024]{1,0:T(8,128)(2,1)}, u32[]{:S(2)}, u32[]{:S(2)}) collective-permute-start(bf16[272,1024]{1,0:T(8,128)(2,1)} %collective-permute-done.3.near_ref), channel_id=1, source_target_pairs={{0,8},{4,12},{8,24},{12,28},{16,0},{20,4},{24,16},{28,20},{1,9},{5... | collective-permute-start | bytes 1671176 | tf_op jit(solution)/shard_map/ppermute | solution.py:131
  56.3 24.1 %collective-permute-start.22 = (bf16[256,1152]{1,0:T(8,128)(2,1)}, bf16[256,1152]{1,0:T(8,128)(2,1)}, u32[]{:S(2)}, u32[]{:S(2)}) collective-permute-start(bf16[256,1152]{1,0:T(8,128)(2,1)} %copy-done.56), channel_id=1, source_target_pairs={{0,1},{1,0},{2,3},{3,2},{4,5},{5,4},{6,7},{7,6},{8,9},{9,8},{10,11... | collective-permute-start | bytes 1769480 | tf_op jit(solution)/shard_map/ppermute | solution.py:44
  56.3 26.3 %collective-permute-start.23 = (bf16[256,1152]{1,0:T(8,128)(2,1)}, bf16[256,1152]{1,0:T(8,128)(2,1)}, u32[]{:S(2)}, u32[]{:S(2)}) collective-permute-start(bf16[256,1152]{1,0:T(8,128)(2,1)} %copy-done.55), channel_id=1, source_target_pairs={{0,2},{1,3},{2,0},{3,1},{4,6},{5,7},{6,4},{7,5},{8,10},{9,11},{10,... | collective-permute-start | bytes 1769480 | tf_op jit(solution)/shard_map/ppermute | solution.py:44
  57.9 38.0 %collective-permute-start.24 = (bf16[256,1152]{1,0:T(8,128)(2,1)}, bf16[256,1152]{1,0:T(8,128)(2,1)}, u32[]{:S(2)}, u32[]{:S(2)}) collective-permute-start(bf16[256,1152]{1,0:T(8,128)(2,1)} %copy-done.54), channel_id=1, source_target_pairs={{0,3},{1,2},{2,1},{3,0},{4,7},{5,6},{6,5},{7,4},{8,11},{9,10},{10,... | collective-permute-start | bytes 1769480 | tf_op jit(solution)/shard_map/ppermute | solution.py:44
  69.2 26.7 %collective-permute-start.12 = (bf16[272,1024]{1,0:T(8,128)(2,1)}, bf16[272,1024]{1,0:T(8,128)(2,1)}, u32[]{:S(2)}, u32[]{:S(2)}) collective-permute-start(bf16[272,1024]{1,0:T(8,128)(2,1)} %collective-permute-done.11.near_ref), channel_id=1, source_target_pairs={{0,4},{1,5},{2,6},{3,7},{4,0},{5,1},{6,2},{7,3},{8,12},{9,13},{10,... | collective-permute-start | bytes 1671176 | tf_op jit(solution)/shard_map/ppermute | solution.py:44
  115.9 19.6 %all-to-all-start = ((bf16[8,256,128]{2,1,0:T(8,128)(2,1)}), bf16[8,256,128]{2,1,0:T(8,128)(2,1)}, u32[]{:S(2)}, u32[]{:S(2)}) async-start(bf16[8,256,128]{2,1,0:T(8,128)(2,1)} %bitcast.138), calls=%async_computation | async-start | bytes 1048576 | tf_op jit(solution)/shard_map/all_to_all | solution.py:1148
  120.1 146.1 %reduce-scatter.2.cloned.1.call-start = ((), (), s32[]{:S(2)}) async-start(), calls=%async_computation.7 | async-start | bytes 2949120 | tf_op jit(solution)/shard_map/reduce_scatter | solution.py:1190
  141.0 26.7 %collective-permute-start.14 = (bf16[256,1024]{1,0:T(8,128)(2,1)S(1)}, bf16[256,1024]{1,0:T(8,128)(2,1)S(1)}, u32[]{:S(2)}, u32[]{:S(2)}) collective-permute-start(bf16[256,1024]{1,0:T(8,128)(2,1)S(1)} %get-tuple-element.264.refs_5_), channel_id=1, source_target_pairs={{0,2},{1,3},{2,0},{3,1},{4,6},{5,7},{6,4},{7,5},{8,10},{9,11},{10,... | collective-permute-start | bytes 1572872 | tf_op jit(solution)/shard_map/ppermute | solution.py:44
  146.0 22.7 %collective-permute-start.16 = (bf16[256,1024]{1,0:T(8,128)(2,1)S(1)}, bf16[256,1024]{1,0:T(8,128)(2,1)S(1)}, u32[]{:S(2)}, u32[]{:S(2)}) collective-permute-start(bf16[256,1024]{1,0:T(8,128)(2,1)S(1)} %get-tuple-element.264.refs_5_), channel_id=1, source_target_pairs={{0,4},{1,5},{2,6},{3,7},{4,0},{5,1},{6,2},{7,3},{8,12},{9,13},{10,... | collective-permute-start | bytes 1572872 | tf_op jit(solution)/shard_map/ppermute | solution.py:44
  147.4 29.3 %collective-permute-start.13 = (bf16[256,1024]{1,0:T(8,128)(2,1)S(1)}, bf16[256,1024]{1,0:T(8,128)(2,1)S(1)}, u32[]{:S(2)}, u32[]{:S(2)}) collective-permute-start(bf16[256,1024]{1,0:T(8,128)(2,1)S(1)} %get-tuple-element.264.refs_5_), channel_id=1, source_target_pairs={{0,1},{1,0},{2,3},{3,2},{4,5},{5,4},{6,7},{7,6},{8,9},{9,8},{10,11... | collective-permute-start | bytes 1572872 | tf_op jit(solution)/shard_map/ppermute | solution.py:44
  168.8 7.5 %collective-permute-start.18 = (bf16[128,1024]{1,0:T(8,128)(2,1)S(1)}, bf16[128,1024]{1,0:T(8,128)(2,1)S(1)}, u32[]{:S(2)}, u32[]{:S(2)}) collective-permute-start(bf16[128,1024]{1,0:T(8,128)(2,1)S(1)} %slice.207), channel_id=1, source_target_pairs={{0,4},{1,5},{2,6},{3,7},{4,0},{5,1},{6,2},{7,3},{8,12},{9,13},{10,... | collective-permute-start | bytes 786440 | tf_op jit(solution)/shard_map/ppermute | solution.py:44
  169.9 6.8 %collective-permute-start.20 = (bf16[128,1024]{1,0:T(8,128)(2,1)S(1)}, bf16[128,1024]{1,0:T(8,128)(2,1)S(1)}, u32[]{:S(2)}, u32[]{:S(2)}) collective-permute-start(bf16[128,1024]{1,0:T(8,128)(2,1)S(1)} %slice.208), channel_id=1, source_target_pairs={{0,2},{1,3},{2,0},{3,1},{4,6},{5,7},{6,4},{7,5},{8,10},{9,11},{10,... | collective-permute-start | bytes 786440 | tf_op jit(solution)/shard_map/ppermute | solution.py:44
  171.0 7.3 %collective-permute-start.15 = (bf16[256,1024]{1,0:T(8,128)(2,1)S(1)}, bf16[256,1024]{1,0:T(8,128)(2,1)S(1)}, u32[]{:S(2)}, u32[]{:S(2)}) collective-permute-start(bf16[256,1024]{1,0:T(8,128)(2,1)S(1)} %collective-permute-done.14.refs_6_), channel_id=1, source_target_pairs={{0,1},{1,0},{2,3},{3,2},{4,5},{5,4},{6,7},{7,6},{8,9},{9,8},{10,11... | collective-permute-start | bytes 1572872 | tf_op jit(solution)/shard_map/ppermute | solution.py:44
  171.0 8.8 %collective-permute-start.17 = (bf16[256,1024]{1,0:T(8,128)(2,1)S(1)}, bf16[256,1024]{1,0:T(8,128)(2,1)}, u32[]{:S(2)}, u32[]{:S(2)}) collective-permute-start(bf16[256,1024]{1,0:T(8,128)(2,1)S(1)} %collective-permute-done.16.refs_7_), channel_id=1, source_target_pairs={{0,1},{1,0},{2,3},{3,2},{4,5},{5,4},{6,7},{7,6},{8,9},{9,8},{10,11... | collective-permute-start | bytes 1572872 | tf_op jit(solution)/shard_map/ppermute | solution.py:44
  176.2 1.5 collective-permute-start.19
  176.7 1.5 collective-permute-start.21
  205.0 10.7 %collective-permute-start.25 = (bf16[1024,1024]{1,0:T(8,128)(2,1)}, bf16[1024,1024]{1,0:T(8,128)(2,1)}, u32[]{:S(2)}, u32[]{:S(2)}) collective-permute-start(bf16[1024,1024]{1,0:T(8,128)(2,1)} %get-tuple-element.277), channel_id=1, source_target_pairs={{0,1},{1,0},{2,3},{3,2},{4,5},{5,4},{6,7},{7,6},{8,9},{9,8},{10,11... | collective-permute-start | bytes 6291464 | tf_op jit(solution)/shard_map/ppermute | solution.py:44
  221.0 15.3 %collective-permute-start.27 = (bf16[2,128,1024]{2,1,0:T(8,128)(2,1)}, bf16[2,128,1024]{2,1,0:T(8,128)(2,1)}, u32[]{:S(2)}, u32[]{:S(2)}) collective-permute-start(bf16[2,128,1024]{2,1,0:T(8,128)(2,1)} %pad_maximum_fusion.5), channel_id=1, source_target_pairs={{0,2},{1,3},{2,0},{3,1},{4,6},{5,7},{6,4},{7,5},{8,10},{9,11},{10,... | collective-permute-start | bytes 1572872 | tf_op jit(solution)/shard_map/ppermute | solution.py:44
  228.0 14.3 %collective-permute-start.28 = (bf16[2,128,1024]{2,1,0:T(8,128)(2,1)S(1)}, bf16[2,128,1024]{2,1,0:T(8,128)(2,1)S(1)}, u32[]{:S(2)}, u32[]{:S(2)}) collective-permute-start(bf16[2,128,1024]{2,1,0:T(8,128)(2,1)S(1)} %get-tuple-element.371), channel_id=1, source_target_pairs={{0,4},{1,5},{2,6},{3,7},{4,0},{5,1},{6,2},{7,3},{8,12},{9,13},{10,... | collective-permute-start | bytes 1572872 | tf_op jit(solution)/shard_map/ppermute | solution.py:44
  242.4 7.9 %collective-permute-start.30 = (bf16[128,1024]{1,0:T(8,128)(2,1)S(1)}, bf16[128,1024]{1,0:T(8,128)(2,1)S(1)}, u32[]{:S(2)}, u32[]{:S(2)}) collective-permute-start(bf16[128,1024]{1,0:T(8,128)(2,1)S(1)} %get-tuple-element.381), channel_id=1, source_target_pairs={{0,2},{1,3},{2,0},{3,1},{4,6},{5,7},{6,4},{7,5},{8,10},{9,11},{10,... | collective-permute-start | bytes 786440 | tf_op jit(solution)/shard_map/ppermute | solution.py:44
  245.4 7.6 %collective-permute-start.29 = (bf16[128,1024]{1,0:T(8,128)(2,1)S(1)}, bf16[128,1024]{1,0:T(8,128)(2,1)S(1)}, u32[]{:S(2)}, u32[]{:S(2)}) collective-permute-start(bf16[128,1024]{1,0:T(8,128)(2,1)S(1)} %get-tuple-element.383), channel_id=1, source_target_pairs={{0,4},{1,5},{2,6},{3,7},{4,0},{5,1},{6,2},{7,3},{8,12},{9,13},{10,... | collective-permute-start | bytes 786440 | tf_op jit(solution)/shard_map/ppermute | solution.py:44
  256.8 20.9 %all-to-all-start.1 = ((bf16[8,256,128]{2,1,0:T(8,128)(2,1)}), bf16[8,256,128]{2,1,0:T(8,128)(2,1)}, u32[]{:S(2)}, u32[]{:S(2)}) async-start(bf16[8,256,128]{2,1,0:T(8,128)(2,1)} %copy-done.48), calls=%async_computation.1 | async-start | bytes 1048576 | tf_op jit(solution)/shard_map/all_to_all | solution.py:1148
  261.2 60.8 %all-reduce.4.cloned.1.call-start = ((), (), s32[]{:S(2)}) async-start(), calls=%async_computation.8 | async-start | bytes 2359296 | tf_op jit(solution)/shard_map/psum | solution.py:1200
  261.7 114.0 %all-gather.16.cloned.1.call-start = ((), (), s32[]{:S(2)}) async-start(), calls=%async_computation.9 | async-start | bytes 1474560 | tf_op jit(solution)/shard_map/all_gather | solution.py:1278
  268.1 20.8 %collective-permute-start.31 = (bf16[64,1152]{1,0:T(8,128)(2,1)}, bf16[64,1152]{1,0:T(8,128)(2,1)S(1)}, u32[]{:S(2)}, u32[]{:S(2)}) collective-permute-start(bf16[64,1152]{1,0:T(8,128)(2,1)} %get-tuple-element.387.refs_0_), channel_id=1, source_target_pairs={{0,1},{1,0},{2,3},{3,2},{4,5},{5,4},{6,7},{7,6},{8,9},{9,8},{10,11... | collective-permute-start | bytes 442376 | tf_op jit(solution)/shard_map/ppermute | solution.py:44
  268.1 20.8 %collective-permute-start.32 = (bf16[64,1152]{1,0:T(8,128)(2,1)}, bf16[64,1152]{1,0:T(8,128)(2,1)S(1)}, u32[]{:S(2)}, u32[]{:S(2)}) collective-permute-start(bf16[64,1152]{1,0:T(8,128)(2,1)} %get-tuple-element.386.refs_1_), channel_id=1, source_target_pairs={{0,2},{1,3},{2,0},{3,1},{4,6},{5,7},{6,4},{7,5},{8,10},{9,11},{10,... | collective-permute-start | bytes 442376 | tf_op jit(solution)/shard_map/ppermute | solution.py:44
  269.4 19.5 %collective-permute-start.33 = (bf16[64,1152]{1,0:T(8,128)(2,1)}, bf16[64,1152]{1,0:T(8,128)(2,1)}, u32[]{:S(2)}, u32[]{:S(2)}) collective-permute-start(bf16[64,1152]{1,0:T(8,128)(2,1)} %get-tuple-element.385.refs_2_), channel_id=1, source_target_pairs={{0,3},{1,2},{2,1},{3,0},{4,7},{5,6},{6,5},{7,4},{8,11},{9,10},{10,... | collective-permute-start | bytes 442376 | tf_op jit(solution)/shard_map/ppermute | solution.py:44
  297.2 26.8 %collective-permute-start.34 = (bf16[2,256,256]{2,1,0:T(8,128)(2,1)S(1)}, bf16[2,256,256]{2,1,0:T(8,128)(2,1)S(1)}, u32[]{:S(2)}, u32[]{:S(2)}) collective-permute-start(bf16[2,256,256]{2,1,0:T(8,128)(2,1)S(1)} %pad_maximum_fusion.9), channel_id=1, source_target_pairs={{0,1},{1,0},{2,3},{3,2},{4,5},{5,4},{6,7},{7,6},{8,9},{9,8},{10,11... | collective-permute-start | bytes 786440 | tf_op jit(solution)/shard_map/ppermute | solution.py:44
  326.3 13.8 %collective-permute-start.35 = (bf16[2,256,1024]{2,1,0:T(8,128)(2,1)}, bf16[2,256,1024]{2,1,0:T(8,128)(2,1)}, u32[]{:S(2)}, u32[]{:S(2)}) collective-permute-start(bf16[2,256,1024]{2,1,0:T(8,128)(2,1)} %pad_maximum_fusion.2), channel_id=1, source_target_pairs={{0,1},{1,0},{2,3},{3,2},{4,5},{5,4},{6,7},{7,6},{8,9},{9,8},{10,11... | collective-permute-start | bytes 3145736 | tf_op jit(solution)/shard_map/ppermute | solution.py:44
  326.3 49.5 %all-to-all-start.2 = ((bf16[8,256,256]{2,1,0:T(8,128)(2,1)}), bf16[8,256,256]{2,1,0:T(8,128)(2,1)S(1)}, u32[]{:S(2)}, u32[]{:S(2)}) async-start(bf16[8,256,256]{2,1,0:T(8,128)(2,1)} %get-tuple-element.319.refs_5_), calls=%async_computation.3 | async-start | bytes 2097152 | tf_op jit(solution)/shard_map/all_to_all | solution.py:1148
  330.4 91.6 %all-gather.20.cloned.1.call-start = ((), (), s32[]{:S(2)}) async-start(), calls=%async_computation.11 | async-start | bytes 1474560 | tf_op jit(solution)/shard_map/all_gather | solution.py:1278
  335.7 51.1 %collective-permute-start.26 = (bf16[1024,1024]{1,0:T(8,128)(2,1)}, bf16[1024,1024]{1,0:T(8,128)(2,1)}, u32[]{:S(2)}, u32[]{:S(2)}) collective-permute-start(bf16[1024,1024]{1,0:T(8,128)(2,1)} %get-tuple-element.362), channel_id=1, source_target_pairs={{0,1},{1,0},{2,3},{3,2},{4,5},{5,4},{6,7},{7,6},{8,9},{9,8},{10,11... | collective-permute-start | bytes 6291464 | tf_op jit(solution)/shard_map/ppermute | solution.py:44
  337.2 84.9 %collective-permute-start.52 = (bf16[576,1024]{1,0:T(8,128)(2,1)S(1)}, bf16[576,1024]{1,0:T(8,128)(2,1)}, u32[]{:S(2)}, u32[]{:S(2)}) collective-permute-start(bf16[576,1024]{1,0:T(8,128)(2,1)S(1)} %copy-done.24), channel_id=1, source_target_pairs={{0,4},{1,5},{2,6},{3,7},{4,0},{5,1},{6,2},{7,3},{8,12},{9,13},{10,... | collective-permute-start | bytes 3538952 | tf_op jit(solution)/shard_map/ppermute | solution.py:44
  342.7 41.2 %collective-permute-start.36 = (bf16[256,1024]{1,0:T(8,128)(2,1)}, bf16[256,1024]{1,0:T(8,128)(2,1)}, u32[]{:S(2)}, u32[]{:S(2)}) collective-permute-start(bf16[256,1024]{1,0:T(8,128)(2,1)} %get-tuple-element.379), channel_id=1, source_target_pairs={{0,2},{1,3},{2,0},{3,1},{4,6},{5,7},{6,4},{7,5},{8,10},{9,11},{10,... | collective-permute-start | bytes 1572872 | tf_op jit(solution)/shard_map/ppermute | solution.py:44
  344.4 151.6 %all-gather.18.cloned.1.call-start = ((), (), s32[]{:S(2)}) async-start(), calls=%async_computation.10 | async-start | bytes 1253376 | tf_op jit(solution)/shard_map/all_gather | solution.py:1340
  345.2 74.8 %collective-permute-start.41 = (bf16[256,256]{1,0:T(8,128)(2,1)}, bf16[256,256]{1,0:T(8,128)(2,1)}, u32[]{:S(2)}, u32[]{:S(2)}) collective-permute-start(bf16[256,256]{1,0:T(8,128)(2,1)} %get-tuple-element.397), channel_id=1, source_target_pairs={{0,2},{1,3},{2,0},{3,1},{4,6},{5,7},{6,4},{7,5},{8,10},{9,11},{10,... | collective-permute-start | bytes 393224 | tf_op jit(solution)/shard_map/ppermute | solution.py:44
  383.8 24.3 %collective-permute-start.42 = (f32[4,544]{1,0:T(4,128)S(1)}, f32[4,544]{1,0:T(4,128)S(1)}, u32[]{:S(2)}, u32[]{:S(2)}) collective-permute-start(f32[4,544]{1,0:T(4,128)S(1)} %pad_maximum_fusion.13), channel_id=1, source_target_pairs={{0,1},{1,0},{2,3},{3,2},{4,5},{5,4},{6,7},{7,6},{8,9},{9,8},{10,11... | collective-permute-start | bytes 26120 | tf_op jit(solution)/shard_map/ppermute | solution.py:44
  385.3 8.8 %collective-permute-start.44 = (bf16[4,32,1024]{2,1,0:T(8,128)(2,1)S(1)}, bf16[4,32,1024]{2,1,0:T(8,128)(2,1)S(1)}, u32[]{:S(2)}, u32[]{:S(2)}) collective-permute-start(bf16[4,32,1024]{2,1,0:T(8,128)(2,1)S(1)} %dynamic-slice_bitcast_fusion), channel_id=1, source_target_pairs={{0,4},{1,5},{2,6},{3,7},{4,0},{5,1},{6,2},{7,3},{8,12},{9,13},{10,... | collective-permute-start | bytes 786440 | tf_op jit(solution)/shard_map/ppermute | solution.py:44
  394.2 12.3 %collective-permute-start.45 = (bf16[2,32,1024]{2,1,0:T(8,128)(2,1)S(1)}, bf16[2,32,1024]{2,1,0:T(8,128)(2,1)S(1)}, u32[]{:S(2)}, u32[]{:S(2)}) collective-permute-start(bf16[2,32,1024]{2,1,0:T(8,128)(2,1)S(1)} %dynamic-slice_bitcast_fusion.5), channel_id=1, source_target_pairs={{0,8},{1,9},{2,10},{3,11},{4,12},{5,13},{6,14},{7,15},{8,0},{9,1},... | collective-permute-start | bytes 393224 | tf_op jit(solution)/shard_map/ppermute | solution.py:44
  395.2 38.4 %collective-permute-start.37 = (bf16[2,128,1024]{2,1,0:T(8,128)(2,1)}, bf16[2,128,1024]{2,1,0:T(8,128)(2,1)}, u32[]{:S(2)}, u32[]{:S(2)}) collective-permute-start(bf16[2,128,1024]{2,1,0:T(8,128)(2,1)} %pad_maximum_fusion.6), channel_id=1, source_target_pairs={{0,2},{1,3},{2,0},{3,1},{4,6},{5,7},{6,4},{7,5},{8,10},{9,11},{10,... | collective-permute-start | bytes 1572872 | tf_op jit(solution)/shard_map/ppermute | solution.py:44
  406.5 27.1 %collective-permute-start.38 = (bf16[2,128,1024]{2,1,0:T(8,128)(2,1)}, bf16[2,128,1024]{2,1,0:T(8,128)(2,1)}, u32[]{:S(2)}, u32[]{:S(2)}) collective-permute-start(bf16[2,128,1024]{2,1,0:T(8,128)(2,1)} %get-tuple-element.363), channel_id=1, source_target_pairs={{0,4},{1,5},{2,6},{3,7},{4,0},{5,1},{6,2},{7,3},{8,12},{9,13},{10,... | collective-permute-start | bytes 1572872 | tf_op jit(solution)/shard_map/ppermute | solution.py:44
  408.1 5.2 %collective-permute-start.46 = (bf16[1,32,1024]{2,1,0:T(8,128)(2,1)S(1)}, bf16[1,32,1024]{2,1,0:T(8,128)(2,1)S(1)}, u32[]{:S(2)}, u32[]{:S(2)}) collective-permute-start(bf16[1,32,1024]{2,1,0:T(8,128)(2,1)S(1)} %constant_dynamic-slice_fusion.1), channel_id=1, source_target_pairs={{0,16},{1,17},{2,18},{3,19},{4,20},{5,21},{6,22},{7,23},{8,24},{9,... | collective-permute-start | bytes 196616 | tf_op jit(solution)/shard_map/ppermute | solution.py:44
  413.4 3.7 collective-permute-start.43
  417.0 13.1 %collective-permute-start.47 = (bf16[1,32,1024]{2,1,0:T(8,128)(2,1)}, bf16[1,32,1024]{2,1,0:T(8,128)(2,1)}, u32[]{:S(2)}, u32[]{:S(2)}) collective-permute-start(bf16[1,32,1024]{2,1,0:T(8,128)(2,1)} %add_convert_fusion.9), channel_id=1, source_target_pairs={{0,16},{1,17},{2,18},{3,19},{4,20},{5,21},{6,22},{7,23},{8,24},{9,... | collective-permute-start | bytes 196616 | tf_op jit(solution)/shard_map/ppermute | solution.py:44
  420.0 71.3 %collective-permute-start.50 = (bf16[4,4,32,1152]{3,2,1,0:T(8,128)(2,1)S(1)}, bf16[4,4,32,1152]{3,2,1,0:T(8,128)(2,1)S(1)}, u32[]{:S(2)}, u32[]{:S(2)}) collective-permute-start(bf16[4,4,32,1152]{3,2,1,0:T(8,128)(2,1)S(1)} %bitcast.129), channel_id=1, source_target_pairs={{0,4},{1,5},{2,6},{3,7},{4,0},{5,1},{6,2},{7,3},{8,12},{9,13},{10,... | collective-permute-start | bytes 3538952 | tf_op jit(solution)/shard_map/ppermute | solution.py:44
  422.1 69.2 %collective-permute-start.51 = (bf16[4,4,32,1152]{3,2,1,0:T(8,128)(2,1)}, bf16[4,4,32,1152]{3,2,1,0:T(8,128)(2,1)S(1)}, u32[]{:S(2)}, u32[]{:S(2)}) collective-permute-start(bf16[4,4,32,1152]{3,2,1,0:T(8,128)(2,1)} %bitcast.131), channel_id=1, source_target_pairs={{0,4},{1,5},{2,6},{3,7},{4,0},{5,1},{6,2},{7,3},{8,12},{9,13},{10,... | collective-permute-start | bytes 3538952 | tf_op jit(solution)/shard_map/ppermute | solution.py:44
  431.1 6.9 %collective-permute-start.48 = (bf16[2,32,1024]{2,1,0:T(8,128)(2,1)S(1)}, bf16[2,32,1024]{2,1,0:T(8,128)(2,1)S(1)}, u32[]{:S(2)}, u32[]{:S(2)}) collective-permute-start(bf16[2,32,1024]{2,1,0:T(8,128)(2,1)S(1)} %pad_maximum_fusion.11), channel_id=1, source_target_pairs={{0,8},{1,9},{2,10},{3,11},{4,12},{5,13},{6,14},{7,15},{8,0},{9,1},... | collective-permute-start | bytes 393224 | tf_op jit(solution)/shard_map/ppermute | solution.py:44
  434.7 6.4 %collective-permute-start.40 = (bf16[128,1024]{1,0:T(8,128)(2,1)S(1)}, bf16[128,1024]{1,0:T(8,128)(2,1)S(1)}, u32[]{:S(2)}, u32[]{:S(2)}) collective-permute-start(bf16[128,1024]{1,0:T(8,128)(2,1)S(1)} %get-tuple-element.375), channel_id=1, source_target_pairs={{0,2},{1,3},{2,0},{3,1},{4,6},{5,7},{6,4},{7,5},{8,10},{9,11},{10,... | collective-permute-start | bytes 786440 | tf_op jit(solution)/shard_map/ppermute | solution.py:44
  437.5 49.7 %collective-permute-start.39 = (bf16[128,1024]{1,0:T(8,128)(2,1)S(1)}, bf16[128,1024]{1,0:T(8,128)(2,1)S(1)}, u32[]{:S(2)}, u32[]{:S(2)}) collective-permute-start(bf16[128,1024]{1,0:T(8,128)(2,1)S(1)} %get-tuple-element.377), channel_id=1, source_target_pairs={{0,4},{1,5},{2,6},{3,7},{4,0},{5,1},{6,2},{7,3},{8,12},{9,13},{10,... | collective-permute-start | bytes 786440 | tf_op jit(solution)/shard_map/ppermute | solution.py:44
  438.1 52.0 %collective-permute-start.49 = (bf16[4,32,1024]{2,1,0:T(8,128)(2,1)S(1)}, bf16[4,32,1024]{2,1,0:T(8,128)(2,1)S(1)}, u32[]{:S(2)}, u32[]{:S(2)}) collective-permute-start(bf16[4,32,1024]{2,1,0:T(8,128)(2,1)S(1)} %pad_maximum_fusion.10), channel_id=1, source_target_pairs={{0,4},{1,5},{2,6},{3,7},{4,0},{5,1},{6,2},{7,3},{8,12},{9,13},{10,... | collective-permute-start | bytes 786440 | tf_op jit(solution)/shard_map/ppermute | solution.py:44
  (82 other events, 460.9 us)
Sparse Core Ops, SparseCore 0:
  13.8 37.1 all-gather.9
  53.1 33.9 all-gather.11
  116.0 53.2 all-gather.13
  215.8 47.7 reduce-scatter.1
  265.8 56.0 all-reduce.3
  324.1 50.8 all-gather.15
  376.5 30.9 all-gather.19
  422.2 47.8 all-gather.17

commit v4 on v3

--- a/solution.py
+++ b/solution.py
@@ -1252,8 +1252,10 @@
             grad_kv, "ctx", scatter_dimension=0, axis_index_groups=outer_groups, tiled=True
         )
         grad_mixed = jnp.concatenate([grad_q, grad_kv], axis=-1)
+    result_send, result_keep = halves(result_part)
+    got = trade(result_send, 1)
     grad_head, head_part = line(
-        lambda *a: unproject(*a, gu_blocks[1:]),
+        lambda *a: unproject(*a, (*gu_blocks[1:], got)),
         grad_mixed.reshape(inner, row_count, mix),
         projected,
         head_gain,
@@ -1261,6 +1263,8 @@
         sine,
     )
     grad_qkv = exchange(grad_head)
+    low_send, high_send, result_low, result_high = line(cut_plane, got, result_keep)
+    result_low_got, result_high_got = trade(low_send, 2), trade(high_send, 4)
     head_rows = line(
         lambda a, b: transpose_by(
             a.reshape(inner * row_count, model_width), b.reshape(-1, mix)
@@ -1295,7 +1299,7 @@
             ((rows_shape, F32), ((1, model_width), F32)),
             rows_flops * KV_HEADS * mix // model_width,
             *a,
-            awaited=(gu_mine[0],),
+            awaited=(gu_mine[0], result_low_got, result_high_got),
         ),
         grad_qkv,
         qkv_weight,
@@ -1321,8 +1325,6 @@
         .reshape(own_rows, model_width)
         .astype(F32)
     )
-    result_send, result_keep = halves(result_part)
-    got = trade(result_send, 1)
     gain_count = gain_parts.size
     gain_near = gain_parts + trade(gain_parts, 1)
     gain_near = gain_near + trade(gain_near, 2)
@@ -1336,18 +1338,16 @@
             add_low(head_first, head_second).astype(F32), "ctx", axis_index_groups=outer_groups
         ).astype(BF16)
         head_second = jnp.zeros_like(head_first)
-    head_own = head_message(head_first, head_second, gain_near, ())
+    low_far, high_far, low_own, high_own = line(
+        join_plane, result_low, result_high, result_low_got, result_high_got
+    )
+    low_got, high_got = trade(low_far, 4), trade(high_far, 2)
+    head_own = head_message(head_first, head_second, gain_near, (low_got, high_got))
     head_blocks = lax.all_gather(
         head_own, "ctx", axis=0, axis_index_groups=inner_groups, tiled=False
     )
     gain_sum = jnp.sum(head_blocks[:, own_rows:].astype(F32), axis=0)
     gain_sum = pick(gain_sum.reshape(-1)[:gain_count].reshape(gain_parts.shape), me_f)
-    low_send, high_send, result_low, result_high = line(cut_plane, got, result_keep)
-    result_low_got, result_high_got = trade(low_send, 2), trade(high_send, 4)
-    low_far, high_far, low_own, high_own = line(
-        join_plane, result_low, result_high, result_low_got, result_high_got
-    )
-    low_got, high_got = trade(low_far, 4), trade(high_far, 2)
     result = line(
         lambda a, b, c, d, e: (
             valid * (e + jnp.concatenate([a + b.astype(F32), c + d.astype(F32)], axis=0))

time: 513 us -> 505 us (0.984)
  waiting for transfers between devices: 208 us -> 200 us
    all_to_all x3, waiting for transfers between devices: 47.1 us -> 41 us  [exchange(): lax.all_to_all(values, 'ctx', 0, 0, axis_index_groups=inner_groups, tiled...]
    unnamed x168 -> x170, local copies, waits for them, and re-layouts: 49.6 us -> 49 us
  transfers between devices with their start and end apart: 64 -> 64, of which waited for: 27 -> 25; matrix products, arithmetic and copies ran while one was open for 13% -> 14% of each run, Pallas kernels for 14% -> 14%
where the time goes in v4:
time: 505 us; the launch traced here: 499 us
  waiting for transfers between devices  200 us (40%)
  Pallas kernels  99.7 us (20%)
  local copies, waits for them, and re-layouts  73.5 us (15%)
  starting transfers between devices  62.9 us (12%)
  other arithmetic  35.3 us (7%)
  between operations  15.6 us (3%)
  matrix products  11.5 us (2%)
    ppermute x50, waiting for transfers between devices, trade(): lax.ppermute(values, ('ctx', 'fsdp'), [(i, i ^ step) for i in range(size)])  128 us
    unnamed x170, local copies, waits for them, and re-layouts  49 us
    ppermute x50, starting transfers between devices, trade(): lax.ppermute(values, ('ctx', 'fsdp'), [(i, i ^ step) for i in range(size)])  43.8 us
    all_to_all x3, waiting for transfers between devices, exchange(): lax.all_to_all(values, 'ctx', 0, 0, axis_index_groups=inner_groups, tiled...  41 us
    psum x1, waiting for transfers between devices, per_device(): down_sum = lax.psum(down_part, 'ctx', axis_index_groups=plane_groups_z)  28.1 us
    pallas_call x1, Pallas kernels, feed(): pl.pallas_call(feed_kernel, out_shape=(shape(count, width), shape(count,...  25.3 us
    convert_element_type x9, other arithmetic, add_low(): return (first.astype(F32) + second.astype(F32)).astype(BF16)  14.4 us
    pallas_call x4, Pallas kernels, project(): pl.pallas_call(project_kernel, out_shape=tuple((jax.ShapeDtypeStruct((blo...  14.2 us
  transfers between devices with their start and end apart: 64, of which 25 were waited for; matrix products, arithmetic and copies ran while one was open for 14% of the time, Pallas kernels for 14%

profile of v4, /device:TPU:0, one launch (start us, length us, event | category | flops | bytes accessed | tf_op | source)
XLA Modules:
  0.0 498.8 jit_solution(7840296382705176848)
XLA Ops:
  13.7 3.0 collective-permute-start
  25.5 2.5 pad_add_fusion.6
  28.4 2.3 copy-done.22
  30.7 2.3 copy-done.23
  33.1 2.0 shard_map.256
  37.1 2.6 collective-permute-start.3
  43.4 2.6 shard_map.257
  46.1 5.5 %collective-permute-done.2.far_ref = bf16[272,1024]{1,0:T(8,128)(2,1)} collective-permute-done((bf16[272,1024]{1,0:T(8,128)(2,1)}, bf16[272,1024]{1,0:T(8,128)(2,1)}, u32[]{:S(2)}, u32[]{:S(2)}) %collective-permute-start.2) | collective-permute-done | bytes 557088 | tf_op jit(solution)/shard_map/ppermute | solution.py:44
  54.3 1.9 collective-permute-start.11
  58.0 3.9 shard_map.258
  61.9 2.0 copy-done
  69.7 2.2 copy-done.1
  76.5 3.7 shard_map.259
  80.2 2.0 collective-permute-done.23.refs_13_
  82.3 13.4 %collective-permute-done.24.refs_14_ = bf16[256,1152]{1,0:T(8,128)(2,1)} collective-permute-done((bf16[256,1152]{1,0:T(8,128)(2,1)}, bf16[256,1152]{1,0:T(8,128)(2,1)}, u32[]{:S(2)}, u32[]{:S(2)}) %collective-permute-start.24) | collective-permute-done | bytes 589856 | tf_op jit(solution)/shard_map/ppermute | solution.py:44
  95.7 3.9 shard_map.260
  99.6 2.1 copy-done.2
  103.6 2.2 copy-done.4
  105.8 7.9 %shard_map.261 = bf16[8,2,128,128]{3,2,1,0:T(8,128)(2,1)S(1)} custom-call(s32[3]{0:T(128)S(1)} %pad_add_fusion.2.info_ref, bf16[8,2,128,256]{3,2,1,0:T(8,128)(2,1)S(1)} %bitcast.122, bf16[8,2,128,256]{3,2,1,0:T(8,128)(2,1)S(1)} %bitcast.123, bf16[1024,2048]{1,0:T(8,128)(2,1)S(1)} %copy-done.4), custom_call_target="tpu_custom_call" | custom-call | flops 536870912 | bytes 4194304 | tf_op jit(solution)/shard_map/pallas_call | solution.py:373
  115.5 4.2 all-to-all-start
  119.8 2.0 fusion.4.refs_5_
  122.8 1.9 dynamic-slice_convert_fusion
  125.9 8.0 %all-to-all-done.refs_0_ = bf16[8,256,128]{2,1,0:T(8,128)(2,1)} async-done(((bf16[8,256,128]{2,1,0:T(8,128)(2,1)}), bf16[8,256,128]{2,1,0:T(8,128)(2,1)}, u32[]{:S(2)}, u32[]{:S(2)}) %all-to-all-start) | async-done | bytes 524320 | tf_op jit(solution)/shard_map/all_to_all | solution.py:1148
  136.5 1.9 shard_map.262
  139.4 2.9 collective-permute-start.14
  142.3 2.1 collective-permute-start.16
  144.7 20.4 %collective-permute-done.14.refs_6_ = bf16[256,1024]{1,0:T(8,128)(2,1)S(1)} collective-permute-done((bf16[256,1024]{1,0:T(8,128)(2,1)S(1)}, bf16[256,1024]{1,0:T(8,128)(2,1)S(1)}, u32[]{:S(2)}, u32[]{:S(2)}) %collective-permute-start.14) | collective-permute-done | bytes 524320 | tf_op jit(solution)/shard_map/ppermute | solution.py:44
  169.5 5.6 %collective-permute-done.18.refs_8_ = bf16[128,1024]{1,0:T(8,128)(2,1)S(1)} collective-permute-done((bf16[128,1024]{1,0:T(8,128)(2,1)S(1)}, bf16[128,1024]{1,0:T(8,128)(2,1)S(1)}, u32[]{:S(2)}, u32[]{:S(2)}) %collective-permute-start.18) | collective-permute-done | bytes 262176 | tf_op jit(solution)/shard_map/ppermute | solution.py:44
  179.0 25.3 %shard_map.263 = (bf16[2048,1024]{1,0:T(8,128)(2,1)}, bf16[2048,1024]{1,0:T(8,128)(2,1)}, bf16[2048,576]{1,0:T(8,128)(2,1)}, bf16[2048,1152]{1,0:T(8,128)(2,1)},...) custom-call(s32[3]{0:T(128)} %get-tuple-element.414.info_ref, bf16[256,1024]{1,0:T(8,128)(2,1)} %copy-done.73, ...), custom_call_target="tpu_custom_call" | custom-call | flops 12079595520 | bytes 25165824 | tf_op jit(solution)/shard_map/pallas_call | solution.py:907
  204.5 9.1 %shard_map.264 = bf16[4,4,64,1152]{3,2,1,0:T(8,128)(2,1)S(1)} custom-call(bf16[2048,1024]{1,0:T(8,128)(2,1)} %get-tuple-element.281.mid_ref, bf16[2048,1152]{1,0:T(8,128)(2,1)} %get-tuple-element.282.grads_ref), custom_call_target="tpu_custom_call" | custom-call | flops 4831838208 | bytes 11272192 | tf_op jit(solution)/shard_map/pallas_call | solution.py:952
  215.0 3.4 add_convert_fusion.1
  221.5 3.6 convolution_convert_fusion.1
  227.8 5.4 %convolution_convert_fusion = bf16[2048,1024]{1,0:T(8,128)(2,1)S(1)} fusion(bf16[2048,576]{1,0:T(8,128)(2,1)} %get-tuple-element.287, bf16[576,1024]{1,0:T(8,128)(2,1)S(1)} %copy-done.65), kind=kOutput, calls=%fused_computation.2 | convolution fusion | flops 2418016256 | bytes 7733248 | tf_op jit(solution)/shard_map/dot_general | solution.py:22
  233.2 2.5 fusion.20
  235.8 4.7 collective-permute-done.28
  244.0 4.3 collective-permute-done.30.refs_3_
  248.3 2.3 collective-permute-done.29.refs_1_
  254.3 4.3 all-to-all-start.1
  259.7 1.8 shard_map.266
  262.9 1.9 dynamic-slice_bitcast_fusion.1
  266.8 4.9 all-to-all-done.1
  271.7 11.3 %shard_map.267 = f32[8,2,128,256]{3,2,1,0:T(8,128)S(1)} custom-call(s32[3]{0:T(128)S(1)} %pad_add_fusion.2.info_ref, bf16[8,2,128,256]{3,2,1,0:T(8,128)(2,1)S(1)} %bitcast.124, bf16[8,2,128,256]{3,2,1,0:T(8,128)(2,1)S(1)} %bitcast.125, bf16[8,2,128,128]{3,2,1,0:T(8,128)(2,1)} %bitcast.28.grad_ref, bf16[64,1152]{1,0:T(8,128)(2,1)} %get-tuple-element.387.refs_0_, ...), custom_call_target="tpu_custom_call" | custom-call | flops 1342177280 | bytes 4194304 | tf_op jit(solution)/shard_map/pallas_call | solution.py:386
  283.1 5.5 %shard_map.268 = (bf16[8,256,256]{2,1,0:T(8,128)(2,1)}, f32[1,256]{1,0:T(1,128)S(1)}) custom-call(f32[8,256,256]{2,1,0:T(8,128)S(1)} %bitcast.127, f32[8,256,256]{2,1,0:T(8,128)S(1)} %get-tuple-element.313.projected_ref, f32[1,256]{1,0:T(1,128)S(1)} %bitcast.150, f32[8,256,128]{2,1,0:T(8,128)S(1)} %copy-done.9, f32[8,256,128]{2,1,0:T(8,128)S(1)} %copy-done.13, ...), custom_call_target="tpu_custom_call" | custom-call | flops 52428800 | bytes 6291456 | tf_op jit(solution)/shard_map/pallas_call | solution.py:566
  288.6 2.7 add_convert_fusion
  292.3 2.5 fusion
  295.0 28.1 %all-reduce.4.cloned.1.call-done.refs_4_.refs_1_ = bf16[576,1024]{1,0:T(8,128)(2,1)} async-done(((bf16[576,1024]{1,0:T(8,128)(2,1)}), bf16[576,1024]{1,0:T(8,128)(2,1)}) %all-reduce.4.cloned.1.call-update) | async-done | bytes 1179664 | tf_op jit(solution)/shard_map/psum | solution.py:1200
  323.1 2.0 shard_map.269
  328.0 4.3 all-to-all-start.2
  333.8 2.1 collective-permute-start.52
  337.3 2.3 slice.261
  344.4 1.9 slice.225
  349.4 28.1 %all-to-all-done.2.refs_0_ = bf16[8,256,256]{2,1,0:T(8,128)(2,1)S(1)} async-done(((bf16[8,256,256]{2,1,0:T(8,128)(2,1)}), bf16[8,256,256]{2,1,0:T(8,128)(2,1)S(1)}, u32[]{:S(2)}, u32[]{:S(2)}) %all-to-all-start.2) | async-done | bytes 1048608 | tf_op jit(solution)/shard_map/all_to_all | solution.py:1148
  377.6 5.7 %collective-permute-done.35.refs_7_ = bf16[2,128,1024]{2,1,0:T(8,128)(2,1)} collective-permute-done((bf16[2,128,1024]{2,1,0:T(8,128)(2,1)}, bf16[2,128,1024]{2,1,0:T(8,128)(2,1)}, u32[]{:S(2)}, u32[]{:S(2)}) %collective-permute-start.35) | collective-permute-done | bytes 524320 | tf_op jit(solution)/shard_map/ppermute | solution.py:44
  383.2 2.4 copy-done.5
  388.1 2.6 shard_map.270
  393.4 2.1 fusion.9
  398.0 3.7 collective-permute-done.44
  402.2 1.8 collective-permute-start.45
  404.1 4.5 collective-permute-done.45
  412.3 2.4 collective-permute-start.46
  423.2 4.2 shard_map.274
  429.1 3.5 collective-permute-done.48
  435.2 44.8 %collective-permute-done.49 = bf16[4,32,1024]{2,1,0:T(8,128)(2,1)S(1)} collective-permute-done((bf16[4,32,1024]{2,1,0:T(8,128)(2,1)S(1)}, bf16[4,32,1024]{2,1,0:T(8,128)(2,1)S(1)}, u32[]{:S(2)}, u32[]{:S(2)}) %collective-permute-start.49) | collective-permute-done | bytes 262176 | tf_op jit(solution)/shard_map/ppermute | solution.py:44
  481.2 6.4 %shard_map.273 = (f32[256,4608]{1,0:T(8,128)}, f32[256,4608]{1,0:T(8,128)}) custom-call(s32[2]{0:T(128)S(1)} %pad_add_fusion.4.info_ref, bf16[4,4,32,1152]{3,2,1,0:T(8,128)(2,1)S(1)} %bitcast.133, bf16[4,4,32,1152]{3,2,1,0:T(8,128)(2,1)S(1)} %bitcast.130, bf16[4,4,32,1152]{3,2,1,0:T(8,128)(2,1)} %collective-permute-done.50.refs_2_, ...), custom_call_target="tpu_custom_call" | custom-call | bytes 14155776 | tf_op jit(solution)/shard_map/pallas_call | solution.py:662
  (370 shorter events, 118.0 us)
Async XLA Ops:
  7.2 96.4 %all-gather.10.cloned.1.call-start = ((), (), s32[]{:S(2)}) async-start(), calls=%async_computation.4 | async-start | bytes 5242880 | tf_op jit(solution)/shard_map/all_gather | solution.py:1138
  13.7 112.2 %all-gather.12.cloned.1.call-start = ((), (), s32[]{:S(2)}) async-start(), calls=%async_computation.5 | async-start | bytes 2621440 | tf_op jit(solution)/shard_map/all_gather | solution.py:1112
  13.7 22.8 %collective-permute-start = (bf16[272,1024]{1,0:T(8,128)(2,1)S(1)}, bf16[272,1024]{1,0:T(8,128)(2,1)S(1)}, u32[]{:S(2)}, u32[]{:S(2)}) collective-permute-start(bf16[272,1024]{1,0:T(8,128)(2,1)S(1)} %pad_maximum_fusion.3.near_ref), channel_id=1, source_target_pairs={{0,4},{1,5},{2,6},{3,7},{4,0},{5,1},{6,2},{7,3},{8,12},{9,13},{10,... | collective-permute-start | bytes 1671176 | tf_op jit(solution)/shard_map/ppermute | solution.py:44
  16.8 19.7 %collective-permute-start.1 = (bf16[272,1024]{1,0:T(8,128)(2,1)S(1)}, bf16[272,1024]{1,0:T(8,128)(2,1)}, u32[]{:S(2)}, u32[]{:S(2)}) collective-permute-start(bf16[272,1024]{1,0:T(8,128)(2,1)S(1)} %pad_maximum_fusion.3.near_ref), channel_id=1, source_target_pairs={{0,8},{4,12},{8,24},{12,28},{16,0},{20,4},{24,16},{28,20},{1,9},{5... | collective-permute-start | bytes 1671176 | tf_op jit(solution)/shard_map/ppermute | solution.py:131
  18.5 9.6 %collective-permute-start.8 = (bf16[1,544]{1,0:T(2,128)(2,1)S(1)}, bf16[1,544]{1,0:T(2,128)(2,1)S(1)}, u32[]{:S(2)}, u32[]{:S(2)}) collective-permute-start(bf16[1,544]{1,0:T(2,128)(2,1)S(1)} %pad_maximum_fusion.14), channel_id=1, source_target_pairs={{0,2},{1,3},{2,0},{3,1},{4,6},{5,7},{6,4},{7,5},{8,10},{9,11},{10,... | collective-permute-start | bytes 3272 | tf_op jit(solution)/shard_map/ppermute | solution.py:44
  20.0 16.0 %collective-permute-start.7 = (bf16[1,544]{1,0:T(2,128)(2,1)S(1)}, bf16[1,544]{1,0:T(2,128)(2,1)S(1)}, u32[]{:S(2)}, u32[]{:S(2)}) collective-permute-start(bf16[1,544]{1,0:T(2,128)(2,1)S(1)} %pad_maximum_fusion.14), channel_id=1, source_target_pairs={{0,1},{1,0},{2,3},{3,2},{4,5},{5,4},{6,7},{7,6},{8,9},{9,8},{10,11... | collective-permute-start | bytes 3272 | tf_op jit(solution)/shard_map/ppermute | solution.py:44
  20.9 18.8 %collective-permute-start.5 = (bf16[256,256]{1,0:T(8,128)(2,1)S(1)}, bf16[256,256]{1,0:T(8,128)(2,1)S(1)}, u32[]{:S(2)}, u32[]{:S(2)}) collective-permute-start(bf16[256,256]{1,0:T(8,128)(2,1)S(1)} %constant_dynamic-slice_fusion.14), channel_id=1, source_target_pairs={{0,2},{1,3},{2,0},{3,1},{4,6},{5,7},{6,4},{7,5},{8,10},{9,11},{10,... | collective-permute-start | bytes 393224 | tf_op jit(solution)/shard_map/ppermute | solution.py:44
  22.4 156.6 %all-gather.14.cloned.1.call-start = ((), (), s32[]{:S(2)}) async-start(), calls=%async_computation.6 | async-start | bytes 4718592 | tf_op jit(solution)/shard_map/all_gather | solution.py:1154
  28.1 8.2 %collective-permute-start.9 = (bf16[1,544]{1,0:T(2,128)(2,1)S(1)}, bf16[1,544]{1,0:T(2,128)(2,1)S(1)}, u32[]{:S(2)}, u32[]{:S(2)}) collective-permute-start(bf16[1,544]{1,0:T(2,128)(2,1)S(1)} %collective-permute-done.8), channel_id=1, source_target_pairs={{0,1},{1,0},{2,3},{3,2},{4,5},{5,4},{6,7},{7,6},{8,9},{9,8},{10,11... | collective-permute-start | bytes 3272 | tf_op jit(solution)/shard_map/ppermute | solution.py:44
  36.0 4.1 collective-permute-start.4
  36.5 15.1 %collective-permute-start.2 = (bf16[272,1024]{1,0:T(8,128)(2,1)}, bf16[272,1024]{1,0:T(8,128)(2,1)}, u32[]{:S(2)}, u32[]{:S(2)}) collective-permute-start(bf16[272,1024]{1,0:T(8,128)(2,1)} %collective-permute-done.1.near_ref), channel_id=1, source_target_pairs={{0,4},{1,5},{2,6},{3,7},{4,0},{5,1},{6,2},{7,3},{8,12},{9,13},{10,... | collective-permute-start | bytes 1671176 | tf_op jit(solution)/shard_map/ppermute | solution.py:44
  37.1 15.7 %collective-permute-start.3 = (bf16[272,1024]{1,0:T(8,128)(2,1)}, bf16[272,1024]{1,0:T(8,128)(2,1)}, u32[]{:S(2)}, u32[]{:S(2)}) collective-permute-start(bf16[272,1024]{1,0:T(8,128)(2,1)} %collective-permute-done.1.near_ref), channel_id=1, source_target_pairs={{0,8},{4,12},{8,24},{12,28},{16,0},{20,4},{24,16},{28,20},{1,9},{5... | collective-permute-start | bytes 1671176 | tf_op jit(solution)/shard_map/ppermute | solution.py:131
  39.7 1.3 collective-permute-start.6
  52.8 13.9 %collective-permute-start.10 = (bf16[272,1024]{1,0:T(8,128)(2,1)}, bf16[272,1024]{1,0:T(8,128)(2,1)S(1)}, u32[]{:S(2)}, u32[]{:S(2)}) collective-permute-start(bf16[272,1024]{1,0:T(8,128)(2,1)} %collective-permute-done.3.near_ref), channel_id=1, source_target_pairs={{0,4},{1,5},{2,6},{3,7},{4,0},{5,1},{6,2},{7,3},{8,12},{9,13},{10,... | collective-permute-start | bytes 1671176 | tf_op jit(solution)/shard_map/ppermute | solution.py:44
  54.3 14.7 %collective-permute-start.11 = (bf16[272,1024]{1,0:T(8,128)(2,1)}, bf16[272,1024]{1,0:T(8,128)(2,1)}, u32[]{:S(2)}, u32[]{:S(2)}) collective-permute-start(bf16[272,1024]{1,0:T(8,128)(2,1)} %collective-permute-done.3.near_ref), channel_id=1, source_target_pairs={{0,8},{4,12},{8,24},{12,28},{16,0},{20,4},{24,16},{28,20},{1,9},{5... | collective-permute-start | bytes 1671176 | tf_op jit(solution)/shard_map/ppermute | solution.py:131
  56.1 24.1 %collective-permute-start.22 = (bf16[256,1152]{1,0:T(8,128)(2,1)}, bf16[256,1152]{1,0:T(8,128)(2,1)}, u32[]{:S(2)}, u32[]{:S(2)}) collective-permute-start(bf16[256,1152]{1,0:T(8,128)(2,1)} %copy-done.53), channel_id=1, source_target_pairs={{0,1},{1,0},{2,3},{3,2},{4,5},{5,4},{6,7},{7,6},{8,9},{9,8},{10,11... | collective-permute-start | bytes 1769480 | tf_op jit(solution)/shard_map/ppermute | solution.py:44
  56.1 26.1 %collective-permute-start.23 = (bf16[256,1152]{1,0:T(8,128)(2,1)}, bf16[256,1152]{1,0:T(8,128)(2,1)}, u32[]{:S(2)}, u32[]{:S(2)}) collective-permute-start(bf16[256,1152]{1,0:T(8,128)(2,1)} %copy-done.52), channel_id=1, source_target_pairs={{0,2},{1,3},{2,0},{3,1},{4,6},{5,7},{6,4},{7,5},{8,10},{9,11},{10,... | collective-permute-start | bytes 1769480 | tf_op jit(solution)/shard_map/ppermute | solution.py:44
  57.7 38.0 %collective-permute-start.24 = (bf16[256,1152]{1,0:T(8,128)(2,1)}, bf16[256,1152]{1,0:T(8,128)(2,1)}, u32[]{:S(2)}, u32[]{:S(2)}) collective-permute-start(bf16[256,1152]{1,0:T(8,128)(2,1)} %copy-done.51), channel_id=1, source_target_pairs={{0,3},{1,2},{2,1},{3,0},{4,7},{5,6},{6,5},{7,4},{8,11},{9,10},{10,... | collective-permute-start | bytes 1769480 | tf_op jit(solution)/shard_map/ppermute | solution.py:44
  69.0 26.7 %collective-permute-start.12 = (bf16[272,1024]{1,0:T(8,128)(2,1)}, bf16[272,1024]{1,0:T(8,128)(2,1)}, u32[]{:S(2)}, u32[]{:S(2)}) collective-permute-start(bf16[272,1024]{1,0:T(8,128)(2,1)} %collective-permute-done.11.near_ref), channel_id=1, source_target_pairs={{0,4},{1,5},{2,6},{3,7},{4,0},{5,1},{6,2},{7,3},{8,12},{9,13},{10,... | collective-permute-start | bytes 1671176 | tf_op jit(solution)/shard_map/ppermute | solution.py:44
  115.5 18.3 %all-to-all-start = ((bf16[8,256,128]{2,1,0:T(8,128)(2,1)}), bf16[8,256,128]{2,1,0:T(8,128)(2,1)}, u32[]{:S(2)}, u32[]{:S(2)}) async-start(bf16[8,256,128]{2,1,0:T(8,128)(2,1)} %bitcast.138), calls=%async_computation | async-start | bytes 1048576 | tf_op jit(solution)/shard_map/all_to_all | solution.py:1148
  119.7 143.2 %reduce-scatter.2.cloned.1.call-start = ((), (), s32[]{:S(2)}) async-start(), calls=%async_computation.7 | async-start | bytes 2949120 | tf_op jit(solution)/shard_map/reduce_scatter | solution.py:1190
  139.4 25.7 %collective-permute-start.14 = (bf16[256,1024]{1,0:T(8,128)(2,1)S(1)}, bf16[256,1024]{1,0:T(8,128)(2,1)S(1)}, u32[]{:S(2)}, u32[]{:S(2)}) collective-permute-start(bf16[256,1024]{1,0:T(8,128)(2,1)S(1)} %get-tuple-element.264.refs_5_), channel_id=1, source_target_pairs={{0,2},{1,3},{2,0},{3,1},{4,6},{5,7},{6,4},{7,5},{8,10},{9,11},{10,... | collective-permute-start | bytes 1572872 | tf_op jit(solution)/shard_map/ppermute | solution.py:44
  142.3 24.4 %collective-permute-start.16 = (bf16[256,1024]{1,0:T(8,128)(2,1)S(1)}, bf16[256,1024]{1,0:T(8,128)(2,1)S(1)}, u32[]{:S(2)}, u32[]{:S(2)}) collective-permute-start(bf16[256,1024]{1,0:T(8,128)(2,1)S(1)} %get-tuple-element.264.refs_5_), channel_id=1, source_target_pairs={{0,4},{1,5},{2,6},{3,7},{4,0},{5,1},{6,2},{7,3},{8,12},{9,13},{10,... | collective-permute-start | bytes 1572872 | tf_op jit(solution)/shard_map/ppermute | solution.py:44
  144.4 32.2 %collective-permute-start.13 = (bf16[256,1024]{1,0:T(8,128)(2,1)S(1)}, bf16[256,1024]{1,0:T(8,128)(2,1)S(1)}, u32[]{:S(2)}, u32[]{:S(2)}) collective-permute-start(bf16[256,1024]{1,0:T(8,128)(2,1)S(1)} %get-tuple-element.264.refs_5_), channel_id=1, source_target_pairs={{0,1},{1,0},{2,3},{3,2},{4,5},{5,4},{6,7},{7,6},{8,9},{9,8},{10,11... | collective-permute-start | bytes 1572872 | tf_op jit(solution)/shard_map/ppermute | solution.py:44
  166.7 8.4 %collective-permute-start.18 = (bf16[128,1024]{1,0:T(8,128)(2,1)S(1)}, bf16[128,1024]{1,0:T(8,128)(2,1)S(1)}, u32[]{:S(2)}, u32[]{:S(2)}) collective-permute-start(bf16[128,1024]{1,0:T(8,128)(2,1)S(1)} %slice.207), channel_id=1, source_target_pairs={{0,4},{1,5},{2,6},{3,7},{4,0},{5,1},{6,2},{7,3},{8,12},{9,13},{10,... | collective-permute-start | bytes 786440 | tf_op jit(solution)/shard_map/ppermute | solution.py:44
  168.3 8.2 %collective-permute-start.20 = (bf16[128,1024]{1,0:T(8,128)(2,1)S(1)}, bf16[128,1024]{1,0:T(8,128)(2,1)S(1)}, u32[]{:S(2)}, u32[]{:S(2)}) collective-permute-start(bf16[128,1024]{1,0:T(8,128)(2,1)S(1)} %slice.208), channel_id=1, source_target_pairs={{0,2},{1,3},{2,0},{3,1},{4,6},{5,7},{6,4},{7,5},{8,10},{9,11},{10,... | collective-permute-start | bytes 786440 | tf_op jit(solution)/shard_map/ppermute | solution.py:44
  169.0 9.1 %collective-permute-start.15 = (bf16[256,1024]{1,0:T(8,128)(2,1)S(1)}, bf16[256,1024]{1,0:T(8,128)(2,1)S(1)}, u32[]{:S(2)}, u32[]{:S(2)}) collective-permute-start(bf16[256,1024]{1,0:T(8,128)(2,1)S(1)} %collective-permute-done.14.refs_6_), channel_id=1, source_target_pairs={{0,1},{1,0},{2,3},{3,2},{4,5},{5,4},{6,7},{7,6},{8,9},{9,8},{10,11... | collective-permute-start | bytes 1572872 | tf_op jit(solution)/shard_map/ppermute | solution.py:44
  169.0 10.0 %collective-permute-start.17 = (bf16[256,1024]{1,0:T(8,128)(2,1)S(1)}, bf16[256,1024]{1,0:T(8,128)(2,1)}, u32[]{:S(2)}, u32[]{:S(2)}) collective-permute-start(bf16[256,1024]{1,0:T(8,128)(2,1)S(1)} %collective-permute-done.16.refs_7_), channel_id=1, source_target_pairs={{0,1},{1,0},{2,3},{3,2},{4,5},{5,4},{6,7},{7,6},{8,9},{9,8},{10,11... | collective-permute-start | bytes 1572872 | tf_op jit(solution)/shard_map/ppermute | solution.py:44
  175.1 1.5 collective-permute-start.19
  176.6 1.5 collective-permute-start.21
  204.3 10.7 %collective-permute-start.25 = (bf16[1024,1024]{1,0:T(8,128)(2,1)}, bf16[1024,1024]{1,0:T(8,128)(2,1)}, u32[]{:S(2)}, u32[]{:S(2)}) collective-permute-start(bf16[1024,1024]{1,0:T(8,128)(2,1)} %get-tuple-element.277), channel_id=1, source_target_pairs={{0,1},{1,0},{2,3},{3,2},{4,5},{5,4},{6,7},{7,6},{8,9},{9,8},{10,11... | collective-permute-start | bytes 6291464 | tf_op jit(solution)/shard_map/ppermute | solution.py:44
  220.7 15.1 %collective-permute-start.27 = (bf16[2,128,1024]{2,1,0:T(8,128)(2,1)}, bf16[2,128,1024]{2,1,0:T(8,128)(2,1)}, u32[]{:S(2)}, u32[]{:S(2)}) collective-permute-start(bf16[2,128,1024]{2,1,0:T(8,128)(2,1)} %pad_maximum_fusion.5), channel_id=1, source_target_pairs={{0,2},{1,3},{2,0},{3,1},{4,6},{5,7},{6,4},{7,5},{8,10},{9,11},{10,... | collective-permute-start | bytes 1572872 | tf_op jit(solution)/shard_map/ppermute | solution.py:44
  226.5 14.0 %collective-permute-start.28 = (bf16[2,128,1024]{2,1,0:T(8,128)(2,1)S(1)}, bf16[2,128,1024]{2,1,0:T(8,128)(2,1)S(1)}, u32[]{:S(2)}, u32[]{:S(2)}) collective-permute-start(bf16[2,128,1024]{2,1,0:T(8,128)(2,1)S(1)} %get-tuple-element.371), channel_id=1, source_target_pairs={{0,4},{1,5},{2,6},{3,7},{4,0},{5,1},{6,2},{7,3},{8,12},{9,13},{10,... | collective-permute-start | bytes 1572872 | tf_op jit(solution)/shard_map/ppermute | solution.py:44
  235.7 47.4 %collective-permute-start.26 = (bf16[1024,1024]{1,0:T(8,128)(2,1)}, bf16[1024,1024]{1,0:T(8,128)(2,1)}, u32[]{:S(2)}, u32[]{:S(2)}) collective-permute-start(bf16[1024,1024]{1,0:T(8,128)(2,1)} %get-tuple-element.362), channel_id=1, source_target_pairs={{0,1},{1,0},{2,3},{3,2},{4,5},{5,4},{6,7},{7,6},{8,9},{9,8},{10,11... | collective-permute-start | bytes 6291464 | tf_op jit(solution)/shard_map/ppermute | solution.py:44
  240.7 7.6 %collective-permute-start.30 = (bf16[128,1024]{1,0:T(8,128)(2,1)S(1)}, bf16[128,1024]{1,0:T(8,128)(2,1)S(1)}, u32[]{:S(2)}, u32[]{:S(2)}) collective-permute-start(bf16[128,1024]{1,0:T(8,128)(2,1)S(1)} %get-tuple-element.381), channel_id=1, source_target_pairs={{0,2},{1,3},{2,0},{3,1},{4,6},{5,7},{6,4},{7,5},{8,10},{9,11},{10,... | collective-permute-start | bytes 786440 | tf_op jit(solution)/shard_map/ppermute | solution.py:44
  243.2 7.4 %collective-permute-start.29 = (bf16[128,1024]{1,0:T(8,128)(2,1)S(1)}, bf16[128,1024]{1,0:T(8,128)(2,1)S(1)}, u32[]{:S(2)}, u32[]{:S(2)}) collective-permute-start(bf16[128,1024]{1,0:T(8,128)(2,1)S(1)} %get-tuple-element.383), channel_id=1, source_target_pairs={{0,4},{1,5},{2,6},{3,7},{4,0},{5,1},{6,2},{7,3},{8,12},{9,13},{10,... | collective-permute-start | bytes 786440 | tf_op jit(solution)/shard_map/ppermute | solution.py:44
  254.3 17.3 %all-to-all-start.1 = ((bf16[8,256,128]{2,1,0:T(8,128)(2,1)}), bf16[8,256,128]{2,1,0:T(8,128)(2,1)}, u32[]{:S(2)}, u32[]{:S(2)}) async-start(bf16[8,256,128]{2,1,0:T(8,128)(2,1)} %copy-done.45), calls=%async_computation.1 | async-start | bytes 1048576 | tf_op jit(solution)/shard_map/all_to_all | solution.py:1148
  258.6 64.5 %all-reduce.4.cloned.1.call-start = ((), (), s32[]{:S(2)}) async-start(), calls=%async_computation.8 | async-start | bytes 2359296 | tf_op jit(solution)/shard_map/psum | solution.py:1200
  264.8 18.2 %collective-permute-start.31 = (bf16[64,1152]{1,0:T(8,128)(2,1)}, bf16[64,1152]{1,0:T(8,128)(2,1)}, u32[]{:S(2)}, u32[]{:S(2)}) collective-permute-start(bf16[64,1152]{1,0:T(8,128)(2,1)} %get-tuple-element.387.refs_0_), channel_id=1, source_target_pairs={{0,1},{1,0},{2,3},{3,2},{4,5},{5,4},{6,7},{7,6},{8,9},{9,8},{10,11... | collective-permute-start | bytes 442376 | tf_op jit(solution)/shard_map/ppermute | solution.py:44
  264.8 18.2 %collective-permute-start.32 = (bf16[64,1152]{1,0:T(8,128)(2,1)S(1)}, bf16[64,1152]{1,0:T(8,128)(2,1)}, u32[]{:S(2)}, u32[]{:S(2)}) collective-permute-start(bf16[64,1152]{1,0:T(8,128)(2,1)S(1)} %get-tuple-element.386.refs_1_), channel_id=1, source_target_pairs={{0,2},{1,3},{2,0},{3,1},{4,6},{5,7},{6,4},{7,5},{8,10},{9,11},{10,... | collective-permute-start | bytes 442376 | tf_op jit(solution)/shard_map/ppermute | solution.py:44
  265.6 17.5 %collective-permute-start.33 = (bf16[64,1152]{1,0:T(8,128)(2,1)S(1)}, bf16[64,1152]{1,0:T(8,128)(2,1)}, u32[]{:S(2)}, u32[]{:S(2)}) collective-permute-start(bf16[64,1152]{1,0:T(8,128)(2,1)S(1)} %get-tuple-element.385.refs_2_), channel_id=1, source_target_pairs={{0,3},{1,2},{2,1},{3,0},{4,7},{5,6},{6,5},{7,4},{8,11},{9,10},{10,... | collective-permute-start | bytes 442376 | tf_op jit(solution)/shard_map/ppermute | solution.py:44
  266.7 116.5 %all-gather.16.cloned.1.call-start = ((), (), s32[]{:S(2)}) async-start(), calls=%async_computation.9 | async-start | bytes 1474560 | tf_op jit(solution)/shard_map/all_gather | solution.py:1282
  294.9 30.3 %collective-permute-start.36 = (bf16[2,256,256]{2,1,0:T(8,128)(2,1)S(1)}, bf16[2,256,256]{2,1,0:T(8,128)(2,1)S(1)}, u32[]{:S(2)}, u32[]{:S(2)}) collective-permute-start(bf16[2,256,256]{2,1,0:T(8,128)(2,1)S(1)} %pad_maximum_fusion.9), channel_id=1, source_target_pairs={{0,1},{1,0},{2,3},{3,2},{4,5},{5,4},{6,7},{7,6},{8,9},{9,8},{10,11... | collective-permute-start | bytes 786440 | tf_op jit(solution)/shard_map/ppermute | solution.py:44
  328.0 12.8 %collective-permute-start.37 = (bf16[2,256,1024]{2,1,0:T(8,128)(2,1)}, bf16[2,256,1024]{2,1,0:T(8,128)(2,1)}, u32[]{:S(2)}, u32[]{:S(2)}) collective-permute-start(bf16[2,256,1024]{2,1,0:T(8,128)(2,1)} %pad_maximum_fusion.2), channel_id=1, source_target_pairs={{0,1},{1,0},{2,3},{3,2},{4,5},{5,4},{6,7},{7,6},{8,9},{9,8},{10,11... | collective-permute-start | bytes 3145736 | tf_op jit(solution)/shard_map/ppermute | solution.py:44
  328.0 49.5 %all-to-all-start.2 = ((bf16[8,256,256]{2,1,0:T(8,128)(2,1)}), bf16[8,256,256]{2,1,0:T(8,128)(2,1)S(1)}, u32[]{:S(2)}, u32[]{:S(2)}) async-start(bf16[8,256,256]{2,1,0:T(8,128)(2,1)} %get-tuple-element.321.refs_5_), calls=%async_computation.3 | async-start | bytes 2097152 | tf_op jit(solution)/shard_map/all_to_all | solution.py:1148
  332.4 84.5 %all-gather.20.cloned.1.call-start = ((), (), s32[]{:S(2)}) async-start(), calls=%async_computation.11 | async-start | bytes 1474560 | tf_op jit(solution)/shard_map/all_gather | solution.py:1282
  333.8 88.6 %collective-permute-start.52 = (bf16[576,1024]{1,0:T(8,128)(2,1)S(1)}, bf16[576,1024]{1,0:T(8,128)(2,1)}, u32[]{:S(2)}, u32[]{:S(2)}) collective-permute-start(bf16[576,1024]{1,0:T(8,128)(2,1)S(1)} %copy-done.21), channel_id=1, source_target_pairs={{0,4},{1,5},{2,6},{3,7},{4,0},{5,1},{6,2},{7,3},{8,12},{9,13},{10,... | collective-permute-start | bytes 3538952 | tf_op jit(solution)/shard_map/ppermute | solution.py:44
  335.8 41.7 %collective-permute-start.34 = (bf16[2,128,1024]{2,1,0:T(8,128)(2,1)}, bf16[2,128,1024]{2,1,0:T(8,128)(2,1)S(1)}, u32[]{:S(2)}, u32[]{:S(2)}) collective-permute-start(bf16[2,128,1024]{2,1,0:T(8,128)(2,1)} %pad_maximum_fusion.6), channel_id=1, source_target_pairs={{0,2},{1,3},{2,0},{3,1},{4,6},{5,7},{6,4},{7,5},{8,10},{9,11},{10,... | collective-permute-start | bytes 1572872 | tf_op jit(solution)/shard_map/ppermute | solution.py:44
  340.6 42.6 %collective-permute-start.35 = (bf16[2,128,1024]{2,1,0:T(8,128)(2,1)}, bf16[2,128,1024]{2,1,0:T(8,128)(2,1)}, u32[]{:S(2)}, u32[]{:S(2)}) collective-permute-start(bf16[2,128,1024]{2,1,0:T(8,128)(2,1)} %get-tuple-element.367), channel_id=1, source_target_pairs={{0,4},{1,5},{2,6},{3,7},{4,0},{5,1},{6,2},{7,3},{8,12},{9,13},{10,... | collective-permute-start | bytes 1572872 | tf_op jit(solution)/shard_map/ppermute | solution.py:44
  343.5 48.0 %collective-permute-start.38 = (bf16[256,1024]{1,0:T(8,128)(2,1)}, bf16[256,1024]{1,0:T(8,128)(2,1)}, u32[]{:S(2)}, u32[]{:S(2)}) collective-permute-start(bf16[256,1024]{1,0:T(8,128)(2,1)} %get-tuple-element.379), channel_id=1, source_target_pairs={{0,2},{1,3},{2,0},{3,1},{4,6},{5,7},{6,4},{7,5},{8,10},{9,11},{10,... | collective-permute-start | bytes 1572872 | tf_op jit(solution)/shard_map/ppermute | solution.py:44
  346.3 141.3 %all-gather.18.cloned.1.call-start = ((), (), s32[]{:S(2)}) async-start(), calls=%async_computation.10 | async-start | bytes 1253376 | tf_op jit(solution)/shard_map/all_gather | solution.py:1346
  348.0 67.4 %collective-permute-start.41 = (bf16[256,256]{1,0:T(8,128)(2,1)}, bf16[256,256]{1,0:T(8,128)(2,1)}, u32[]{:S(2)}, u32[]{:S(2)}) collective-permute-start(bf16[256,256]{1,0:T(8,128)(2,1)} %get-tuple-element.397), channel_id=1, source_target_pairs={{0,2},{1,3},{2,0},{3,1},{4,6},{5,7},{6,4},{7,5},{8,10},{9,11},{10,... | collective-permute-start | bytes 393224 | tf_op jit(solution)/shard_map/ppermute | solution.py:44
  391.5 10.7 %collective-permute-start.42 = (f32[4,544]{1,0:T(4,128)S(1)}, f32[4,544]{1,0:T(4,128)S(1)}, u32[]{:S(2)}, u32[]{:S(2)}) collective-permute-start(f32[4,544]{1,0:T(4,128)S(1)} %pad_maximum_fusion.13), channel_id=1, source_target_pairs={{0,1},{1,0},{2,3},{3,2},{4,5},{5,4},{6,7},{7,6},{8,9},{9,8},{10,11... | collective-permute-start | bytes 26120 | tf_op jit(solution)/shard_map/ppermute | solution.py:44
  392.9 8.8 %collective-permute-start.44 = (bf16[4,32,1024]{2,1,0:T(8,128)(2,1)S(1)}, bf16[4,32,1024]{2,1,0:T(8,128)(2,1)S(1)}, u32[]{:S(2)}, u32[]{:S(2)}) collective-permute-start(bf16[4,32,1024]{2,1,0:T(8,128)(2,1)S(1)} %dynamic-slice_bitcast_fusion), channel_id=1, source_target_pairs={{0,4},{1,5},{2,6},{3,7},{4,0},{5,1},{6,2},{7,3},{8,12},{9,13},{10,... | collective-permute-start | bytes 786440 | tf_op jit(solution)/shard_map/ppermute | solution.py:44
  395.5 21.4 %collective-permute-start.40 = (bf16[128,1024]{1,0:T(8,128)(2,1)}, bf16[128,1024]{1,0:T(8,128)(2,1)}, u32[]{:S(2)}, u32[]{:S(2)}) collective-permute-start(bf16[128,1024]{1,0:T(8,128)(2,1)} %get-tuple-element.375), channel_id=1, source_target_pairs={{0,2},{1,3},{2,0},{3,1},{4,6},{5,7},{6,4},{7,5},{8,10},{9,11},{10,... | collective-permute-start | bytes 786440 | tf_op jit(solution)/shard_map/ppermute | solution.py:44
  401.7 15.8 %collective-permute-start.39 = (bf16[128,1024]{1,0:T(8,128)(2,1)}, bf16[128,1024]{1,0:T(8,128)(2,1)}, u32[]{:S(2)}, u32[]{:S(2)}) collective-permute-start(bf16[128,1024]{1,0:T(8,128)(2,1)} %get-tuple-element.377), channel_id=1, source_target_pairs={{0,4},{1,5},{2,6},{3,7},{4,0},{5,1},{6,2},{7,3},{8,12},{9,13},{10,... | collective-permute-start | bytes 786440 | tf_op jit(solution)/shard_map/ppermute | solution.py:44
  402.2 6.4 %collective-permute-start.45 = (bf16[2,32,1024]{2,1,0:T(8,128)(2,1)S(1)}, bf16[2,32,1024]{2,1,0:T(8,128)(2,1)S(1)}, u32[]{:S(2)}, u32[]{:S(2)}) collective-permute-start(bf16[2,32,1024]{2,1,0:T(8,128)(2,1)S(1)} %dynamic-slice_bitcast_fusion.5), channel_id=1, source_target_pairs={{0,8},{1,9},{2,10},{3,11},{4,12},{5,13},{6,14},{7,15},{8,0},{9,1},... | collective-permute-start | bytes 393224 | tf_op jit(solution)/shard_map/ppermute | solution.py:44
  408.6 3.7 collective-permute-start.43
  412.3 6.9 %collective-permute-start.46 = (bf16[1,32,1024]{2,1,0:T(8,128)(2,1)}, bf16[1,32,1024]{2,1,0:T(8,128)(2,1)}, u32[]{:S(2)}, u32[]{:S(2)}) collective-permute-start(bf16[1,32,1024]{2,1,0:T(8,128)(2,1)} %constant_dynamic-slice_fusion.1), channel_id=1, source_target_pairs={{0,16},{1,17},{2,18},{3,19},{4,20},{5,21},{6,22},{7,23},{8,24},{9,... | collective-permute-start | bytes 196616 | tf_op jit(solution)/shard_map/ppermute | solution.py:44
  415.4 65.8 %collective-permute-start.50 = (bf16[4,4,32,1152]{3,2,1,0:T(8,128)(2,1)S(1)}, bf16[4,4,32,1152]{3,2,1,0:T(8,128)(2,1)}, u32[]{:S(2)}, u32[]{:S(2)}) collective-permute-start(bf16[4,4,32,1152]{3,2,1,0:T(8,128)(2,1)S(1)} %bitcast.132), channel_id=1, source_target_pairs={{0,4},{1,5},{2,6},{3,7},{4,0},{5,1},{6,2},{7,3},{8,12},{9,13},{10,... | collective-permute-start | bytes 3538952 | tf_op jit(solution)/shard_map/ppermute | solution.py:44
  416.9 64.3 %collective-permute-start.51 = (bf16[4,4,32,1152]{3,2,1,0:T(8,128)(2,1)}, bf16[4,4,32,1152]{3,2,1,0:T(8,128)(2,1)}, u32[]{:S(2)}, u32[]{:S(2)}) collective-permute-start(bf16[4,4,32,1152]{3,2,1,0:T(8,128)(2,1)} %bitcast.128), channel_id=1, source_target_pairs={{0,4},{1,5},{2,6},{3,7},{4,0},{5,1},{6,2},{7,3},{8,12},{9,13},{10,... | collective-permute-start | bytes 3538952 | tf_op jit(solution)/shard_map/ppermute | solution.py:44
  420.1 7.3 %collective-permute-start.47 = (bf16[1,32,1024]{2,1,0:T(8,128)(2,1)S(1)}, bf16[1,32,1024]{2,1,0:T(8,128)(2,1)S(1)}, u32[]{:S(2)}, u32[]{:S(2)}) collective-permute-start(bf16[1,32,1024]{2,1,0:T(8,128)(2,1)S(1)} %add_convert_fusion.9), channel_id=1, source_target_pairs={{0,16},{1,17},{2,18},{3,19},{4,20},{5,21},{6,22},{7,23},{8,24},{9,... | collective-permute-start | bytes 196616 | tf_op jit(solution)/shard_map/ppermute | solution.py:44
  427.5 5.1 %collective-permute-start.48 = (bf16[2,32,1024]{2,1,0:T(8,128)(2,1)S(1)}, bf16[2,32,1024]{2,1,0:T(8,128)(2,1)S(1)}, u32[]{:S(2)}, u32[]{:S(2)}) collective-permute-start(bf16[2,32,1024]{2,1,0:T(8,128)(2,1)S(1)} %pad_maximum_fusion.11), channel_id=1, source_target_pairs={{0,8},{1,9},{2,10},{3,11},{4,12},{5,13},{6,14},{7,15},{8,0},{9,1},... | collective-permute-start | bytes 393224 | tf_op jit(solution)/shard_map/ppermute | solution.py:44
  432.6 47.3 %collective-permute-start.49 = (bf16[4,32,1024]{2,1,0:T(8,128)(2,1)S(1)}, bf16[4,32,1024]{2,1,0:T(8,128)(2,1)S(1)}, u32[]{:S(2)}, u32[]{:S(2)}) collective-permute-start(bf16[4,32,1024]{2,1,0:T(8,128)(2,1)S(1)} %pad_maximum_fusion.10), channel_id=1, source_target_pairs={{0,4},{1,5},{2,6},{3,7},{4,0},{5,1},{6,2},{7,3},{8,12},{9,13},{10,... | collective-permute-start | bytes 786440 | tf_op jit(solution)/shard_map/ppermute | solution.py:44
  (83 other events, 426.9 us)
Sparse Core Ops, SparseCore 0:
  13.8 37.1 all-gather.9
  53.1 33.9 all-gather.11
  115.7 52.1 all-gather.13
  215.1 46.1 reduce-scatter.1
  266.8 56.2 all-reduce.3
  325.2 50.8 all-gather.15
  377.7 29.1 all-gather.19
  419.3 45.3 all-gather.17
